TPU v7x, 768 devices: a whole 4x8x12 slice. The times are simulated.
768 devices in a mesh: occ: 96 (over x, y, z_hi), aux: 8 (over z_lo, core).
Axes of the slice: x: 4, y: 8, z: 12 (z_hi: 3, z_lo: 4; z = z_hi * 4 + z_lo), core: 2. Of those that a mesh axis runs over, the one named last changes fastest.
Arguments:
- factors: float32 [96, 3072, 512], P('occ', 'aux'), may hold values from -0.8 to 0.8
- occ_energy: float32 [96], P('occ'), may hold values from -1.5 to -0.5
- virt_energy: float32 [512], replicated, may hold values from 0.2 to 3
Outputs:
- density: float32 [96, 3072, 512], P('occ', 'aux')
All inputs are finite; a program needn't handle non-finite values.
Results may differ from a plain program's by a relative error of at most 0.000052.
Values sent between devices are 32-bit elements; how exact they have to be, the bound alone decides.
No kernel may reach another device: no remote copies, remote signals or barrier semaphores. Data moves between devices by JAX's collectives and lax.ppermute only.
A program may use at most 32 MiB of HBM per device.

v0:
```python
import jax
import jax.numpy as jnp
from jax import lax
from jax.sharding import PartitionSpec as P


def passed_along(x, axis, by):
    size = lax.axis_size(axis)
    return lax.ppermute(x, axis, [(i, (i + by) % size) for i in range(size)])


def amplitudes(tiles, pair_energy, virt_energy):
    totals = lax.psum(tiles, "aux")
    denom = virt_energy[None, :, None] + virt_energy[None, None, :] - pair_energy[:, None, None]
    return totals / denom


def local(factors, occ_energy, virt_energy):
    own_slab = factors[0]
    lower, lower_energy = passed_along((own_slab, occ_energy), "occ", 1)
    upper, upper_energy = passed_along((own_slab, occ_energy), "occ", -1)
    left = jnp.stack([own_slab, upper])
    right = jnp.stack([lower, own_slab])
    tiles = jnp.einsum(
        "nqa,nqb->nab",
        left,
        right,
        precision=lax.Precision.HIGHEST,
        preferred_element_type=jnp.float32,
    )
    pair_energy = jnp.concatenate([occ_energy + lower_energy, upper_energy + occ_energy])
    amps = amplitudes(tiles, pair_energy, virt_energy)
    own_part = jnp.einsum(
        "qb,ab->qa",
        lower,
        amps[0],
        precision=lax.Precision.HIGHEST,
        preferred_element_type=jnp.float32,
    )
    other_part = jnp.einsum(
        "qc,ca->qa",
        upper,
        amps[1],
        precision=lax.Precision.HIGHEST,
        preferred_element_type=jnp.float32,
    )
    return (own_part + other_part)[None]


def solution(mesh):
    in_specs = (P("occ", "aux", None), P("occ"), P())
    out_specs = P("occ", "aux", None)
    return jax.shard_map(local, mesh=mesh, in_specs=in_specs, out_specs=out_specs, check_vma=False)
```

profile of v0, /device:TPU:1, one launch (start us, length us, event | category | flops | bytes accessed | tf_op | source)
XLA Modules:
  0.0 204.9 jit_solution(420809091398029301)
XLA Ops:
  6.5 0.0 all-reduce.2.cloned.1.call-start
  6.5 20.2 %collective-permute-start = (f32[384,512]{1,0:T(8,128)}, f32[384,512]{1,0:T(8,128)S(1)}, u32[]{:S(2)}, u32[]{:S(2)}) collective-permute-start(f32[384,512]{1,0:T(8,128)} %bitcast.16), channel_id=1, source_target_pairs={{0,760},{8,0},{16,8},{24,16},{32,24},{40,32},{48,40},{56,48},{64,5... | collective-permute-start | bytes 2359304 | tf_op jit(solution)/shard_map/ppermute | solution.py:9
  26.7 1.9 collective-permute-start.1
  28.7 65.2 %collective-permute-done = f32[384,512]{1,0:T(8,128)S(1)} collective-permute-done((f32[384,512]{1,0:T(8,128)}, f32[384,512]{1,0:T(8,128)S(1)}, u32[]{:S(2)}, u32[]{:S(2)}) %collective-permute-start) | collective-permute-done | bytes 786464 | tf_op jit(solution)/shard_map/ppermute | solution.py:9
  93.9 11.6 %collective-permute-done.1 = f32[384,512]{1,0:T(8,128)S(1)} collective-permute-done((f32[384,512]{1,0:T(8,128)}, f32[384,512]{1,0:T(8,128)S(1)}, u32[]{:S(2)}, u32[]{:S(2)}) %collective-permute-start.1) | collective-permute-done | bytes 786464 | tf_op jit(solution)/shard_map/ppermute | solution.py:9
  105.4 6.2 %fusion = f32[2,512,512]{2,1,0:T(8,128)} fusion(f32[1,384,512]{2,1,0:T(8,128)S(1)} %bitcast.15, f32[1,384,512]{2,1,0:T(8,128)} %param.3, f32[1,384,512]{2,1,0:T(8,128)S(1)} %bitcast.18), kind=kOutput, calls=%fused_computation.1 | convolution fusion | flops 2416705536 | bytes 4456448 | tf_op jit(solution)/shard_map/nqa,nqb->nab/dot_general | solution.py:24
  111.6 0.0 copy-start
  111.6 0.0 all-reduce.2.cloned.1.call-update
  111.7 1.9 collective-permute-start.2
  113.6 11.5 %collective-permute-start.3 = (f32[1]{0:T(128)}, f32[1]{0:T(128)}, u32[]{:S(2)}, u32[]{:S(2)}) collective-permute-start(f32[1]{0:T(128)} %param.4), channel_id=1, source_target_pairs={{0,760},{8,0},{16,8},{24,16},{32,24},{40,32},{48,40},{56,48},{64,5... | collective-permute-start | bytes 20 | tf_op jit(solution)/shard_map/ppermute | solution.py:9
  125.8 0.0 copy-done
  125.8 0.1 broadcast_add_fusion
  125.9 0.0 collective-permute-done.2
  126.5 0.0 collective-permute-done.3
  127.2 0.1 pad_maximum_fusion
  127.2 62.3 %all-reduce.2.cloned.1.call-done = f32[2,512,512]{2,1,0:T(8,128)} async-done(((f32[2,512,512]{2,1,0:T(8,128)}), f32[2,512,512]{2,1,0:T(8,128)}) %all-reduce.2.cloned.1.call-update) | async-done | bytes 2097168 | tf_op jit(solution)/shard_map/psum | solution.py:13
  189.5 2.0 subtract_divide_fusion
  191.6 3.5 %fusion.8 = f32[512,384]{1,0:T(8,128)S(1)} fusion(f32[384,512]{1,0:T(8,128)S(1)} %collective-permute-done, f32[2,512,512]{2,1,0:T(8,128)S(1)} %subtract_divide_fusion), kind=kOutput, calls=%fused_computation.11 | convolution fusion | flops 1207959552 | bytes 2621440 | tf_op jit(solution)/shard_map/qc,ca->qa/dot_general | solution.py:40
  195.1 1.8 fusion.7
  196.9 1.1 copy.5
Async XLA Ops:
  6.5 183.0 %all-reduce.2.cloned.1.call-start = ((), (), s32[]{:S(2)}) async-start(), calls=%async_computation | async-start | bytes 4194304 | tf_op jit(solution)/shard_map/psum | solution.py:13
  6.5 87.3 %collective-permute-start = (f32[384,512]{1,0:T(8,128)}, f32[384,512]{1,0:T(8,128)S(1)}, u32[]{:S(2)}, u32[]{:S(2)}) collective-permute-start(f32[384,512]{1,0:T(8,128)} %bitcast.16), channel_id=1, source_target_pairs={{0,760},{8,0},{16,8},{24,16},{32,24},{40,32},{48,40},{56,48},{64,5... | collective-permute-start | bytes 2359304 | tf_op jit(solution)/shard_map/ppermute | solution.py:9
  26.7 78.7 %collective-permute-start.1 = (f32[384,512]{1,0:T(8,128)}, f32[384,512]{1,0:T(8,128)S(1)}, u32[]{:S(2)}, u32[]{:S(2)}) collective-permute-start(f32[384,512]{1,0:T(8,128)} %bitcast.17), channel_id=1, source_target_pairs={{0,8},{8,16},{16,24},{24,32},{32,40},{40,48},{48,56},{56,64},{64,7... | collective-permute-start | bytes 2359304 | tf_op jit(solution)/shard_map/ppermute | solution.py:9
  111.6 14.1 %copy-start = (f32[512]{0:T(512)S(1)}, f32[512]{0:T(512)}, u32[]{:S(2)}) copy-start(f32[512]{0:T(512)} %param.5) | copy-start | bytes 6148
  111.7 14.2 %collective-permute-start.2 = (f32[1]{0:T(128)}, f32[1]{0:T(128)}, u32[]{:S(2)}, u32[]{:S(2)}) collective-permute-start(f32[1]{0:T(128)} %param.4), channel_id=1, source_target_pairs={{0,8},{8,16},{16,24},{24,32},{32,40},{40,48},{48,56},{56,64},{64,7... | collective-permute-start | bytes 20 | tf_op jit(solution)/shard_map/ppermute | solution.py:9
  113.6 12.9 %collective-permute-start.3 = (f32[1]{0:T(128)}, f32[1]{0:T(128)}, u32[]{:S(2)}, u32[]{:S(2)}) collective-permute-start(f32[1]{0:T(128)} %param.4), channel_id=1, source_target_pairs={{0,760},{8,0},{16,8},{24,16},{32,24},{40,32},{48,40},{56,48},{64,5... | collective-permute-start | bytes 20 | tf_op jit(solution)/shard_map/ppermute | solution.py:9
Sparse Core Ops, SparseCore 0:
  111.8 77.7 all-reduce.1
where the time goes:
time: 206 us; the launch traced here: 205 us
  waiting for transfers between devices  139 us (67%)
  starting transfers between devices  35.5 us (17%)
  between operations  15.4 us (7%)
  matrix products  11.5 us (6%)
  other arithmetic  2.23 us (1%)
    ppermute x4, waiting for transfers between devices, passed_along(): return lax.ppermute(x, axis, [(i, (i + by) % size) for i in range(size)])  76.8 us
    psum x1, waiting for transfers between devices, amplitudes(): totals = lax.psum(tiles, 'aux')  62.3 us
    ppermute x4, starting transfers between devices, passed_along(): return lax.ppermute(x, axis, [(i, (i + by) % size) for i in range(size)])  35.5 us
    dot_general x1, matrix products, local(): jnp.einsum('nqa,nqb->nab', left, right, precision=lax.Precision.HIGHEST,...  6.2 us
  transfers between devices with their start and end apart: 5, of which 3 were waited for; matrix products, arithmetic and copies ran while one was open for 0% of the time, Pallas kernels for 0%

commit v1 on v0

v1 whole, which is shorter than its diff:
```python
import jax
import jax.numpy as jnp
from jax import lax
from jax.sharding import Mesh, PartitionSpec as P

CHIPS = 4


def cells(fn, occupied):
    pairs = []
    for i in range(occupied):
        for z in range(CHIPS):
            for h in range(2):
                j, w, k = fn(i, z, h)
                pairs.append(((i * CHIPS + z) * 2 + h, ((j % occupied) * CHIPS + w) * 2 + k))
    return pairs


ALL = ("occ", "z", "core")


def along_occ(x, by, cross):
    n = lax.axis_size("occ")
    return lax.ppermute(x, ALL, cells(lambda i, z, h: (i + by, z, h ^ cross), n))


def core_swap(x):
    return lax.ppermute(x, "core", [(0, 1), (1, 0)])


def local(factors, occ_energy, virt_energy):
    own = factors[0]
    rows, virt = own.shape
    half, quarter = virt // 2, virt // CHIPS
    core = lax.axis_index("core")
    z = lax.axis_index("z")

    same = lax.dynamic_slice_in_dim(own, core * half, half, 1)
    cross = lax.dynamic_slice_in_dim(own, (1 - core) * half, half, 1)
    low_same = along_occ(same, 1, 0)
    up_same = along_occ(same, -1, 0)
    low_cross = along_occ(cross, 1, 1)
    up_cross = along_occ(cross, -1, 1)
    other = core_swap(own)
    energy, other = lax.optimization_barrier((occ_energy, other))
    lower_energy = along_occ(energy, 1, 0)
    upper_energy = along_occ(energy, -1, 0)

    left = jnp.concatenate([own, other])
    right = jnp.concatenate(
        [jnp.concatenate([low_same, up_same], 1), jnp.concatenate([low_cross, up_cross], 1)]
    )
    tile = jnp.einsum("qa,qn->an", left, right, precision=lax.Precision.HIGH, preferred_element_type=jnp.float32)
    parts = lax.all_to_all(tile.reshape(CHIPS, quarter, virt), "z", 0, 0, tiled=True)
    total = (parts[0] + parts[1]) + (parts[2] + parts[3])
    row_energy = lax.dynamic_slice_in_dim(virt_energy, z * quarter, quarter, 0)
    half_energy = lax.dynamic_slice_in_dim(virt_energy, core * half, half, 0)
    column_energy = jnp.concatenate(
        [half_energy - (occ_energy + lower_energy), half_energy - (upper_energy + occ_energy)]
    )
    amps = total / (row_energy[:, None] + column_energy[None, :])
    pieces = [amps] + [lax.ppermute(amps, "z", [(k, k ^ d) for k in range(CHIPS)]) for d in (1, 2, 3)]
    def place(d):
        return lax.dynamic_index_in_dim(stacked, z ^ d, 0, keepdims=False)

    stacked = jnp.stack(pieces)
    whole = jnp.concatenate([place(d) for d in range(CHIPS)])
    partial = jnp.einsum("qn,an->qa", right, whole, precision=lax.Precision.HIGH, preferred_element_type=jnp.float32)
    return (partial[:rows] + core_swap(partial[rows:]))[None]


def solution(mesh):
    cube = Mesh(mesh.devices.reshape(mesh.devices.shape[0], CHIPS, 2), ALL)
    spec = P("occ", ("z", "core"), None)
    return jax.shard_map(local, mesh=cube, in_specs=(spec, P("occ"), P()), out_specs=spec, check_vma=False)
```

time: 206 us -> 171 us (0.83)
  waiting for transfers between devices: 139 us -> 97.4 us
  starting transfers between devices: 35.5 us -> 64.2 us
  between operations: 15.4 us -> 2.05 us
  matrix products: 11.5 us -> 3.88 us
    psum x1 -> x0, waiting for transfers between devices: 62.3 us -> none  [amplitudes(): totals = lax.psum(tiles, 'aux')]
    ppermute x4 -> x11, starting transfers between devices: 35.5 us -> 59.7 us  [the longest x6 35.3 us: along_occ(): lax.ppermute(x, ALL, cells(lambda i, z, h: (i + by, z, h ^ cross), n))]
    ppermute x4 -> x11, waiting for transfers between devices: 76.8 us -> 89.4 us  [the longest x6 70.6 us: along_occ(): lax.ppermute(x, ALL, cells(lambda i, z, h: (i + by, z, h ^ cross), n))]
    all_to_all x0 -> x1, waiting for transfers between devices: none -> 7.92 us  [local(): lax.all_to_all(tile.reshape(CHIPS, quarter, virt), 'z', 0, 0, tiled=True)]
    dot_general x3 -> x2, matrix products: 11.5 us -> 3.88 us  [the longest x1 2.41 us: local(): jnp.einsum('qa,qn->an', left, right, precision=lax.Precision.HIGH, prefer...]
    all_to_all x0 -> x1, starting transfers between devices: none -> 4.42 us  [local(): lax.all_to_all(tile.reshape(CHIPS, quarter, virt), 'z', 0, 0, tiled=True)]
  transfers between devices with their start and end apart: 5 -> 12, of which waited for: 3 -> 8; matrix products, arithmetic and copies ran while one was open for 0% -> 1% of each run, Pallas kernels for 0% -> 0%
where the time goes in v1:
time: 171 us; the launch traced here: 170 us
  waiting for transfers between devices  97.4 us (57%)
  starting transfers between devices  64.2 us (38%)
  matrix products  3.88 us (2%)
  between operations  2.05 us (1%)
    ppermute x6, waiting for transfers between devices, along_occ(): lax.ppermute(x, ALL, cells(lambda i, z, h: (i + by, z, h ^ cross), n))  70.6 us
    ppermute x6, starting transfers between devices, along_occ(): lax.ppermute(x, ALL, cells(lambda i, z, h: (i + by, z, h ^ cross), n))  35.3 us
    ppermute x3, waiting for transfers between devices, local(): lax.ppermute(amps, 'z', [(k, k ^ d) for k in range(CHIPS)])  17 us
    ppermute x2, starting transfers between devices, core_swap(): return lax.ppermute(x, 'core', [(0, 1), (1, 0)])  15.1 us
    ppermute x3, starting transfers between devices, local(): lax.ppermute(amps, 'z', [(k, k ^ d) for k in range(CHIPS)])  9.27 us
    all_to_all x1, waiting for transfers between devices, local(): lax.all_to_all(tile.reshape(CHIPS, quarter, virt), 'z', 0, 0, tiled=True)  7.92 us
    all_to_all x1, starting transfers between devices, local(): lax.all_to_all(tile.reshape(CHIPS, quarter, virt), 'z', 0, 0, tiled=True)  4.42 us
  transfers between devices with their start and end apart: 12, of which 8 were waited for; matrix products, arithmetic and copies ran while one was open for 1% of the time, Pallas kernels for 0%

profile of v1, /device:TPU:1, one launch (start us, length us, event | category | flops | bytes accessed | tf_op | source)
XLA Modules:
  0.0 170.3 jit_solution(10297506604160737239)
XLA Ops:
  0.0 12.5 %collective-permute-start.4 = (f32[384,512]{1,0:T(8,128)}, f32[384,512]{1,0:T(8,128)S(1)}, u32[]{:S(2)}, u32[]{:S(2)}) collective-permute-start(f32[384,512]{1,0:T(8,128)} %bitcast.23), channel_id=1, source_target_pairs={{0,1},{1,0},{2,3},{3,2},{4,5},{5,4},{6,7},{7,6},{8,9},{9,8},{10,11... | collective-permute-start | bytes 2359304 | tf_op jit(solution)/shard_map/ppermute | solution.py:28
  12.6 1.2 dynamic-slice_bitcast_fusion.1
  13.7 10.4 %collective-permute-start.1 = (f32[384,256]{1,0:T(8,128)S(1)}, f32[384,256]{1,0:T(8,128)S(1)}, u32[]{:S(2)}, u32[]{:S(2)}) collective-permute-start(f32[384,256]{1,0:T(8,128)S(1)} %get-tuple-element.15), channel_id=1, source_target_pairs={{0,760},{1,761},{2,762},{3,763},{4,764},{5,765},{6,766},{7,767},{8... | collective-permute-start | bytes 1179656 | tf_op jit(solution)/shard_map/ppermute | solution.py:24
  24.1 1.9 %collective-permute-start = (f32[384,256]{1,0:T(8,128)S(1)}, f32[384,256]{1,0:T(8,128)S(1)}, u32[]{:S(2)}, u32[]{:S(2)}) collective-permute-start(f32[384,256]{1,0:T(8,128)S(1)} %get-tuple-element.15), channel_id=1, source_target_pairs={{0,8},{1,9},{2,10},{3,11},{4,12},{5,13},{6,14},{7,15},{8,16},{9,17... | collective-permute-start | bytes 1179656 | tf_op jit(solution)/shard_map/ppermute | solution.py:24
  26.0 11.9 %collective-permute-start.3 = (f32[384,256]{1,0:T(8,128)S(1)}, f32[384,256]{1,0:T(8,128)S(1)}, u32[]{:S(2)}, u32[]{:S(2)}) collective-permute-start(f32[384,256]{1,0:T(8,128)S(1)} %get-tuple-element.16), channel_id=1, source_target_pairs={{0,761},{1,760},{2,763},{3,762},{4,765},{5,764},{6,767},{7,766},{8... | collective-permute-start | bytes 1179656 | tf_op jit(solution)/shard_map/ppermute | solution.py:24
  38.0 1.9 %collective-permute-start.2 = (f32[384,256]{1,0:T(8,128)S(1)}, f32[384,256]{1,0:T(8,128)S(1)}, u32[]{:S(2)}, u32[]{:S(2)}) collective-permute-start(f32[384,256]{1,0:T(8,128)S(1)} %get-tuple-element.16), channel_id=1, source_target_pairs={{0,9},{1,8},{2,11},{3,10},{4,13},{5,12},{6,15},{7,14},{8,17},{9,16... | collective-permute-start | bytes 1179656 | tf_op jit(solution)/shard_map/ppermute | solution.py:24
  39.9 37.6 %collective-permute-done.1 = f32[384,256]{1,0:T(8,128)S(1)} collective-permute-done((f32[384,256]{1,0:T(8,128)S(1)}, f32[384,256]{1,0:T(8,128)S(1)}, u32[]{:S(2)}, u32[]{:S(2)}) %collective-permute-start.1) | collective-permute-done | bytes 393248 | tf_op jit(solution)/shard_map/ppermute | solution.py:24
  77.5 8.5 %collective-permute-done.3 = f32[384,256]{1,0:T(8,128)S(1)} collective-permute-done((f32[384,256]{1,0:T(8,128)S(1)}, f32[384,256]{1,0:T(8,128)S(1)}, u32[]{:S(2)}, u32[]{:S(2)}) %collective-permute-start.3) | collective-permute-done | bytes 393248 | tf_op jit(solution)/shard_map/ppermute | solution.py:24
  86.0 18.0 %collective-permute-done.2 = f32[384,256]{1,0:T(8,128)S(1)} collective-permute-done((f32[384,256]{1,0:T(8,128)S(1)}, f32[384,256]{1,0:T(8,128)S(1)}, u32[]{:S(2)}, u32[]{:S(2)}) %collective-permute-start.2) | collective-permute-done | bytes 393248 | tf_op jit(solution)/shard_map/ppermute | solution.py:24
  104.0 2.4 %fusion = f32[512,512]{1,0:T(8,128)} fusion(f32[384,512]{1,0:T(8,128)S(1)} %collective-permute-done.4, f32[384,512]{1,0:T(8,128)S(1)} %bitcast.24, f32[384,256]{1,0:T(8,128)S(1)} %collective-permute-done.3, f32[384,256]{1,0:T(8,128)S(1)} %collective-permute-done.2, f32[384,256]{1,0:T(8,128)S(1)} %collective-permute-done.1, ...), kind=kOutput, calls=%fused_computation.1 | convolution fusion | flops 1209532416 | bytes 4194304 | tf_op jit(solution)/shard_map/qa,qn->an/dot_general | solution.py:53
  106.4 4.4 %all-to-all-start = ((f32[4,128,512]{2,1,0:T(8,128)}), f32[4,128,512]{2,1,0:T(8,128)S(1)}, u32[]{:S(2)}, u32[]{:S(2)}) async-start(f32[4,128,512]{2,1,0:T(8,128)} %bitcast.3), calls=%async_computation | async-start | bytes 2097152 | tf_op jit(solution)/shard_map/all_to_all | solution.py:54
  111.6 1.9 %collective-permute-start.6 = (f32[1]{0:T(128)}, f32[1]{0:T(128)}, u32[]{:S(2)}, u32[]{:S(2)}) collective-permute-start(f32[1]{0:T(128)} %param.4), channel_id=1, source_target_pairs={{0,760},{1,761},{2,762},{3,763},{4,764},{5,765},{6,766},{7,767},{8... | collective-permute-start | bytes 20 | tf_op jit(solution)/shard_map/ppermute | solution.py:24
  113.5 7.3 %collective-permute-start.5 = (f32[1]{0:T(128)}, f32[1]{0:T(128)}, u32[]{:S(2)}, u32[]{:S(2)}) collective-permute-start(f32[1]{0:T(128)} %param.4), channel_id=1, source_target_pairs={{0,8},{1,9},{2,10},{3,11},{4,12},{5,13},{6,14},{7,15},{8,16},{9,17... | collective-permute-start | bytes 20 | tf_op jit(solution)/shard_map/ppermute | solution.py:24
  121.4 6.5 %collective-permute-done.5 = f32[1]{0:T(128)} collective-permute-done((f32[1]{0:T(128)}, f32[1]{0:T(128)}, u32[]{:S(2)}, u32[]{:S(2)}) %collective-permute-start.5) | collective-permute-done | bytes 36 | tf_op jit(solution)/shard_map/ppermute | solution.py:24
  128.6 7.9 %all-to-all-done = f32[4,128,512]{2,1,0:T(8,128)S(1)} async-done(((f32[4,128,512]{2,1,0:T(8,128)}), f32[4,128,512]{2,1,0:T(8,128)S(1)}, u32[]{:S(2)}, u32[]{:S(2)}) %all-to-all-start) | async-done | bytes 1048608 | tf_op jit(solution)/shard_map/all_to_all | solution.py:54
  136.8 3.1 %collective-permute-start.9 = (f32[128,512]{1,0:T(8,128)S(1)}, f32[128,512]{1,0:T(8,128)S(1)}, u32[]{:S(2)}, u32[]{:S(2)}) collective-permute-start(f32[128,512]{1,0:T(8,128)S(1)} %bitcast_divide_fusion), channel_id=1, source_target_pairs={{0,6},{2,4},{4,2},{6,0},{1,7},{3,5},{5,3},{7,1},{8,14},{10,12},{12... | collective-permute-start | bytes 786440 | tf_op jit(solution)/shard_map/ppermute | solution.py:62
  139.8 1.9 %collective-permute-start.8 = (f32[128,512]{1,0:T(8,128)S(1)}, f32[128,512]{1,0:T(8,128)S(1)}, u32[]{:S(2)}, u32[]{:S(2)}) collective-permute-start(f32[128,512]{1,0:T(8,128)S(1)} %bitcast_divide_fusion), channel_id=1, source_target_pairs={{0,4},{2,6},{4,0},{6,2},{1,5},{3,7},{5,1},{7,3},{8,12},{10,14},{12... | collective-permute-start | bytes 786440 | tf_op jit(solution)/shard_map/ppermute | solution.py:62
  141.8 4.3 %collective-permute-start.7 = (f32[128,512]{1,0:T(8,128)S(1)}, f32[128,512]{1,0:T(8,128)S(1)}, u32[]{:S(2)}, u32[]{:S(2)}) collective-permute-start(f32[128,512]{1,0:T(8,128)S(1)} %bitcast_divide_fusion), channel_id=1, source_target_pairs={{0,2},{2,0},{4,6},{6,4},{1,3},{3,1},{5,7},{7,5},{8,10},{10,8},{12,... | collective-permute-start | bytes 786440 | tf_op jit(solution)/shard_map/ppermute | solution.py:62
  146.1 1.9 %collective-permute-done.9 = f32[128,512]{1,0:T(8,128)S(1)} collective-permute-done((f32[128,512]{1,0:T(8,128)S(1)}, f32[128,512]{1,0:T(8,128)S(1)}, u32[]{:S(2)}, u32[]{:S(2)}) %collective-permute-start.9) | collective-permute-done | bytes 262176 | tf_op jit(solution)/shard_map/ppermute | solution.py:62
  148.0 15.1 %collective-permute-done.8 = f32[128,512]{1,0:T(8,128)S(1)} collective-permute-done((f32[128,512]{1,0:T(8,128)S(1)}, f32[128,512]{1,0:T(8,128)S(1)}, u32[]{:S(2)}, u32[]{:S(2)}) %collective-permute-start.8) | collective-permute-done | bytes 262176 | tf_op jit(solution)/shard_map/ppermute | solution.py:62
  163.2 1.5 fusion.4
  164.8 2.6 %collective-permute-start.10 = (f32[384,512]{1,0:T(8,128)S(1)}, f32[384,512]{1,0:T(8,128)S(1)}, u32[]{:S(2)}, u32[]{:S(2)}) collective-permute-start(f32[384,512]{1,0:T(8,128)S(1)} %slice.29), channel_id=1, source_target_pairs={{0,1},{1,0},{2,3},{3,2},{4,5},{5,4},{6,7},{7,6},{8,9},{9,8},{10,11... | collective-permute-start | bytes 2359304 | tf_op jit(solution)/shard_map/ppermute | solution.py:28
  167.4 1.9 %collective-permute-done.10 = f32[384,512]{1,0:T(8,128)S(1)} collective-permute-done((f32[384,512]{1,0:T(8,128)S(1)}, f32[384,512]{1,0:T(8,128)S(1)}, u32[]{:S(2)}, u32[]{:S(2)}) %collective-permute-start.10) | collective-permute-done | bytes 786464 | tf_op jit(solution)/shard_map/ppermute | solution.py:28
  169.2 1.0 fusion.12
  (16 shorter events, 0.6 us)
Async XLA Ops:
  0.0 104.0 %copy-start = (f32[1,384,512]{2,1,0:T(8,128)S(1)}, f32[1,384,512]{2,1,0:T(8,128)}, u32[]{:S(2)}) copy-start(f32[1,384,512]{2,1,0:T(8,128)} %param.3) | copy-start | bytes 2359300
  0.0 39.9 %collective-permute-start.4 = (f32[384,512]{1,0:T(8,128)}, f32[384,512]{1,0:T(8,128)S(1)}, u32[]{:S(2)}, u32[]{:S(2)}) collective-permute-start(f32[384,512]{1,0:T(8,128)} %bitcast.23), channel_id=1, source_target_pairs={{0,1},{1,0},{2,3},{3,2},{4,5},{5,4},{6,7},{7,6},{8,9},{9,8},{10,11... | collective-permute-start | bytes 2359304 | tf_op jit(solution)/shard_map/ppermute | solution.py:28
  13.7 63.8 %collective-permute-start.1 = (f32[384,256]{1,0:T(8,128)S(1)}, f32[384,256]{1,0:T(8,128)S(1)}, u32[]{:S(2)}, u32[]{:S(2)}) collective-permute-start(f32[384,256]{1,0:T(8,128)S(1)} %get-tuple-element.15), channel_id=1, source_target_pairs={{0,760},{1,761},{2,762},{3,763},{4,764},{5,765},{6,766},{7,767},{8... | collective-permute-start | bytes 1179656 | tf_op jit(solution)/shard_map/ppermute | solution.py:24
  24.1 53.4 %collective-permute-start = (f32[384,256]{1,0:T(8,128)S(1)}, f32[384,256]{1,0:T(8,128)S(1)}, u32[]{:S(2)}, u32[]{:S(2)}) collective-permute-start(f32[384,256]{1,0:T(8,128)S(1)} %get-tuple-element.15), channel_id=1, source_target_pairs={{0,8},{1,9},{2,10},{3,11},{4,12},{5,13},{6,14},{7,15},{8,16},{9,17... | collective-permute-start | bytes 1179656 | tf_op jit(solution)/shard_map/ppermute | solution.py:24
  26.0 60.0 %collective-permute-start.3 = (f32[384,256]{1,0:T(8,128)S(1)}, f32[384,256]{1,0:T(8,128)S(1)}, u32[]{:S(2)}, u32[]{:S(2)}) collective-permute-start(f32[384,256]{1,0:T(8,128)S(1)} %get-tuple-element.16), channel_id=1, source_target_pairs={{0,761},{1,760},{2,763},{3,762},{4,765},{5,764},{6,767},{7,766},{8... | collective-permute-start | bytes 1179656 | tf_op jit(solution)/shard_map/ppermute | solution.py:24
  38.0 66.0 %collective-permute-start.2 = (f32[384,256]{1,0:T(8,128)S(1)}, f32[384,256]{1,0:T(8,128)S(1)}, u32[]{:S(2)}, u32[]{:S(2)}) collective-permute-start(f32[384,256]{1,0:T(8,128)S(1)} %get-tuple-element.16), channel_id=1, source_target_pairs={{0,9},{1,8},{2,11},{3,10},{4,13},{5,12},{6,15},{7,14},{8,17},{9,16... | collective-permute-start | bytes 1179656 | tf_op jit(solution)/shard_map/ppermute | solution.py:24
  106.4 5.1 %copy-start.1 = (f32[512]{0:T(512)S(1)}, f32[512]{0:T(512)}, u32[]{:S(2)}) copy-start(f32[512]{0:T(512)} %param.5) | copy-start | bytes 6148
  106.4 30.1 %all-to-all-start = ((f32[4,128,512]{2,1,0:T(8,128)}), f32[4,128,512]{2,1,0:T(8,128)S(1)}, u32[]{:S(2)}, u32[]{:S(2)}) async-start(f32[4,128,512]{2,1,0:T(8,128)} %bitcast.3), calls=%async_computation | async-start | bytes 2097152 | tf_op jit(solution)/shard_map/all_to_all | solution.py:54
  111.6 9.2 %collective-permute-start.6 = (f32[1]{0:T(128)}, f32[1]{0:T(128)}, u32[]{:S(2)}, u32[]{:S(2)}) collective-permute-start(f32[1]{0:T(128)} %param.4), channel_id=1, source_target_pairs={{0,760},{1,761},{2,762},{3,763},{4,764},{5,765},{6,766},{7,767},{8... | collective-permute-start | bytes 20 | tf_op jit(solution)/shard_map/ppermute | solution.py:24
  113.5 14.4 %collective-permute-start.5 = (f32[1]{0:T(128)}, f32[1]{0:T(128)}, u32[]{:S(2)}, u32[]{:S(2)}) collective-permute-start(f32[1]{0:T(128)} %param.4), channel_id=1, source_target_pairs={{0,8},{1,9},{2,10},{3,11},{4,12},{5,13},{6,14},{7,15},{8,16},{9,17... | collective-permute-start | bytes 20 | tf_op jit(solution)/shard_map/ppermute | solution.py:24
  136.8 11.2 %collective-permute-start.9 = (f32[128,512]{1,0:T(8,128)S(1)}, f32[128,512]{1,0:T(8,128)S(1)}, u32[]{:S(2)}, u32[]{:S(2)}) collective-permute-start(f32[128,512]{1,0:T(8,128)S(1)} %bitcast_divide_fusion), channel_id=1, source_target_pairs={{0,6},{2,4},{4,2},{6,0},{1,7},{3,5},{5,3},{7,1},{8,14},{10,12},{12... | collective-permute-start | bytes 786440 | tf_op jit(solution)/shard_map/ppermute | solution.py:62
  139.8 23.2 %collective-permute-start.8 = (f32[128,512]{1,0:T(8,128)S(1)}, f32[128,512]{1,0:T(8,128)S(1)}, u32[]{:S(2)}, u32[]{:S(2)}) collective-permute-start(f32[128,512]{1,0:T(8,128)S(1)} %bitcast_divide_fusion), channel_id=1, source_target_pairs={{0,4},{2,6},{4,0},{6,2},{1,5},{3,7},{5,1},{7,3},{8,12},{10,14},{12... | collective-permute-start | bytes 786440 | tf_op jit(solution)/shard_map/ppermute | solution.py:62
  141.8 21.3 %collective-permute-start.7 = (f32[128,512]{1,0:T(8,128)S(1)}, f32[128,512]{1,0:T(8,128)S(1)}, u32[]{:S(2)}, u32[]{:S(2)}) collective-permute-start(f32[128,512]{1,0:T(8,128)S(1)} %bitcast_divide_fusion), channel_id=1, source_target_pairs={{0,2},{2,0},{4,6},{6,4},{1,3},{3,1},{5,7},{7,5},{8,10},{10,8},{12,... | collective-permute-start | bytes 786440 | tf_op jit(solution)/shard_map/ppermute | solution.py:62
  164.8 4.5 %collective-permute-start.10 = (f32[384,512]{1,0:T(8,128)S(1)}, f32[384,512]{1,0:T(8,128)S(1)}, u32[]{:S(2)}, u32[]{:S(2)}) collective-permute-start(f32[384,512]{1,0:T(8,128)S(1)} %slice.29), channel_id=1, source_target_pairs={{0,1},{1,0},{2,3},{3,2},{4,5},{5,4},{6,7},{7,6},{8,9},{9,8},{10,11... | collective-permute-start | bytes 2359304 | tf_op jit(solution)/shard_map/ppermute | solution.py:28

commit v2 on v1

v2 whole, which is shorter than its diff:
```python
import jax
import jax.numpy as jnp
from jax import lax
from jax.sharding import Mesh, PartitionSpec as P

CHIPS = 4
ALL = ("occ", "z", "core")
PRECISION = lax.Precision.HIGH


def along_occ(x, by):
    n = lax.axis_size("occ")
    return lax.ppermute(x, "occ", [(i, (i + by) % n) for i in range(n)])


def core_swap(x):
    return lax.ppermute(x, "core", [(0, 1), (1, 0)])


def local(factors, occ_energy, virt_energy):
    own = factors[0]
    rows, virt = own.shape
    half, quarter = virt // 2, virt // CHIPS
    core = lax.axis_index("core")
    z = lax.axis_index("z")

    chip = jnp.concatenate([own, core_swap(own)])
    columns = lax.dynamic_slice_in_dim(chip, core * half, half, 1)
    parcel = jnp.concatenate([columns, jnp.broadcast_to(occ_energy, (8, half))])
    lower = along_occ(parcel, 1)
    upper = along_occ(parcel, -1)
    right = jnp.concatenate([lower[: 2 * rows], upper[: 2 * rows]], 1)
    tile = jnp.einsum("qa,qn->an", chip, right, precision=PRECISION, preferred_element_type=jnp.float32)
    parts = lax.all_to_all(tile.reshape(CHIPS, quarter, virt), "z", 0, 0, tiled=True)
    total = (parts[0] + parts[1]) + (parts[2] + parts[3])
    row_energy = lax.dynamic_slice_in_dim(virt_energy, z * quarter, quarter, 0)
    half_energy = lax.dynamic_slice_in_dim(virt_energy, core * half, half, 0)
    column_energy = jnp.concatenate(
        [half_energy - (occ_energy + lower[2 * rows, 0]), half_energy - (upper[2 * rows, 0] + occ_energy)]
    )
    amps = total / (row_energy[:, None] + column_energy[None, :])
    whole = lax.all_to_all(jnp.broadcast_to(amps, (CHIPS, quarter, virt)), "z", 0, 0, tiled=True)
    whole = whole.reshape(virt, virt)
    partial = jnp.einsum("qn,an->qa", right, whole, precision=PRECISION, preferred_element_type=jnp.float32)
    return (partial[:rows] + core_swap(partial[rows:]))[None]


def solution(mesh):
    cube = Mesh(mesh.devices.reshape(mesh.devices.shape[0], CHIPS, 2), ALL)
    spec = P("occ", ("z", "core"), None)
    return jax.shard_map(local, mesh=cube, in_specs=(spec, P("occ"), P()), out_specs=spec, check_vma=False)
```

time: 171 us -> 174 us (1.018)
  starting transfers between devices: 64.2 us -> 32.3 us
  blocking collectives: 0 us -> 27.3 us
  waiting for transfers between devices: 97.4 us -> 103 us
  local copies, waits for them, and re-layouts: 1.39 us -> 3.18 us
    ppermute x9 -> x2, starting transfers between devices: 44.6 us -> 12.4 us  [along_occ(): return lax.ppermute(x, 'occ', [(i, (i + by) % n) for i in range(n)])]
    all_to_all x0 -> x1, blocking collectives: none -> 27.3 us  [local(): lax.all_to_all(jnp.broadcast_to(amps, (CHIPS, quarter, virt)), 'z', 0, 0,...]
    all_to_all x1, waiting for transfers between devices: 7.92 us -> 21.8 us  [local(): lax.all_to_all(tile.reshape(CHIPS, quarter, virt), 'z', 0, 0, tiled=True)]
    ppermute x9 -> x2, waiting for transfers between devices: 87.6 us -> 77.6 us  [along_occ(): return lax.ppermute(x, 'occ', [(i, (i + by) % n) for i in range(n)])]
    slice x0 -> x4, local copies, waits for them, and re-layouts: none -> 1.92 us  [the longest x1 1.25 us: local(): lower[2 * rows, 0]]
  transfers between devices with their start and end apart: 12 -> 5, of which waited for: 8 -> 5; matrix products, arithmetic and copies ran while one was open for 1% -> 1% of each run, Pallas kernels for 0% -> 0%
where the time goes in v2:
time: 174 us
  waiting for transfers between devices  103 us (59%)
  starting transfers between devices  32.3 us (19%)
  blocking collectives  27.3 us (16%)
  matrix products  3.91 us (2%)
  local copies, waits for them, and re-layouts  3.18 us (2%)
  other arithmetic  2.28 us (1%)
  between operations  2.12 us (1%)
    ppermute x2, waiting for transfers between devices, along_occ(): return lax.ppermute(x, 'occ', [(i, (i + by) % n) for i in range(n)])  77.6 us
    all_to_all x1, blocking collectives, local(): lax.all_to_all(jnp.broadcast_to(amps, (CHIPS, quarter, virt)), 'z', 0, 0,...  27.3 us
    all_to_all x1, waiting for transfers between devices, local(): lax.all_to_all(tile.reshape(CHIPS, quarter, virt), 'z', 0, 0, tiled=True)  21.8 us
    ppermute x2, starting transfers between devices, core_swap(): return lax.ppermute(x, 'core', [(0, 1), (1, 0)])  16.2 us
    ppermute x2, starting transfers between devices, along_occ(): return lax.ppermute(x, 'occ', [(i, (i + by) % n) for i in range(n)])  12.4 us
    all_to_all x1, starting transfers between devices, local(): lax.all_to_all(tile.reshape(CHIPS, quarter, virt), 'z', 0, 0, tiled=True)  3.65 us
  transfers between devices with their start and end apart: 5, of which 5 were waited for; matrix products, arithmetic and copies ran while one was open for 1% of the time, Pallas kernels for 0%

profile of v2, /device:TPU:1, one launch (start us, length us, event | category | flops | bytes accessed | tf_op | source)
XLA Modules:
  0.0 173.7 jit_solution(11344549235404652480)
XLA Ops:
  0.0 12.4 %collective-permute-start = (f32[384,512]{1,0:T(8,128)}, f32[384,512]{1,0:T(8,128)S(1)}, u32[]{:S(2)}, u32[]{:S(2)}) collective-permute-start(f32[384,512]{1,0:T(8,128)} %bitcast.18), channel_id=1, source_target_pairs={{0,1},{1,0},{2,3},{3,2},{4,5},{5,4},{6,7},{7,6},{8,9},{9,8},{10,11... | collective-permute-start | bytes 2359304 | tf_op jit(solution)/shard_map/ppermute | solution.py:17
  13.1 1.4 collective-permute-done
  14.5 1.1 fusion.2
  15.6 0.1 concatenate.13
  15.7 10.5 %collective-permute-start.2 = (f32[776,256]{1,0:T(8,128)S(1)}, f32[776,256]{1,0:T(8,128)S(1)}, u32[]{:S(2)}, u32[]{:S(2)}) collective-permute-start(f32[776,256]{1,0:T(8,128)S(1)} %concatenate.13), channel_id=1, source_target_pairs={{0,760},{8,0},{16,8},{24,16},{32,24},{40,32},{48,40},{56,48},{64,5... | collective-permute-start | bytes 2383880 | tf_op jit(solution)/shard_map/ppermute | solution.py:13
  26.2 1.9 %collective-permute-start.1 = (f32[776,256]{1,0:T(8,128)S(1)}, f32[776,256]{1,0:T(8,128)S(1)}, u32[]{:S(2)}, u32[]{:S(2)}) collective-permute-start(f32[776,256]{1,0:T(8,128)S(1)} %concatenate.13), channel_id=1, source_target_pairs={{0,8},{8,16},{16,24},{24,32},{32,40},{40,48},{48,56},{56,64},{64,7... | collective-permute-start | bytes 2383880 | tf_op jit(solution)/shard_map/ppermute | solution.py:13
  28.1 60.5 %collective-permute-done.2 = f32[776,256]{1,0:T(8,128)S(1)} collective-permute-done((f32[776,256]{1,0:T(8,128)S(1)}, f32[776,256]{1,0:T(8,128)S(1)}, u32[]{:S(2)}, u32[]{:S(2)}) %collective-permute-start.2) | collective-permute-done | bytes 794656 | tf_op jit(solution)/shard_map/ppermute | solution.py:13
  88.7 17.0 %collective-permute-done.1 = f32[776,256]{1,0:T(8,128)S(1)} collective-permute-done((f32[776,256]{1,0:T(8,128)S(1)}, f32[776,256]{1,0:T(8,128)S(1)}, u32[]{:S(2)}, u32[]{:S(2)}) %collective-permute-start.1) | collective-permute-done | bytes 794656 | tf_op jit(solution)/shard_map/ppermute | solution.py:13
  105.7 0.9 copy-done.1
  106.7 2.4 %fusion = f32[512,512]{1,0:T(8,128)} fusion(f32[384,512]{1,0:T(8,128)S(1)} %collective-permute-done, f32[384,512]{1,0:T(8,128)S(1)} %bitcast.20, f32[768,256]{1,0:T(8,128)S(1)} %slice.41, f32[768,256]{1,0:T(8,128)S(1)} %slice.40), kind=kOutput, calls=%fused_computation.3 | convolution fusion | flops 1208745984 | bytes 4194304 | tf_op jit(solution)/shard_map/qa,qn->an/dot_general | solution.py:33
  109.2 3.6 %all-to-all-start = ((f32[4,128,512]{2,1,0:T(8,128)}), f32[4,128,512]{2,1,0:T(8,128)S(1)}, u32[]{:S(2)}, u32[]{:S(2)}) async-start(f32[4,128,512]{2,1,0:T(8,128)} %bitcast.16), calls=%async_computation | async-start | bytes 2097152 | tf_op jit(solution)/shard_map/all_to_all | solution.py:34
  112.8 0.1 dynamic_slice.10
  112.9 0.6 slice.47
  114.1 1.2 slice.46
  116.1 0.1 dynamic-slice_subtract_fusion.1
  116.2 21.8 %all-to-all-done = f32[4,128,512]{2,1,0:T(8,128)S(1)} async-done(((f32[4,128,512]{2,1,0:T(8,128)}), f32[4,128,512]{2,1,0:T(8,128)S(1)}, u32[]{:S(2)}, u32[]{:S(2)}) %all-to-all-start) | async-done | bytes 1048608 | tf_op jit(solution)/shard_map/all_to_all | solution.py:34
  138.0 0.1 fusion.6
  138.1 0.1 broadcast_in_dim.4
  138.2 27.3 %all_to_all.10 = f32[4,128,512]{2,1,0:T(8,128)S(1)} all-to-all(f32[4,128,512]{2,1,0:T(8,128)S(1)} %broadcast_in_dim.4), channel_id=1, replica_groups=mesh['occ'=96,'z'=4,'core'=2] {'z'}, dimensions={0} | all-to-all | bytes 2097152 | tf_op jit(solution)/shard_map/all_to_all | solution.py:42
  165.5 1.5 fusion.1
  167.0 0.1 slice.49
  167.0 3.8 %collective-permute-start.3 = (f32[384,512]{1,0:T(8,128)S(1)}, f32[384,512]{1,0:T(8,128)S(1)}, u32[]{:S(2)}, u32[]{:S(2)}) collective-permute-start(f32[384,512]{1,0:T(8,128)S(1)} %slice.49), channel_id=1, source_target_pairs={{0,1},{1,0},{2,3},{3,2},{4,5},{5,4},{6,7},{7,6},{8,9},{9,8},{10,11... | collective-permute-start | bytes 2359304 | tf_op jit(solution)/shard_map/ppermute | solution.py:17
  170.8 1.9 %collective-permute-done.3 = f32[384,512]{1,0:T(8,128)S(1)} collective-permute-done((f32[384,512]{1,0:T(8,128)S(1)}, f32[384,512]{1,0:T(8,128)S(1)}, u32[]{:S(2)}, u32[]{:S(2)}) %collective-permute-start.3) | collective-permute-done | bytes 786464 | tf_op jit(solution)/shard_map/ppermute | solution.py:17
  172.7 1.0 fusion.3
  (8 shorter events, 0.1 us)
Async XLA Ops:
  0.0 14.5 %collective-permute-start = (f32[384,512]{1,0:T(8,128)}, f32[384,512]{1,0:T(8,128)S(1)}, u32[]{:S(2)}, u32[]{:S(2)}) collective-permute-start(f32[384,512]{1,0:T(8,128)} %bitcast.18), channel_id=1, source_target_pairs={{0,1},{1,0},{2,3},{3,2},{4,5},{5,4},{6,7},{7,6},{8,9},{9,8},{10,11... | collective-permute-start | bytes 2359304 | tf_op jit(solution)/shard_map/ppermute | solution.py:17
  15.6 91.1 %copy-start = (f32[1,384,512]{2,1,0:T(8,128)S(1)}, f32[1,384,512]{2,1,0:T(8,128)}, u32[]{:S(2)}) copy-start(f32[1,384,512]{2,1,0:T(8,128)} %param.3) | copy-start | bytes 2359300
  15.7 73.0 %collective-permute-start.2 = (f32[776,256]{1,0:T(8,128)S(1)}, f32[776,256]{1,0:T(8,128)S(1)}, u32[]{:S(2)}, u32[]{:S(2)}) collective-permute-start(f32[776,256]{1,0:T(8,128)S(1)} %concatenate.13), channel_id=1, source_target_pairs={{0,760},{8,0},{16,8},{24,16},{32,24},{40,32},{48,40},{56,48},{64,5... | collective-permute-start | bytes 2383880 | tf_op jit(solution)/shard_map/ppermute | solution.py:13
  26.2 79.5 %collective-permute-start.1 = (f32[776,256]{1,0:T(8,128)S(1)}, f32[776,256]{1,0:T(8,128)S(1)}, u32[]{:S(2)}, u32[]{:S(2)}) collective-permute-start(f32[776,256]{1,0:T(8,128)S(1)} %concatenate.13), channel_id=1, source_target_pairs={{0,8},{8,16},{16,24},{24,32},{32,40},{40,48},{48,56},{56,64},{64,7... | collective-permute-start | bytes 2383880 | tf_op jit(solution)/shard_map/ppermute | solution.py:13
  105.7 0.9 copy-start.1
  109.2 3.7 %copy-start.2 = (f32[512]{0:T(512)S(1)}, f32[512]{0:T(512)}, u32[]{:S(2)}) copy-start(f32[512]{0:T(512)} %param.5) | copy-start | bytes 6148
  109.2 28.8 %all-to-all-start = ((f32[4,128,512]{2,1,0:T(8,128)}), f32[4,128,512]{2,1,0:T(8,128)S(1)}, u32[]{:S(2)}, u32[]{:S(2)}) async-start(f32[4,128,512]{2,1,0:T(8,128)} %bitcast.16), calls=%async_computation | async-start | bytes 2097152 | tf_op jit(solution)/shard_map/all_to_all | solution.py:34
  167.0 5.7 %collective-permute-start.3 = (f32[384,512]{1,0:T(8,128)S(1)}, f32[384,512]{1,0:T(8,128)S(1)}, u32[]{:S(2)}, u32[]{:S(2)}) collective-permute-start(f32[384,512]{1,0:T(8,128)S(1)} %slice.49), channel_id=1, source_target_pairs={{0,1},{1,0},{2,3},{3,2},{4,5},{5,4},{6,7},{7,6},{8,9},{9,8},{10,11... | collective-permute-start | bytes 2359304 | tf_op jit(solution)/shard_map/ppermute | solution.py:17

commit v3 on v2

v3 whole, which is shorter than its diff:
```python
import jax
import jax.numpy as jnp
from jax import lax
from jax.experimental import pallas as pl
from jax.experimental.pallas import tpu as pltpu
from jax.sharding import Mesh, PartitionSpec as P

CHIPS = 4
ALL = ("occ", "z", "core")
SMEM = pl.BlockSpec(memory_space=pltpu.SMEM)
VMEM = pl.BlockSpec(memory_space=pltpu.VMEM)
ANY = pl.BlockSpec(memory_space=pl.ANY)


def along_occ(x, by, cross=0):
    n = lax.axis_size("occ")
    pairs = [
        ((i * CHIPS + z) * 2 + h, ((i + by) % n * CHIPS + z) * 2 + (h ^ cross))
        for i in range(n)
        for z in range(CHIPS)
        for h in range(2)
    ]
    return lax.ppermute(x, ALL, pairs)


def core_swap(x):
    return lax.ppermute(x, "core", [(0, 1), (1, 0)])


def kernel(body, shapes, scalars, arrays, after=(), flops=0):
    used = len(scalars) + len(arrays)

    def run(*refs):
        body(*refs[:used], *refs[used + len(after) :])

    return pl.pallas_call(
        run,
        out_shape=[jax.ShapeDtypeStruct(s, jnp.float32) for s in shapes],
        in_specs=[SMEM] * len(scalars) + [VMEM] * len(arrays) + [ANY] * len(after),
        out_specs=[VMEM] * len(shapes),
        cost_estimate=pl.CostEstimate(flops=flops, bytes_accessed=0, transcendentals=0),
        compiler_params=pltpu.CompilerParams(vmem_limit_bytes=40 * 2**20),
    )(*[s.reshape(1) for s in scalars], *arrays, *after)


def split(x):
    high = x.astype(jnp.bfloat16)
    return high, (x - high.astype(jnp.float32)).astype(jnp.bfloat16)


def dot(x, y, dims):
    x_high, x_low = split(x)
    y_high, y_low = split(y)

    def one(u, v):
        return lax.dot_general(u, v, (dims, ((), ())), preferred_element_type=jnp.float32)

    return one(x_high, y_high) + (one(x_high, y_low) + one(x_low, y_high))


def pair_tile(own_ref, other_ref, near_ref, far_ref, out_ref):
    rows = own_ref.shape[0]
    chip = jnp.concatenate([own_ref[...], other_ref[...]])
    right = jnp.concatenate([near_ref[:rows], far_ref[...]])
    out_ref[...] = dot(chip, right, ((0,), (0,))).reshape(out_ref.shape)


def divide(parts_ref, denominator_ref, tile_ref, out_ref):
    total = (parts_ref[0] + parts_ref[1]) + (parts_ref[2] + parts_ref[3])
    amplitude = total / denominator_ref[...]
    tile_ref[...] = amplitude
    for k in range(CHIPS):
        out_ref[k] = amplitude


def repeat(tile_ref, out_ref):
    for k in range(CHIPS):
        out_ref[k] = tile_ref[...]


def lower_part(near_ref, far_ref, amp_ref, mine_ref, others_ref):
    rows, virt = mine_ref.shape
    right = jnp.concatenate([near_ref[:rows], far_ref[...]])
    product = dot(right, amp_ref[...].reshape(virt, -1), ((1,), (1,)))
    mine_ref[...] = product[:rows]
    others_ref[...] = product[rows:]


def upper_part(here_ref, up_ref, up_other_ref, amp_ref, mine_ref, others_ref, out_ref, out_others_ref):
    rows, virt = mine_ref.shape
    chip = jnp.concatenate([up_ref[...], up_other_ref[...]])
    product = dot(chip, amp_ref[...].reshape(virt, -1), ((1,), (0,)))
    width = product.shape[1]
    columns = pl.ds(pl.multiple_of(here_ref[0], width), width)
    out_ref[...] = mine_ref[...]
    out_ref[:, columns] += product[:rows]
    out_others_ref[...] = others_ref[...]
    out_others_ref[:, columns] += product[rows:]


def local(factors, occ_energy, virt_energy):
    own = factors[0]
    rows, virt = own.shape
    half, quarter = virt // 2, virt // CHIPS
    core = lax.axis_index("core")
    z = lax.axis_index("z")
    here = core * half

    def columns(start):
        return lax.dynamic_slice_in_dim(own, start, half, 1)

    def shared(x):
        return lax.all_to_all(x, "z", 0, 0, tiled=True)

    near = along_occ(jnp.concatenate([columns(here), jnp.broadcast_to(occ_energy, (8, half))]), 1)
    far = along_occ(columns(half - here), 1, cross=1)
    upper = along_occ(own, -1)
    other = core_swap(own)
    upper_other = core_swap(upper)

    row_energy = lax.dynamic_slice_in_dim(virt_energy, z * quarter, quarter, 0) - (occ_energy + near[rows, 0])
    denominator = row_energy[:, None] + lax.dynamic_slice_in_dim(virt_energy, here, half, 0)[None, :]

    whole = (CHIPS, quarter, half)
    parts = shared(kernel(pair_tile, [whole], [], [own, other, near, far])[0])
    tile, copies = kernel(divide, [(quarter, half), whole], [], [parts, denominator], (upper_other,))
    upper_tile = along_occ(tile, -1)
    amp = shared(copies)
    upper_amp = shared(kernel(repeat, [whole], [], [upper_tile])[0])
    slab = (rows, virt)
    mine, others = kernel(lower_part, [slab] * 2, [], [near, far, amp])
    mine, others = kernel(upper_part, [slab] * 2, [here], [upper, upper_other, upper_amp, mine, others])
    return (mine + core_swap(others))[None]


def solution(mesh):
    cube = Mesh(mesh.devices.reshape(mesh.devices.shape[0], CHIPS, 2), ALL)
    spec = P("occ", ("z", "core"), None)
    return jax.shard_map(local, mesh=cube, in_specs=(spec, P("occ"), P()), out_specs=spec, check_vma=False)
```

time: 174 us -> 169 us (0.971)
  starting transfers between devices: 32.3 us -> 98.9 us
  waiting for transfers between devices: 103 us -> 55.3 us
  blocking collectives: 27.3 us -> 0 us
  Pallas kernels: 0 us -> 4.97 us
  matrix products: 3.91 us -> 0 us
  local copies, waits for them, and re-layouts: 3.18 us -> 6.56 us
    ppermute x2 -> x4, waiting for transfers between devices: 77.6 us -> 21 us  [along_occ(): return lax.ppermute(x, ALL, pairs)]
    all_to_all x1 -> x3, starting transfers between devices: 3.65 us -> 58.8 us  [shared(): return lax.all_to_all(x, 'z', 0, 0, tiled=True)]
    all_to_all x1 -> x0, blocking collectives: 27.3 us -> none  [local(): lax.all_to_all(jnp.broadcast_to(amps, (CHIPS, quarter, virt)), 'z', 0, 0,...]
    all_to_all x1 -> x3, waiting for transfers between devices: 21.8 us -> 32.5 us  [shared(): return lax.all_to_all(x, 'z', 0, 0, tiled=True)]
    ppermute x2 -> x4, starting transfers between devices: 12.4 us -> 21.7 us  [along_occ(): return lax.ppermute(x, ALL, pairs)]
    pallas_call x0 -> x5, Pallas kernels: none -> 4.97 us  [kernel(): pl.pallas_call(run, out_shape=[jax.ShapeDtypeStruct(s, jnp.float32) for s...]
    dot_general x2 -> x0, matrix products: 3.91 us -> none  [the longest x1 2.44 us: local(): jnp.einsum('qa,qn->an', chip, right, precision=PRECISION, preferred_eleme...]
    unnamed x6 -> x12, local copies, waits for them, and re-layouts: 0.96 us -> 4.71 us
  transfers between devices with their start and end apart: 5 -> 10, of which waited for: 5 -> 6; matrix products, arithmetic and copies ran while one was open for 1% -> 1% of each run, Pallas kernels for 0% -> 2%
where the time goes in v3:
time: 169 us; the launch traced here: 168 us
  starting transfers between devices  98.9 us (59%)
  waiting for transfers between devices  55.3 us (33%)
  local copies, waits for them, and re-layouts  6.56 us (4%)
  Pallas kernels  4.97 us (3%)
    all_to_all x3, starting transfers between devices, shared(): return lax.all_to_all(x, 'z', 0, 0, tiled=True)  58.8 us
    all_to_all x3, waiting for transfers between devices, shared(): return lax.all_to_all(x, 'z', 0, 0, tiled=True)  32.5 us
    ppermute x4, starting transfers between devices, along_occ(): return lax.ppermute(x, ALL, pairs)  21.7 us
    ppermute x4, waiting for transfers between devices, along_occ(): return lax.ppermute(x, ALL, pairs)  21 us
    ppermute x3, starting transfers between devices, core_swap(): return lax.ppermute(x, 'core', [(0, 1), (1, 0)])  18.4 us
    pallas_call x5, Pallas kernels, kernel(): pl.pallas_call(run, out_shape=[jax.ShapeDtypeStruct(s, jnp.float32) for s...  4.97 us
    unnamed x12, local copies, waits for them, and re-layouts  4.71 us
  transfers between devices with their start and end apart: 10, of which 6 were waited for; matrix products, arithmetic and copies ran while one was open for 1% of the time, Pallas kernels for 2%

profile of v3, /device:TPU:1, one launch (start us, length us, event | category | flops | bytes accessed | tf_op | source)
XLA Modules:
  0.0 168.3 jit_solution(7198378961962585811)
XLA Ops:
  0.0 12.4 %collective-permute-start.2 = (f32[384,512]{1,0:T(8,128)}, f32[384,512]{1,0:T(8,128)S(1)}, u32[]{:S(2)}, u32[]{:S(2)}) collective-permute-start(f32[384,512]{1,0:T(8,128)} %bitcast.12), channel_id=1, source_target_pairs={{0,1},{1,0},{2,3},{3,2},{4,5},{5,4},{6,7},{7,6},{8,9},{9,8},{10,11... | collective-permute-start | bytes 2359304 | tf_op jit(solution)/shard_map/ppermute | solution.py:27
  13.1 1.2 dynamic-slice_bitcast_fusion
  14.3 2.1 %collective-permute-start.3 = (f32[392,256]{1,0:T(8,128)S(1)}, f32[392,256]{1,0:T(8,128)S(1)}, u32[]{:S(2)}, u32[]{:S(2)}) collective-permute-start(f32[392,256]{1,0:T(8,128)S(1)} %concatenate.3), channel_id=1, source_target_pairs={{0,8},{1,9},{2,10},{3,11},{4,12},{5,13},{6,14},{7,15},{8,16},{9,17... | collective-permute-start | bytes 1204232 | tf_op jit(solution)/shard_map/ppermute | solution.py:23
  16.4 8.1 %collective-permute-start.4 = (f32[384,256]{1,0:T(8,128)S(1)}, f32[384,256]{1,0:T(8,128)S(1)}, u32[]{:S(2)}, u32[]{:S(2)}) collective-permute-start(f32[384,256]{1,0:T(8,128)S(1)} %get-tuple-element.17), channel_id=1, source_target_pairs={{0,9},{1,8},{2,11},{3,10},{4,13},{5,12},{6,15},{7,14},{8,17},{9,16... | collective-permute-start | bytes 1179656 | tf_op jit(solution)/shard_map/ppermute | solution.py:23
  24.5 5.3 %collective-permute-start = (f32[384,512]{1,0:T(8,128)S(1)}, f32[384,512]{1,0:T(8,128)S(1)}, u32[]{:S(2)}, u32[]{:S(2)}) collective-permute-start(f32[384,512]{1,0:T(8,128)S(1)} %bitcast.13), channel_id=1, source_target_pairs={{0,760},{1,761},{2,762},{3,763},{4,764},{5,765},{6,766},{7,767},{8... | collective-permute-start | bytes 2359304 | tf_op jit(solution)/shard_map/ppermute | solution.py:23
  29.8 17.4 %collective-permute-done.4.refs_3_.refs_1_ = f32[384,256]{1,0:T(8,128)S(1)} collective-permute-done((f32[384,256]{1,0:T(8,128)S(1)}, f32[384,256]{1,0:T(8,128)S(1)}, u32[]{:S(2)}, u32[]{:S(2)}) %collective-permute-start.4) | collective-permute-done | bytes 393248 | tf_op jit(solution)/shard_map/ppermute | solution.py:23
  47.2 1.6 shard_map.40
  48.9 51.2 %all-to-all-start = ((f32[4,128,256]{2,1,0:T(8,128)}), f32[4,128,256]{2,1,0:T(8,128)S(1)}, u32[]{:S(2)}, u32[]{:S(2)}) async-start(f32[4,128,256]{2,1,0:T(8,128)} %shard_map.40), calls=%async_computation | async-start | bytes 1048576 | tf_op jit(solution)/shard_map/all_to_all | solution.py:113
  100.0 2.6 %collective-permute-start.1 = (f32[384,512]{1,0:T(8,128)S(1)}, f32[384,512]{1,0:T(8,128)S(1)}, u32[]{:S(2)}, u32[]{:S(2)}) collective-permute-start(f32[384,512]{1,0:T(8,128)S(1)} %collective-permute-done.refs_1_), channel_id=1, source_target_pairs={{0,1},{1,0},{2,3},{3,2},{4,5},{5,4},{6,7},{7,6},{8,9},{9,8},{10,11... | collective-permute-start | bytes 2359304 | tf_op jit(solution)/shard_map/ppermute | solution.py:27
  104.8 9.3 %all-to-all-done.refs_0_ = f32[4,128,256]{2,1,0:T(8,128)S(1)} async-done(((f32[4,128,256]{2,1,0:T(8,128)}), f32[4,128,256]{2,1,0:T(8,128)S(1)}, u32[]{:S(2)}, u32[]{:S(2)}) %all-to-all-start) | async-done | bytes 524320 | tf_op jit(solution)/shard_map/all_to_all | solution.py:113
  114.1 0.8 shard_map.41
  114.9 3.5 %all-to-all-start.2 = ((f32[4,128,256]{2,1,0:T(8,128)}), f32[4,128,256]{2,1,0:T(8,128)S(1)}, u32[]{:S(2)}, u32[]{:S(2)}) async-start(f32[4,128,256]{2,1,0:T(8,128)} %get-tuple-element.12), calls=%async_computation.2 | async-start | bytes 1048576 | tf_op jit(solution)/shard_map/all_to_all | solution.py:113
  118.4 6.2 %collective-permute-start.5 = (f32[128,256]{1,0:T(8,128)S(1)}, f32[128,256]{1,0:T(8,128)S(1)}, u32[]{:S(2)}, u32[]{:S(2)}) collective-permute-start(f32[128,256]{1,0:T(8,128)S(1)} %get-tuple-element.11), channel_id=1, source_target_pairs={{0,760},{1,761},{2,762},{3,763},{4,764},{5,765},{6,766},{7,767},{8... | collective-permute-start | bytes 393224 | tf_op jit(solution)/shard_map/ppermute | solution.py:23
  124.6 3.5 %collective-permute-done.5.refs_0_ = f32[128,256]{1,0:T(8,128)S(1)} collective-permute-done((f32[128,256]{1,0:T(8,128)S(1)}, f32[128,256]{1,0:T(8,128)S(1)}, u32[]{:S(2)}, u32[]{:S(2)}) %collective-permute-start.5) | collective-permute-done | bytes 131104 | tf_op jit(solution)/shard_map/ppermute | solution.py:23
  129.0 11.8 %all-to-all-done.2.refs_2_ = f32[4,128,256]{2,1,0:T(8,128)S(1)} async-done(((f32[4,128,256]{2,1,0:T(8,128)}), f32[4,128,256]{2,1,0:T(8,128)S(1)}, u32[]{:S(2)}, u32[]{:S(2)}) %all-to-all-start.2) | async-done | bytes 524320 | tf_op jit(solution)/shard_map/all_to_all | solution.py:113
  140.8 4.2 %all-to-all-start.1 = ((f32[4,128,256]{2,1,0:T(8,128)}), f32[4,128,256]{2,1,0:T(8,128)S(1)}, u32[]{:S(2)}, u32[]{:S(2)}) async-start(f32[4,128,256]{2,1,0:T(8,128)} %shard_map.42), calls=%async_computation.1 | async-start | bytes 1048576 | tf_op jit(solution)/shard_map/all_to_all | solution.py:113
  145.8 0.9 copy-done.1
  146.7 0.9 copy-done.3
  147.6 11.4 %all-to-all-done.1.refs_3_ = f32[4,128,256]{2,1,0:T(8,128)S(1)} async-done(((f32[4,128,256]{2,1,0:T(8,128)}), f32[4,128,256]{2,1,0:T(8,128)S(1)}, u32[]{:S(2)}, u32[]{:S(2)}) %all-to-all-start.1) | async-done | bytes 524320 | tf_op jit(solution)/shard_map/all_to_all | solution.py:113
  159.0 1.1 copy-done.2
  160.1 1.1 copy-done.4
  162.1 3.4 %collective-permute-start.6 = (f32[384,512]{1,0:T(8,128)S(1)}, f32[384,512]{1,0:T(8,128)S(1)}, u32[]{:S(2)}, u32[]{:S(2)}) collective-permute-start(f32[384,512]{1,0:T(8,128)S(1)} %get-tuple-element.16), channel_id=1, source_target_pairs={{0,1},{1,0},{2,3},{3,2},{4,5},{5,4},{6,7},{7,6},{8,9},{9,8},{10,11... | collective-permute-start | bytes 2359304 | tf_op jit(solution)/shard_map/ppermute | solution.py:27
  165.4 1.9 %collective-permute-done.6 = f32[384,512]{1,0:T(8,128)S(1)} collective-permute-done((f32[384,512]{1,0:T(8,128)S(1)}, f32[384,512]{1,0:T(8,128)S(1)}, u32[]{:S(2)}, u32[]{:S(2)}) %collective-permute-start.6) | collective-permute-done | bytes 786464 | tf_op jit(solution)/shard_map/ppermute | solution.py:27
  167.3 1.0 add_bitcast_fusion
  (20 shorter events, 4.0 us)
Async XLA Ops:
  0.0 47.2 %collective-permute-start.2 = (f32[384,512]{1,0:T(8,128)}, f32[384,512]{1,0:T(8,128)S(1)}, u32[]{:S(2)}, u32[]{:S(2)}) collective-permute-start(f32[384,512]{1,0:T(8,128)} %bitcast.12), channel_id=1, source_target_pairs={{0,1},{1,0},{2,3},{3,2},{4,5},{5,4},{6,7},{7,6},{8,9},{9,8},{10,11... | collective-permute-start | bytes 2359304 | tf_op jit(solution)/shard_map/ppermute | solution.py:27
  14.2 10.2 %copy-start = (f32[1,384,512]{2,1,0:T(8,128)S(1)}, f32[1,384,512]{2,1,0:T(8,128)}, u32[]{:S(2)}) copy-start(f32[1,384,512]{2,1,0:T(8,128)} %param.3) | copy-start | bytes 2359300
  14.3 32.9 %collective-permute-start.3 = (f32[392,256]{1,0:T(8,128)S(1)}, f32[392,256]{1,0:T(8,128)S(1)}, u32[]{:S(2)}, u32[]{:S(2)}) collective-permute-start(f32[392,256]{1,0:T(8,128)S(1)} %concatenate.3), channel_id=1, source_target_pairs={{0,8},{1,9},{2,10},{3,11},{4,12},{5,13},{6,14},{7,15},{8,16},{9,17... | collective-permute-start | bytes 1204232 | tf_op jit(solution)/shard_map/ppermute | solution.py:23
  16.4 30.8 %collective-permute-start.4 = (f32[384,256]{1,0:T(8,128)S(1)}, f32[384,256]{1,0:T(8,128)S(1)}, u32[]{:S(2)}, u32[]{:S(2)}) collective-permute-start(f32[384,256]{1,0:T(8,128)S(1)} %get-tuple-element.17), channel_id=1, source_target_pairs={{0,9},{1,8},{2,11},{3,10},{4,13},{5,12},{6,15},{7,14},{8,17},{9,16... | collective-permute-start | bytes 1179656 | tf_op jit(solution)/shard_map/ppermute | solution.py:23
  24.5 75.6 %collective-permute-start = (f32[384,512]{1,0:T(8,128)S(1)}, f32[384,512]{1,0:T(8,128)S(1)}, u32[]{:S(2)}, u32[]{:S(2)}) collective-permute-start(f32[384,512]{1,0:T(8,128)S(1)} %bitcast.13), channel_id=1, source_target_pairs={{0,760},{1,761},{2,762},{3,763},{4,764},{5,765},{6,766},{7,767},{8... | collective-permute-start | bytes 2359304 | tf_op jit(solution)/shard_map/ppermute | solution.py:23
  48.9 65.2 %all-to-all-start = ((f32[4,128,256]{2,1,0:T(8,128)}), f32[4,128,256]{2,1,0:T(8,128)S(1)}, u32[]{:S(2)}, u32[]{:S(2)}) async-start(f32[4,128,256]{2,1,0:T(8,128)} %shard_map.40), calls=%async_computation | async-start | bytes 1048576 | tf_op jit(solution)/shard_map/all_to_all | solution.py:113
  100.0 4.7 %collective-permute-start.1 = (f32[384,512]{1,0:T(8,128)S(1)}, f32[384,512]{1,0:T(8,128)S(1)}, u32[]{:S(2)}, u32[]{:S(2)}) collective-permute-start(f32[384,512]{1,0:T(8,128)S(1)} %collective-permute-done.refs_1_), channel_id=1, source_target_pairs={{0,1},{1,0},{2,3},{3,2},{4,5},{5,4},{6,7},{7,6},{8,9},{9,8},{10,11... | collective-permute-start | bytes 2359304 | tf_op jit(solution)/shard_map/ppermute | solution.py:27
  102.6 0.7 copy-start.5
  114.9 25.9 %all-to-all-start.2 = ((f32[4,128,256]{2,1,0:T(8,128)}), f32[4,128,256]{2,1,0:T(8,128)S(1)}, u32[]{:S(2)}, u32[]{:S(2)}) async-start(f32[4,128,256]{2,1,0:T(8,128)} %get-tuple-element.12), calls=%async_computation.2 | async-start | bytes 1048576 | tf_op jit(solution)/shard_map/all_to_all | solution.py:113
  118.4 9.7 %collective-permute-start.5 = (f32[128,256]{1,0:T(8,128)S(1)}, f32[128,256]{1,0:T(8,128)S(1)}, u32[]{:S(2)}, u32[]{:S(2)}) collective-permute-start(f32[128,256]{1,0:T(8,128)S(1)} %get-tuple-element.11), channel_id=1, source_target_pairs={{0,760},{1,761},{2,762},{3,763},{4,764},{5,765},{6,766},{7,767},{8... | collective-permute-start | bytes 393224 | tf_op jit(solution)/shard_map/ppermute | solution.py:23
  140.8 18.2 %all-to-all-start.1 = ((f32[4,128,256]{2,1,0:T(8,128)}), f32[4,128,256]{2,1,0:T(8,128)S(1)}, u32[]{:S(2)}, u32[]{:S(2)}) async-start(f32[4,128,256]{2,1,0:T(8,128)} %shard_map.42), calls=%async_computation.1 | async-start | bytes 1048576 | tf_op jit(solution)/shard_map/all_to_all | solution.py:113
  145.8 0.9 copy-start.1
  146.7 0.9 copy-start.3
  159.0 1.1 copy-start.2
  160.1 1.1 copy-start.4
  162.1 5.3 %collective-permute-start.6 = (f32[384,512]{1,0:T(8,128)S(1)}, f32[384,512]{1,0:T(8,128)S(1)}, u32[]{:S(2)}, u32[]{:S(2)}) collective-permute-start(f32[384,512]{1,0:T(8,128)S(1)} %get-tuple-element.16), channel_id=1, source_target_pairs={{0,1},{1,0},{2,3},{3,2},{4,5},{5,4},{6,7},{7,6},{8,9},{9,8},{10,11... | collective-permute-start | bytes 2359304 | tf_op jit(solution)/shard_map/ppermute | solution.py:27

commit v4 on v3

v4 whole, which is shorter than its diff:
```python
import jax
import jax.numpy as jnp
from jax import lax
from jax.experimental import pallas as pl
from jax.experimental.pallas import tpu as pltpu
from jax.sharding import Mesh, PartitionSpec as P

CHIPS = 4
ALL = ("occ", "z", "core")
SMEM = pl.BlockSpec(memory_space=pltpu.SMEM)
VMEM = pl.BlockSpec(memory_space=pltpu.VMEM)
ANY = pl.BlockSpec(memory_space=pl.ANY)


def along_occ(x, by, cross=0):
    n = lax.axis_size("occ")
    pairs = [
        ((i * CHIPS + z) * 2 + h, ((i + by) % n * CHIPS + z) * 2 + (h ^ cross))
        for i in range(n)
        for z in range(CHIPS)
        for h in range(2)
    ]
    return lax.ppermute(x, ALL, pairs)


def core_swap(x):
    return lax.ppermute(x, "core", [(0, 1), (1, 0)])


def kernel(body, shapes, scalars, arrays, after=(), flops=0):
    used = len(scalars) + len(arrays)

    def run(*refs):
        body(*refs[:used], *refs[used + len(after) :])

    return pl.pallas_call(
        run,
        out_shape=[jax.ShapeDtypeStruct(s, jnp.float32) for s in shapes],
        in_specs=[SMEM] * len(scalars) + [VMEM] * len(arrays) + [ANY] * len(after),
        out_specs=[VMEM] * len(shapes),
        cost_estimate=pl.CostEstimate(flops=flops, bytes_accessed=0, transcendentals=0),
        compiler_params=pltpu.CompilerParams(vmem_limit_bytes=24 * 2**20),
    )(*[s.reshape(1) for s in scalars], *arrays, *after)


def split(x):
    high = x.astype(jnp.bfloat16)
    return high, (x - high.astype(jnp.float32)).astype(jnp.bfloat16)


def dot(x, y, dims):
    def one(u, v):
        return lax.dot_general(u, v, (dims, ((), ())), preferred_element_type=jnp.float32)

    return one(x[0], y[0]) + (one(x[0], y[1]) + one(x[1], y[0]))


ROWS = ((0,), (0,))
LAST = ((1,), (1,))
PLAIN = ((1,), (0,))


def block(start_ref, width):
    return pl.ds(pl.multiple_of(start_ref[0], width), width)


def pair_tiles(here_ref, there_ref, own_ref, other_ref, low_ref, low_far_ref, up_ref, up_far_ref, out_ref):
    rows, width = low_far_ref.shape
    here, there = block(here_ref, width), block(there_ref, width)
    chip_here = split(jnp.concatenate([own_ref[:, here], other_ref[:, here]]))
    chip_there = split(jnp.concatenate([own_ref[:, there], other_ref[:, there]]))
    lower = split(jnp.concatenate([low_ref[:rows], low_far_ref[...]]))
    upper = split(jnp.concatenate([up_ref[:rows], up_far_ref[...]]))
    part = (CHIPS, width // CHIPS, width)
    out_ref[:, :, :width] = dot(chip_there, lower, ROWS).reshape(part)
    out_ref[:, :, width:] = dot(upper, chip_here, ROWS).reshape(part)


def divide(parts_ref, denominator_ref, low_ref, up_ref):
    total = (parts_ref[0] + parts_ref[1]) + (parts_ref[2] + parts_ref[3])
    amplitude = total / denominator_ref[...]
    width = low_ref.shape[1]
    low_ref[...] = amplitude[:, :width]
    up_ref[...] = amplitude[:, width:]


def lay_out(*refs):
    out_ref = refs[-1]
    width = refs[0].shape[1]
    for n, ref in enumerate(refs[:-1]):
        for k in range(CHIPS):
            out_ref[k, :, n * width : (n + 1) * width] = ref[...]


def density_part(here_ref, there_ref, low_ref, low_far_ref, up_ref, up_far_ref, amps_ref, mine_ref, others_ref):
    rows, width = low_far_ref.shape
    lower = split(jnp.concatenate([low_ref[:rows], low_far_ref[...]]))
    upper = split(jnp.concatenate([up_ref[:rows], up_far_ref[...]]))
    amps = amps_ref[...].reshape(width, 4 * width)
    low_there, up_here, low_here, up_there = (split(amps[:, n * width : (n + 1) * width]) for n in range(4))
    for start_ref, low_amp, up_amp in ((here_ref, low_here, up_here), (there_ref, low_there, up_there)):
        product = dot(lower, low_amp, LAST) + dot(upper, up_amp, PLAIN)
        columns = block(start_ref, width)
        mine_ref[:, columns] = product[:rows]
        others_ref[:, columns] = product[rows:]


def local(factors, occ_energy, virt_energy):
    own = factors[0]
    rows, virt = own.shape
    half = virt // 2
    part = half // CHIPS
    core = lax.axis_index("core")
    z = lax.axis_index("z")
    here = core * half
    there = half - here

    def columns(start):
        return lax.dynamic_slice_in_dim(own, start, half, 1)

    def energies(start, length):
        return lax.dynamic_slice_in_dim(virt_energy, start, length, 0)

    def shared(x):
        return lax.all_to_all(x, "z", 0, 0, tiled=True)

    near = jnp.concatenate([columns(here), jnp.broadcast_to(occ_energy, (8, half))])
    far = columns(there)
    low, up = along_occ(near, 1), along_occ(near, -1)
    low_far, up_far = along_occ(far, 1, cross=1), along_occ(far, -1, cross=1)
    other = core_swap(own)

    def denominator(rows_start, neighbour):
        row_energy = energies(rows_start + z * part, part) - (occ_energy + neighbour[rows, 0])
        return row_energy[:, None] + energies(here, half)[None, :]

    tiles = kernel(
        pair_tiles, [(CHIPS, part, virt)], [here, there], [own, other, low, low_far, up, up_far]
    )[0]
    denominators = jnp.concatenate([denominator(there, low), denominator(here, up)], 1)
    low_tile, up_tile = kernel(divide, [(part, half)] * 2, [], [shared(tiles), denominators])
    low_rest, up_rest = along_occ(up_tile, 1), along_occ(low_tile, -1, cross=1)
    whole = kernel(lay_out, [(CHIPS, part, 2 * virt)], [], [low_tile, up_tile, low_rest, up_rest])[0]
    mine, others = kernel(
        density_part, [(rows, virt)] * 2, [here, there], [low, low_far, up, up_far, shared(whole)]
    )
    return (mine + core_swap(others))[None]


def solution(mesh):
    cube = Mesh(mesh.devices.reshape(mesh.devices.shape[0], CHIPS, 2), ALL)
    spec = P("occ", ("z", "core"), None)
    return jax.shard_map(local, mesh=cube, in_specs=(spec, P("occ"), P()), out_specs=spec, check_vma=False)
```

time: 169 us -> 181 us (1.071)
  starting transfers between devices: 98.9 us -> 56.2 us
  blocking collectives: 0 us -> 31.8 us
  waiting for transfers between devices: 55.3 us -> 83.5 us
  local copies, waits for them, and re-layouts: 6.56 us -> 3 us
    all_to_all x3 -> x1, starting transfers between devices: 58.8 us -> 4.29 us  [shared(): return lax.all_to_all(x, 'z', 0, 0, tiled=True)]
    ppermute x4 -> x6, waiting for transfers between devices: 21 us -> 70.5 us  [along_occ(): return lax.ppermute(x, ALL, pairs)]
    all_to_all x0 -> x1, blocking collectives: none -> 31.8 us  [shared(): return lax.all_to_all(x, 'z', 0, 0, tiled=True)]
    all_to_all x3 -> x1, waiting for transfers between devices: 32.5 us -> 11.1 us  [shared(): return lax.all_to_all(x, 'z', 0, 0, tiled=True)]
    ppermute x4 -> x6, starting transfers between devices: 21.7 us -> 35.7 us  [along_occ(): return lax.ppermute(x, ALL, pairs)]
    unnamed x12 -> x4, local copies, waits for them, and re-layouts: 4.71 us -> 0.69 us
    ppermute x3 -> x2, starting transfers between devices: 18.4 us -> 16.2 us  [core_swap(): return lax.ppermute(x, 'core', [(0, 1), (1, 0)])]
    pallas_call x5 -> x4, Pallas kernels: 4.97 us -> 3.28 us  [kernel(): pl.pallas_call(run, out_shape=[jax.ShapeDtypeStruct(s, jnp.float32) for s...]
  transfers between devices with their start and end apart: 10 -> 9, of which waited for: 6 -> 6; matrix products, arithmetic and copies ran while one was open for 1% -> 1% of each run, Pallas kernels for 2% -> 0%
where the time goes in v4:
time: 181 us
  waiting for transfers between devices  83.5 us (46%)
  starting transfers between devices  56.2 us (31%)
  blocking collectives  31.8 us (18%)
  Pallas kernels  3.28 us (2%)
  local copies, waits for them, and re-layouts  3 us (2%)
  between operations  1.99 us (1%)
    ppermute x6, waiting for transfers between devices, along_occ(): return lax.ppermute(x, ALL, pairs)  70.5 us
    ppermute x6, starting transfers between devices, along_occ(): return lax.ppermute(x, ALL, pairs)  35.7 us
    all_to_all x1, blocking collectives, shared(): return lax.all_to_all(x, 'z', 0, 0, tiled=True)  31.8 us
    ppermute x2, starting transfers between devices, core_swap(): return lax.ppermute(x, 'core', [(0, 1), (1, 0)])  16.2 us
    all_to_all x1, waiting for transfers between devices, shared(): return lax.all_to_all(x, 'z', 0, 0, tiled=True)  11.1 us
    all_to_all x1, starting transfers between devices, shared(): return lax.all_to_all(x, 'z', 0, 0, tiled=True)  4.29 us
  transfers between devices with their start and end apart: 9, of which 6 were waited for; matrix products, arithmetic and copies ran while one was open for 1% of the time, Pallas kernels for 0%

profile of v4, /device:TPU:1, one launch (start us, length us, event | category | flops | bytes accessed | tf_op | source)
XLA Modules:
  0.0 180.9 jit_solution(7080913280424763983)
XLA Ops:
  0.0 12.4 %collective-permute-start.4 = (f32[384,512]{1,0:T(8,128)}, f32[384,512]{1,0:T(8,128)S(1)}, u32[]{:S(2)}, u32[]{:S(2)}) collective-permute-start(f32[384,512]{1,0:T(8,128)} %bitcast.15), channel_id=1, source_target_pairs={{0,1},{1,0},{2,3},{3,2},{4,5},{5,4},{6,7},{7,6},{8,9},{9,8},{10,11... | collective-permute-start | bytes 2359304 | tf_op jit(solution)/shard_map/ppermute | solution.py:27
  13.1 1.2 dynamic-slice_bitcast_fusion
  14.3 10.5 %collective-permute-start.2 = (f32[392,256]{1,0:T(8,128)S(1)}, f32[392,256]{1,0:T(8,128)S(1)}, u32[]{:S(2)}, u32[]{:S(2)}) collective-permute-start(f32[392,256]{1,0:T(8,128)S(1)} %concatenate.6), channel_id=1, source_target_pairs={{0,760},{1,761},{2,762},{3,763},{4,764},{5,765},{6,766},{7,767},{8... | collective-permute-start | bytes 1204232 | tf_op jit(solution)/shard_map/ppermute | solution.py:23
  24.8 1.9 %collective-permute-start = (f32[392,256]{1,0:T(8,128)S(1)}, f32[392,256]{1,0:T(8,128)S(1)}, u32[]{:S(2)}, u32[]{:S(2)}) collective-permute-start(f32[392,256]{1,0:T(8,128)S(1)} %concatenate.6), channel_id=1, source_target_pairs={{0,8},{1,9},{2,10},{3,11},{4,12},{5,13},{6,14},{7,15},{8,16},{9,17... | collective-permute-start | bytes 1204232 | tf_op jit(solution)/shard_map/ppermute | solution.py:23
  26.7 11.9 %collective-permute-start.3 = (f32[384,256]{1,0:T(8,128)S(1)}, f32[384,256]{1,0:T(8,128)S(1)}, u32[]{:S(2)}, u32[]{:S(2)}) collective-permute-start(f32[384,256]{1,0:T(8,128)S(1)} %get-tuple-element.13), channel_id=1, source_target_pairs={{0,761},{1,760},{2,763},{3,762},{4,765},{5,764},{6,767},{7,766},{8... | collective-permute-start | bytes 1179656 | tf_op jit(solution)/shard_map/ppermute | solution.py:23
  38.7 1.9 %collective-permute-start.1 = (f32[384,256]{1,0:T(8,128)S(1)}, f32[384,256]{1,0:T(8,128)S(1)}, u32[]{:S(2)}, u32[]{:S(2)}) collective-permute-start(f32[384,256]{1,0:T(8,128)S(1)} %get-tuple-element.13), channel_id=1, source_target_pairs={{0,9},{1,8},{2,11},{3,10},{4,13},{5,12},{6,15},{7,14},{8,17},{9,16... | collective-permute-start | bytes 1179656 | tf_op jit(solution)/shard_map/ppermute | solution.py:23
  40.6 46.8 %collective-permute-done.3.refs_7_.refs_5_ = f32[384,256]{1,0:T(8,128)S(1)} collective-permute-done((f32[384,256]{1,0:T(8,128)S(1)}, f32[384,256]{1,0:T(8,128)S(1)}, u32[]{:S(2)}, u32[]{:S(2)}) %collective-permute-start.3) | collective-permute-done | bytes 393248 | tf_op jit(solution)/shard_map/ppermute | solution.py:23
  87.4 18.0 %collective-permute-done.1.refs_5_.refs_3_ = f32[384,256]{1,0:T(8,128)S(1)} collective-permute-done((f32[384,256]{1,0:T(8,128)S(1)}, f32[384,256]{1,0:T(8,128)S(1)}, u32[]{:S(2)}, u32[]{:S(2)}) %collective-permute-start.1) | collective-permute-done | bytes 393248 | tf_op jit(solution)/shard_map/ppermute | solution.py:23
  105.4 1.7 shard_map.40
  107.1 4.3 %all-to-all-start = ((f32[4,64,512]{2,1,0:T(8,128)}), f32[4,64,512]{2,1,0:T(8,128)S(1)}, u32[]{:S(2)}, u32[]{:S(2)}) async-start(f32[4,64,512]{2,1,0:T(8,128)} %shard_map.40), calls=%async_computation | async-start | bytes 1048576 | tf_op jit(solution)/shard_map/all_to_all | solution.py:125
  111.4 0.7 copy-done.1
  112.2 0.5 slice.9
  113.3 0.5 slice.8
  114.4 0.1 dynamic-slice_subtract_fusion.1
  114.6 11.1 %all-to-all-done.refs_0_ = f32[4,64,512]{2,1,0:T(8,128)S(1)} async-done(((f32[4,64,512]{2,1,0:T(8,128)}), f32[4,64,512]{2,1,0:T(8,128)S(1)}, u32[]{:S(2)}, u32[]{:S(2)}) %all-to-all-start) | async-done | bytes 524320 | tf_op jit(solution)/shard_map/all_to_all | solution.py:125
  125.8 1.9 %collective-permute-start.6 = (f32[64,256]{1,0:T(8,128)S(1)}, f32[64,256]{1,0:T(8,128)S(1)}, u32[]{:S(2)}, u32[]{:S(2)}) collective-permute-start(f32[64,256]{1,0:T(8,128)S(1)} %get-tuple-element.9.refs_0_), channel_id=1, source_target_pairs={{0,761},{1,760},{2,763},{3,762},{4,765},{5,764},{6,767},{7,766},{8... | collective-permute-start | bytes 196616 | tf_op jit(solution)/shard_map/ppermute | solution.py:23
  127.7 7.5 %collective-permute-start.5 = (f32[64,256]{1,0:T(8,128)S(1)}, f32[64,256]{1,0:T(8,128)S(1)}, u32[]{:S(2)}, u32[]{:S(2)}) collective-permute-start(f32[64,256]{1,0:T(8,128)S(1)} %get-tuple-element.10.refs_1_), channel_id=1, source_target_pairs={{0,8},{1,9},{2,10},{3,11},{4,12},{5,13},{6,14},{7,15},{8,16},{9,17... | collective-permute-start | bytes 196616 | tf_op jit(solution)/shard_map/ppermute | solution.py:23
  135.2 3.4 %collective-permute-done.6.refs_3_ = f32[64,256]{1,0:T(8,128)S(1)} collective-permute-done((f32[64,256]{1,0:T(8,128)S(1)}, f32[64,256]{1,0:T(8,128)S(1)}, u32[]{:S(2)}, u32[]{:S(2)}) %collective-permute-start.6) | collective-permute-done | bytes 65568 | tf_op jit(solution)/shard_map/ppermute | solution.py:23
  138.6 2.3 %collective-permute-done.5.refs_2_ = f32[64,256]{1,0:T(8,128)S(1)} collective-permute-done((f32[64,256]{1,0:T(8,128)S(1)}, f32[64,256]{1,0:T(8,128)S(1)}, u32[]{:S(2)}, u32[]{:S(2)}) %collective-permute-start.5) | collective-permute-done | bytes 65568 | tf_op jit(solution)/shard_map/ppermute | solution.py:23
  141.0 31.8 %all_to_all.10.refs_6_ = f32[4,64,1024]{2,1,0:T(8,128)S(1)} all-to-all(f32[4,64,1024]{2,1,0:T(8,128)S(1)} %shard_map.42), channel_id=1, replica_groups=mesh['occ'=96,'z'=4,'core'=2] {'z'}, dimensions={0} | all-to-all | bytes 2097152 | tf_op jit(solution)/shard_map/all_to_all | solution.py:125
  172.8 1.5 shard_map.43
  174.2 3.8 %collective-permute-start.7 = (f32[384,512]{1,0:T(8,128)S(1)}, f32[384,512]{1,0:T(8,128)S(1)}, u32[]{:S(2)}, u32[]{:S(2)}) collective-permute-start(f32[384,512]{1,0:T(8,128)S(1)} %get-tuple-element.12), channel_id=1, source_target_pairs={{0,1},{1,0},{2,3},{3,2},{4,5},{5,4},{6,7},{7,6},{8,9},{9,8},{10,11... | collective-permute-start | bytes 2359304 | tf_op jit(solution)/shard_map/ppermute | solution.py:27
  178.0 1.9 %collective-permute-done.7 = f32[384,512]{1,0:T(8,128)S(1)} collective-permute-done((f32[384,512]{1,0:T(8,128)S(1)}, f32[384,512]{1,0:T(8,128)S(1)}, u32[]{:S(2)}, u32[]{:S(2)}) %collective-permute-start.7) | collective-permute-done | bytes 786464 | tf_op jit(solution)/shard_map/ppermute | solution.py:27
  179.9 1.0 add_bitcast_fusion
  (12 shorter events, 0.3 us)
Async XLA Ops:
  0.0 105.4 %collective-permute-start.4 = (f32[384,512]{1,0:T(8,128)}, f32[384,512]{1,0:T(8,128)S(1)}, u32[]{:S(2)}, u32[]{:S(2)}) collective-permute-start(f32[384,512]{1,0:T(8,128)} %bitcast.15), channel_id=1, source_target_pairs={{0,1},{1,0},{2,3},{3,2},{4,5},{5,4},{6,7},{7,6},{8,9},{9,8},{10,11... | collective-permute-start | bytes 2359304 | tf_op jit(solution)/shard_map/ppermute | solution.py:27
  14.3 91.2 %copy-start = (f32[1,384,512]{2,1,0:T(8,128)S(1)}, f32[1,384,512]{2,1,0:T(8,128)}, u32[]{:S(2)}) copy-start(f32[1,384,512]{2,1,0:T(8,128)} %param.3) | copy-start | bytes 2359300
  14.3 91.1 %collective-permute-start.2 = (f32[392,256]{1,0:T(8,128)S(1)}, f32[392,256]{1,0:T(8,128)S(1)}, u32[]{:S(2)}, u32[]{:S(2)}) collective-permute-start(f32[392,256]{1,0:T(8,128)S(1)} %concatenate.6), channel_id=1, source_target_pairs={{0,760},{1,761},{2,762},{3,763},{4,764},{5,765},{6,766},{7,767},{8... | collective-permute-start | bytes 1204232 | tf_op jit(solution)/shard_map/ppermute | solution.py:23
  24.8 80.6 %collective-permute-start = (f32[392,256]{1,0:T(8,128)S(1)}, f32[392,256]{1,0:T(8,128)S(1)}, u32[]{:S(2)}, u32[]{:S(2)}) collective-permute-start(f32[392,256]{1,0:T(8,128)S(1)} %concatenate.6), channel_id=1, source_target_pairs={{0,8},{1,9},{2,10},{3,11},{4,12},{5,13},{6,14},{7,15},{8,16},{9,17... | collective-permute-start | bytes 1204232 | tf_op jit(solution)/shard_map/ppermute | solution.py:23
  26.7 60.7 %collective-permute-start.3 = (f32[384,256]{1,0:T(8,128)S(1)}, f32[384,256]{1,0:T(8,128)S(1)}, u32[]{:S(2)}, u32[]{:S(2)}) collective-permute-start(f32[384,256]{1,0:T(8,128)S(1)} %get-tuple-element.13), channel_id=1, source_target_pairs={{0,761},{1,760},{2,763},{3,762},{4,765},{5,764},{6,767},{7,766},{8... | collective-permute-start | bytes 1179656 | tf_op jit(solution)/shard_map/ppermute | solution.py:23
  38.7 66.7 %collective-permute-start.1 = (f32[384,256]{1,0:T(8,128)S(1)}, f32[384,256]{1,0:T(8,128)S(1)}, u32[]{:S(2)}, u32[]{:S(2)}) collective-permute-start(f32[384,256]{1,0:T(8,128)S(1)} %get-tuple-element.13), channel_id=1, source_target_pairs={{0,9},{1,8},{2,11},{3,10},{4,13},{5,12},{6,15},{7,14},{8,17},{9,16... | collective-permute-start | bytes 1179656 | tf_op jit(solution)/shard_map/ppermute | solution.py:23
  107.1 18.6 %all-to-all-start = ((f32[4,64,512]{2,1,0:T(8,128)}), f32[4,64,512]{2,1,0:T(8,128)S(1)}, u32[]{:S(2)}, u32[]{:S(2)}) async-start(f32[4,64,512]{2,1,0:T(8,128)} %shard_map.40), calls=%async_computation | async-start | bytes 1048576 | tf_op jit(solution)/shard_map/all_to_all | solution.py:125
  111.4 0.7 copy-start.1
  125.8 12.8 %collective-permute-start.6 = (f32[64,256]{1,0:T(8,128)S(1)}, f32[64,256]{1,0:T(8,128)S(1)}, u32[]{:S(2)}, u32[]{:S(2)}) collective-permute-start(f32[64,256]{1,0:T(8,128)S(1)} %get-tuple-element.9.refs_0_), channel_id=1, source_target_pairs={{0,761},{1,760},{2,763},{3,762},{4,765},{5,764},{6,767},{7,766},{8... | collective-permute-start | bytes 196616 | tf_op jit(solution)/shard_map/ppermute | solution.py:23
  127.7 13.2 %collective-permute-start.5 = (f32[64,256]{1,0:T(8,128)S(1)}, f32[64,256]{1,0:T(8,128)S(1)}, u32[]{:S(2)}, u32[]{:S(2)}) collective-permute-start(f32[64,256]{1,0:T(8,128)S(1)} %get-tuple-element.10.refs_1_), channel_id=1, source_target_pairs={{0,8},{1,9},{2,10},{3,11},{4,12},{5,13},{6,14},{7,15},{8,16},{9,17... | collective-permute-start | bytes 196616 | tf_op jit(solution)/shard_map/ppermute | solution.py:23
  174.2 5.7 %collective-permute-start.7 = (f32[384,512]{1,0:T(8,128)S(1)}, f32[384,512]{1,0:T(8,128)S(1)}, u32[]{:S(2)}, u32[]{:S(2)}) collective-permute-start(f32[384,512]{1,0:T(8,128)S(1)} %get-tuple-element.12), channel_id=1, source_target_pairs={{0,1},{1,0},{2,3},{3,2},{4,5},{5,4},{6,7},{7,6},{8,9},{9,8},{10,11... | collective-permute-start | bytes 2359304 | tf_op jit(solution)/shard_map/ppermute | solution.py:27

commit v5 on v2

v5 whole, which is shorter than its diff:
```python
import jax
import jax.numpy as jnp
from jax import lax
from jax.experimental import pallas as pl
from jax.experimental.pallas import tpu as pltpu
from jax.sharding import Mesh, PartitionSpec as P

CHIPS = 4
LEVELS = 3
RING = CHIPS * LEVELS
PLACES = ("occ", "z")
SMEM = pl.BlockSpec(memory_space=pltpu.SMEM)
VMEM = pl.BlockSpec(memory_space=pltpu.VMEM)


def meetings(occupied):
    columns = occupied // LEVELS
    above, below = [], []
    for place in range(occupied * CHIPS):
        column, height = divmod(place, RING)
        above.append(column * RING + (height + CHIPS // 2) % RING)
        shift = 1 if height < CHIPS else 0
        below.append((column - shift) % columns * RING + (height - CHIPS // 2) % RING)
    return above, below


def there(goals):
    return [(place, goal) for place, goal in enumerate(goals)]


def back(goals):
    return [(goal, place) for place, goal in enumerate(goals)]


def move(x, pairs):
    return lax.ppermute(x, PLACES, pairs)


def core_swap(x):
    return lax.ppermute(x, "core", [(0, 1), (1, 0)])


def kernel(body, shapes, scalars, arrays):
    return pl.pallas_call(
        body,
        out_shape=[jax.ShapeDtypeStruct(s, jnp.float32) for s in shapes],
        in_specs=[SMEM] * len(scalars) + [VMEM] * len(arrays),
        out_specs=[VMEM] * len(shapes),
        compiler_params=pltpu.CompilerParams(vmem_limit_bytes=24 * 2**20),
    )(*[s.reshape(1) for s in scalars], *arrays)


def split(x):
    high = x.astype(jnp.bfloat16)
    return high, (x - high.astype(jnp.float32)).astype(jnp.bfloat16)


def dot(x, y, dims):
    def one(u, v):
        return lax.dot_general(u, v, (dims, ((), ())), preferred_element_type=jnp.float32)

    return one(x[0], y[0]) + (one(x[0], y[1]) + one(x[1], y[0]))


def block(start_ref, width):
    return pl.ds(pl.multiple_of(start_ref[0], width), width)


def pair_tile(mine_ref, other_ref, lower_ref, upper_ref, keep_ref, give_ref):
    width = keep_ref.shape[1]
    rows = lower_ref.shape[0] - 8
    upper = split(upper_ref[:rows])
    for start_ref, out_ref in ((other_ref, give_ref), (mine_ref, keep_ref)):
        out_ref[...] = dot(upper, split(lower_ref[:rows, block(start_ref, width)]), ((0,), (0,)))


def add_tiles(keep_ref, got_ref, out_ref):
    out_ref[...] = (keep_ref[...] + got_ref[...]).reshape(out_ref.shape)


def divide(parts_ref, denominator_ref, out_ref):
    total = (parts_ref[0] + parts_ref[1]) + (parts_ref[2] + parts_ref[3])
    amplitude = total / denominator_ref[...]
    for k in range(CHIPS):
        out_ref[k] = amplitude


def density_parts(mine_ref, other_ref, lower_ref, upper_ref, amp_ref, swapped_ref, up_ref, down_ref):
    rows, virt = up_ref.shape
    width = amp_ref.shape[2]
    upper = split(upper_ref[:rows])
    total = None
    for start_ref, half_ref in ((mine_ref, amp_ref), (other_ref, swapped_ref)):
        columns = block(start_ref, width)
        amp = split(half_ref[...].reshape(virt, width))
        down_ref[:, columns] = dot(upper, amp, ((1,), (0,)))
        part = dot(split(lower_ref[:rows, columns]), amp, ((1,), (1,)))
        total = part if total is None else total + part
    up_ref[...] = total


def local(factors, occ_energy, virt_energy):
    own = factors[0]
    rows, virt = own.shape
    half, quarter = virt // 2, virt // CHIPS
    occupied = lax.axis_size("occ")
    above, below = meetings(occupied)
    groups = [
        [above[(level * CHIPS) + RING * column + c] for c in range(CHIPS)]
        for column in range(occupied // LEVELS)
        for level in range(LEVELS)
    ]
    mine = lax.axis_index("core") * half
    other = half - mine
    chip = lax.rem(lax.axis_index("z") + CHIPS // 2, CHIPS)

    def shared(x):
        return lax.all_to_all(x, PLACES, 0, 0, axis_index_groups=groups, tiled=True)

    parcel = jnp.concatenate([own, jnp.broadcast_to(occ_energy, (8, virt))])
    lower = move(parcel, there(above))
    upper = move(parcel, there(below))
    keep, give = kernel(pair_tile, [(virt, half)] * 2, [mine, other], [lower, upper])
    whole = (CHIPS, quarter, half)
    tile = kernel(add_tiles, [whole], [], [keep, core_swap(give)])[0]
    row_energy = lax.dynamic_slice_in_dim(virt_energy, chip * quarter, quarter, 0)
    column_energy = lax.dynamic_slice_in_dim(virt_energy, mine, half, 0)
    pair_energy = lower[rows, 0] + upper[rows, 0]
    denominator = (row_energy - pair_energy)[:, None] + column_energy[None, :]
    amp = shared(kernel(divide, [whole], [], [shared(tile), denominator])[0])
    up, down = kernel(density_parts, [(rows, virt)] * 2, [mine, other], [lower, upper, amp, core_swap(amp)])
    return (move(up, back(below)) + move(down, back(above)))[None]


def solution(mesh):
    cube = Mesh(mesh.devices.reshape(mesh.devices.shape[0], CHIPS, 2), (*PLACES, "core"))
    spec = P("occ", ("z", "core"), None)
    return jax.shard_map(local, mesh=cube, in_specs=(spec, P("occ"), P()), out_specs=spec, check_vma=False)
```

time: 174 us -> 155 us (0.89)
  waiting for transfers between devices: 103 us -> 83.5 us
  starting transfers between devices: 32.3 us -> 42.7 us
  blocking collectives: 27.3 us -> 18.3 us
  matrix products: 3.91 us -> 0 us
  Pallas kernels: 0 us -> 3.36 us
    ppermute x2 -> x4, starting transfers between devices: 12.4 us -> 29.6 us  [move(): return lax.ppermute(x, PLACES, pairs)]
    all_to_all x1, waiting for transfers between devices: 21.8 us -> 7.73 us  [shared(): return lax.all_to_all(x, PLACES, 0, 0, axis_index_groups=groups, tiled=True)]
    all_to_all x1, blocking collectives: 27.3 us -> 18.3 us  [shared(): return lax.all_to_all(x, PLACES, 0, 0, axis_index_groups=groups, tiled=True)]
    ppermute x2, starting transfers between devices: 16.2 us -> 7.23 us  [core_swap(): return lax.ppermute(x, 'core', [(0, 1), (1, 0)])]
    ppermute x2 -> x4, waiting for transfers between devices: 77.6 us -> 72.7 us  [move(): return lax.ppermute(x, PLACES, pairs)]
    dot_general x2 -> x0, matrix products: 3.91 us -> none  [the longest x1 2.44 us: local(): jnp.einsum('qa,qn->an', chip, right, precision=PRECISION, preferred_eleme...]
    pallas_call x0 -> x4, Pallas kernels: none -> 3.36 us  [kernel(): pl.pallas_call(body, out_shape=[jax.ShapeDtypeStruct(s, jnp.float32) for...]
    all_to_all x1, starting transfers between devices: 3.65 us -> 5.82 us  [shared(): return lax.all_to_all(x, PLACES, 0, 0, axis_index_groups=groups, tiled=True)]
  transfers between devices with their start and end apart: 5 -> 7, of which waited for: 5 -> 6; matrix products, arithmetic and copies ran while one was open for 1% -> 1% of each run, Pallas kernels for 0% -> 0%
where the time goes in v5:
time: 155 us; the launch traced here: 154 us
  waiting for transfers between devices  83.5 us (54%)
  starting transfers between devices  42.7 us (28%)
  blocking collectives  18.3 us (12%)
  Pallas kernels  3.36 us (2%)
  local copies, waits for them, and re-layouts  2.99 us (2%)
  between operations  1.94 us (1%)
    ppermute x4, waiting for transfers between devices, move(): return lax.ppermute(x, PLACES, pairs)  72.7 us
    ppermute x4, starting transfers between devices, move(): return lax.ppermute(x, PLACES, pairs)  29.6 us
    all_to_all x1, blocking collectives, shared(): return lax.all_to_all(x, PLACES, 0, 0, axis_index_groups=groups, tiled=True)  18.3 us
    all_to_all x1, waiting for transfers between devices, shared(): return lax.all_to_all(x, PLACES, 0, 0, axis_index_groups=groups, tiled=True)  7.73 us
    ppermute x2, starting transfers between devices, core_swap(): return lax.ppermute(x, 'core', [(0, 1), (1, 0)])  7.23 us
    all_to_all x1, starting transfers between devices, shared(): return lax.all_to_all(x, PLACES, 0, 0, axis_index_groups=groups, tiled=True)  5.82 us
    pallas_call x4, Pallas kernels, kernel(): pl.pallas_call(body, out_shape=[jax.ShapeDtypeStruct(s, jnp.float32) for...  3.36 us
  transfers between devices with their start and end apart: 7, of which 6 were waited for; matrix products, arithmetic and copies ran while one was open for 1% of the time, Pallas kernels for 0%

profile of v5, /device:TPU:1, one launch (start us, length us, event | category | flops | bytes accessed | tf_op | source)
XLA Modules:
  0.0 153.9 jit_solution(7863662975071594677)
XLA Ops:
  0.7 1.2 concatenate.3
  1.8 20.2 %collective-permute-start.1 = (f32[392,512]{1,0:T(8,128)S(1)}, f32[392,512]{1,0:T(8,128)S(1)}, u32[]{:S(2)}, u32[]{:S(2)}) collective-permute-start(f32[392,512]{1,0:T(8,128)S(1)} %concatenate.3), channel_id=1, source_target_pairs={{0,764},{2,766},{4,744},{6,746},{8,4},{10,6},{12,8},{14,10},{16,12... | collective-permute-start | bytes 2408456 | tf_op jit(solution)/shard_map/ppermute | solution.py:36
  22.1 1.9 %collective-permute-start = (f32[392,512]{1,0:T(8,128)S(1)}, f32[392,512]{1,0:T(8,128)S(1)}, u32[]{:S(2)}, u32[]{:S(2)}) collective-permute-start(f32[392,512]{1,0:T(8,128)S(1)} %concatenate.3), channel_id=1, source_target_pairs={{0,4},{2,6},{4,8},{6,10},{8,12},{10,14},{12,16},{14,18},{16,20},{1... | collective-permute-start | bytes 2408456 | tf_op jit(solution)/shard_map/ppermute | solution.py:36
  24.0 31.9 %collective-permute-done.1.upper_ref = f32[392,512]{1,0:T(8,128)S(1)} collective-permute-done((f32[392,512]{1,0:T(8,128)S(1)}, f32[392,512]{1,0:T(8,128)S(1)}, u32[]{:S(2)}, u32[]{:S(2)}) %collective-permute-start.1) | collective-permute-done | bytes 802848 | tf_op jit(solution)/shard_map/ppermute | solution.py:36
  55.9 5.7 %collective-permute-done.lower_ref = f32[392,512]{1,0:T(8,128)S(1)} collective-permute-done((f32[392,512]{1,0:T(8,128)S(1)}, f32[392,512]{1,0:T(8,128)S(1)}, u32[]{:S(2)}, u32[]{:S(2)}) %collective-permute-start) | collective-permute-done | bytes 802848 | tf_op jit(solution)/shard_map/ppermute | solution.py:36
  61.6 1.0 shard_map.40
  62.7 3.8 %collective-permute-start.2 = (f32[512,256]{1,0:T(8,128)S(1)}, f32[512,256]{1,0:T(8,128)S(1)}, u32[]{:S(2)}, u32[]{:S(2)}) collective-permute-start(f32[512,256]{1,0:T(8,128)S(1)} %get-tuple-element.10), channel_id=1, source_target_pairs={{0,1},{1,0},{2,3},{3,2},{4,5},{5,4},{6,7},{7,6},{8,9},{9,8},{10,11... | collective-permute-start | bytes 1572872 | tf_op jit(solution)/shard_map/ppermute | solution.py:40
  66.5 1.5 collective-permute-done.2.got_ref
  68.0 0.8 shard_map.41
  68.9 5.8 %all-to-all-start = ((f32[4,128,256]{2,1,0:T(8,128)}), f32[4,128,256]{2,1,0:T(8,128)S(1)}, u32[]{:S(2)}, u32[]{:S(2)}) async-start(f32[4,128,256]{2,1,0:T(8,128)} %shard_map.41), calls=%async_computation | async-start | bytes 1048576 | tf_op jit(solution)/shard_map/all_to_all | solution.py:118
  74.7 0.7 copy-done
  75.5 0.5 slice.9
  76.0 0.5 slice.8
  77.7 0.1 dynamic-slice_subtract_fusion
  77.8 0.1 broadcast_add_fusion.denominator_ref
  77.9 7.7 %all-to-all-done.parts_ref = f32[4,128,256]{2,1,0:T(8,128)S(1)} async-done(((f32[4,128,256]{2,1,0:T(8,128)}), f32[4,128,256]{2,1,0:T(8,128)S(1)}, u32[]{:S(2)}, u32[]{:S(2)}) %all-to-all-start) | async-done | bytes 524320 | tf_op jit(solution)/shard_map/all_to_all | solution.py:118
  85.7 18.3 %all_to_all.10.amp_ref = f32[4,128,256]{2,1,0:T(8,128)S(1)} all-to-all(f32[4,128,256]{2,1,0:T(8,128)S(1)} %shard_map.42), channel_id=1, replica_groups={{4,6,8,10},{12,14,16,18},{20,22,0,2},{28,30,32,34},{36,38,40,42},{44,46..., dimensions={0} | all-to-all | bytes 1048576 | tf_op jit(solution)/shard_map/all_to_all | solution.py:118
  103.9 3.4 %collective-permute-start.3 = (f32[4,128,256]{2,1,0:T(8,128)S(1)}, f32[4,128,256]{2,1,0:T(8,128)S(1)}, u32[]{:S(2)}, u32[]{:S(2)}) collective-permute-start(f32[4,128,256]{2,1,0:T(8,128)S(1)} %all_to_all.10.amp_ref), channel_id=1, source_target_pairs={{0,1},{1,0},{2,3},{3,2},{4,5},{5,4},{6,7},{7,6},{8,9},{9,8},{10,11... | collective-permute-start | bytes 1572872 | tf_op jit(solution)/shard_map/ppermute | solution.py:40
  107.3 1.5 collective-permute-done.3.swapped_ref
  108.8 1.4 shard_map.43
  110.3 1.9 %collective-permute-start.4 = (f32[384,512]{1,0:T(8,128)S(1)}, f32[384,512]{1,0:T(8,128)S(1)}, u32[]{:S(2)}, u32[]{:S(2)}) collective-permute-start(f32[384,512]{1,0:T(8,128)S(1)} %get-tuple-element.11), channel_id=1, source_target_pairs={{764,0},{766,2},{744,4},{746,6},{4,8},{6,10},{8,12},{10,14},{12,16... | collective-permute-start | bytes 2359304 | tf_op jit(solution)/shard_map/ppermute | solution.py:36
  112.2 5.6 %collective-permute-start.5 = (f32[384,512]{1,0:T(8,128)S(1)}, f32[384,512]{1,0:T(8,128)S(1)}, u32[]{:S(2)}, u32[]{:S(2)}) collective-permute-start(f32[384,512]{1,0:T(8,128)S(1)} %get-tuple-element.12), channel_id=1, source_target_pairs={{4,0},{6,2},{8,4},{10,6},{12,8},{14,10},{16,12},{18,14},{20,16},{2... | collective-permute-start | bytes 2359304 | tf_op jit(solution)/shard_map/ppermute | solution.py:36
  117.8 35.1 %collective-permute-done.4 = f32[384,512]{1,0:T(8,128)S(1)} collective-permute-done((f32[384,512]{1,0:T(8,128)S(1)}, f32[384,512]{1,0:T(8,128)S(1)}, u32[]{:S(2)}, u32[]{:S(2)}) %collective-permute-start.4) | collective-permute-done | bytes 786464 | tf_op jit(solution)/shard_map/ppermute | solution.py:36
  152.9 1.0 add_bitcast_fusion
  (4 shorter events, 0.1 us)
Async XLA Ops:
  1.8 54.1 %collective-permute-start.1 = (f32[392,512]{1,0:T(8,128)S(1)}, f32[392,512]{1,0:T(8,128)S(1)}, u32[]{:S(2)}, u32[]{:S(2)}) collective-permute-start(f32[392,512]{1,0:T(8,128)S(1)} %concatenate.3), channel_id=1, source_target_pairs={{0,764},{2,766},{4,744},{6,746},{8,4},{10,6},{12,8},{14,10},{16,12... | collective-permute-start | bytes 2408456 | tf_op jit(solution)/shard_map/ppermute | solution.py:36
  22.1 39.6 %collective-permute-start = (f32[392,512]{1,0:T(8,128)S(1)}, f32[392,512]{1,0:T(8,128)S(1)}, u32[]{:S(2)}, u32[]{:S(2)}) collective-permute-start(f32[392,512]{1,0:T(8,128)S(1)} %concatenate.3), channel_id=1, source_target_pairs={{0,4},{2,6},{4,8},{6,10},{8,12},{10,14},{12,16},{14,18},{16,20},{1... | collective-permute-start | bytes 2408456 | tf_op jit(solution)/shard_map/ppermute | solution.py:36
  62.7 5.3 %collective-permute-start.2 = (f32[512,256]{1,0:T(8,128)S(1)}, f32[512,256]{1,0:T(8,128)S(1)}, u32[]{:S(2)}, u32[]{:S(2)}) collective-permute-start(f32[512,256]{1,0:T(8,128)S(1)} %get-tuple-element.10), channel_id=1, source_target_pairs={{0,1},{1,0},{2,3},{3,2},{4,5},{5,4},{6,7},{7,6},{8,9},{9,8},{10,11... | collective-permute-start | bytes 1572872 | tf_op jit(solution)/shard_map/ppermute | solution.py:40
  68.9 16.7 %all-to-all-start = ((f32[4,128,256]{2,1,0:T(8,128)}), f32[4,128,256]{2,1,0:T(8,128)S(1)}, u32[]{:S(2)}, u32[]{:S(2)}) async-start(f32[4,128,256]{2,1,0:T(8,128)} %shard_map.41), calls=%async_computation | async-start | bytes 1048576 | tf_op jit(solution)/shard_map/all_to_all | solution.py:118
  74.7 0.7 copy-start
  103.9 4.9 %collective-permute-start.3 = (f32[4,128,256]{2,1,0:T(8,128)S(1)}, f32[4,128,256]{2,1,0:T(8,128)S(1)}, u32[]{:S(2)}, u32[]{:S(2)}) collective-permute-start(f32[4,128,256]{2,1,0:T(8,128)S(1)} %all_to_all.10.amp_ref), channel_id=1, source_target_pairs={{0,1},{1,0},{2,3},{3,2},{4,5},{5,4},{6,7},{7,6},{8,9},{9,8},{10,11... | collective-permute-start | bytes 1572872 | tf_op jit(solution)/shard_map/ppermute | solution.py:40
  110.3 42.6 %collective-permute-start.4 = (f32[384,512]{1,0:T(8,128)S(1)}, f32[384,512]{1,0:T(8,128)S(1)}, u32[]{:S(2)}, u32[]{:S(2)}) collective-permute-start(f32[384,512]{1,0:T(8,128)S(1)} %get-tuple-element.11), channel_id=1, source_target_pairs={{764,0},{766,2},{744,4},{746,6},{4,8},{6,10},{8,12},{10,14},{12,16... | collective-permute-start | bytes 2359304 | tf_op jit(solution)/shard_map/ppermute | solution.py:36
  112.2 40.7 %collective-permute-start.5 = (f32[384,512]{1,0:T(8,128)S(1)}, f32[384,512]{1,0:T(8,128)S(1)}, u32[]{:S(2)}, u32[]{:S(2)}) collective-permute-start(f32[384,512]{1,0:T(8,128)S(1)} %get-tuple-element.12), channel_id=1, source_target_pairs={{4,0},{6,2},{8,4},{10,6},{12,8},{14,10},{16,12},{18,14},{20,16},{2... | collective-permute-start | bytes 2359304 | tf_op jit(solution)/shard_map/ppermute | solution.py:36

commit v6 on v5

v6 whole, which is shorter than its diff:
```python
import jax
import jax.numpy as jnp
from jax import lax
from jax.experimental import pallas as pl
from jax.experimental.pallas import tpu as pltpu
from jax.sharding import Mesh, PartitionSpec as P

CHIPS = 4
LEVELS = 3
RING = CHIPS * LEVELS
PLACES = ("occ", "z")
SMEM = pl.BlockSpec(memory_space=pltpu.SMEM)
VMEM = pl.BlockSpec(memory_space=pltpu.VMEM)
ANY = pl.BlockSpec(memory_space=pl.ANY)


def meetings(occupied):
    columns = occupied // LEVELS
    above, below = [], []
    for place in range(occupied * CHIPS):
        column, height = divmod(place, RING)
        above.append(column * RING + (height + CHIPS // 2) % RING)
        shift = 1 if height < CHIPS else 0
        below.append((column - shift) % columns * RING + (height - CHIPS // 2) % RING)
    return above, below


def in_two(above, below):
    up_first = [place % CHIPS < CHIPS // 2 for place in range(len(above))]
    first = [a if up else b for a, b, up in zip(above, below, up_first)]
    second = [b if up else a for a, b, up in zip(above, below, up_first)]
    return first, second


def there(goals):
    return [(place, goal) for place, goal in enumerate(goals)]


def back(goals):
    return [(goal, place) for place, goal in enumerate(goals)]


def move(x, pairs):
    return lax.ppermute(x, PLACES, pairs)


def core_swap(x):
    return lax.ppermute(x, "core", [(0, 1), (1, 0)])


def kernel(body, shapes, scalars, arrays, after=()):
    used = len(scalars) + len(arrays)

    def run(*refs):
        body(*refs[:used], *refs[used + len(after) :])

    return pl.pallas_call(
        run,
        out_shape=[jax.ShapeDtypeStruct(s, jnp.float32) for s in shapes],
        in_specs=[SMEM] * len(scalars) + [VMEM] * len(arrays) + [ANY] * len(after),
        out_specs=[VMEM] * len(shapes),
        compiler_params=pltpu.CompilerParams(vmem_limit_bytes=24 * 2**20),
    )(*[s.reshape(1) for s in scalars], *arrays, *after)


def split(x):
    high = x.astype(jnp.bfloat16)
    return high, (x - high.astype(jnp.float32)).astype(jnp.bfloat16)


def dot(x, y, dims):
    def one(u, v):
        return lax.dot_general(u, v, (dims, ((), ())), preferred_element_type=jnp.float32)

    return one(x[0], y[0]) + (one(x[0], y[1]) + one(x[1], y[0]))


def block(start_ref, width):
    return pl.ds(pl.multiple_of(start_ref[0], width), width)


def ordered(chip_ref, first_ref, second_ref, body):
    low_first = chip_ref[0] < CHIPS // 2
    pl.when(low_first)(lambda: body(first_ref, second_ref))
    pl.when(jnp.logical_not(low_first))(lambda: body(second_ref, first_ref))


def pair_tile(chip_ref, mine_ref, other_ref, first_ref, second_ref, keep_ref, give_ref):
    def body(lower_ref, upper_ref):
        upper = split(upper_ref[...])
        for start_ref, out_ref in ((other_ref, give_ref), (mine_ref, keep_ref)):
            columns = block(start_ref, out_ref.shape[1])
            out_ref[...] = dot(upper, split(lower_ref[:, columns]), ((0,), (0,)))

    ordered(chip_ref, first_ref, second_ref, body)


def add_tiles(keep_ref, got_ref, out_ref):
    out_ref[...] = (keep_ref[...] + got_ref[...]).reshape(out_ref.shape)


def divide(parts_ref, denominator_ref, out_ref):
    total = (parts_ref[0] + parts_ref[1]) + (parts_ref[2] + parts_ref[3])
    amplitude = total / denominator_ref[...]
    for k in range(CHIPS):
        out_ref[k] = amplitude


def density_parts(chip_ref, mine_ref, other_ref, first_ref, second_ref, amp_ref, swapped_ref, out_1_ref, out_2_ref):
    virt, width = first_ref.shape[1], amp_ref.shape[2]

    def body(lower_ref, upper_ref, for_lower_ref, for_upper_ref):
        upper = split(upper_ref[...])
        total = None
        for start_ref, half_ref in ((mine_ref, amp_ref), (other_ref, swapped_ref)):
            columns = block(start_ref, width)
            amp = split(half_ref[...].reshape(virt, width))
            for_lower_ref[:, columns] = dot(upper, amp, ((1,), (0,)))
            part = dot(split(lower_ref[:, columns]), amp, ((1,), (1,)))
            total = part if total is None else total + part
        for_upper_ref[...] = total

    low_first = chip_ref[0] < CHIPS // 2
    pl.when(low_first)(lambda: body(first_ref, second_ref, out_1_ref, out_2_ref))
    pl.when(jnp.logical_not(low_first))(lambda: body(second_ref, first_ref, out_2_ref, out_1_ref))


def local(factors, occ_energy, virt_energy):
    own = factors[0]
    rows, virt = own.shape
    half, quarter = virt // 2, virt // CHIPS
    occupied = lax.axis_size("occ")
    above, below = meetings(occupied)
    first, second = in_two(above, below)
    groups = [
        [above[level * CHIPS + RING * column + c] for c in range(CHIPS)]
        for column in range(occupied // LEVELS)
        for level in range(LEVELS)
    ]
    mine = lax.axis_index("core") * half
    other = half - mine
    chip = lax.rem(lax.axis_index("z") + CHIPS // 2, CHIPS)

    def shared(x):
        return lax.all_to_all(x, PLACES, 0, 0, axis_index_groups=groups, tiled=True)

    got_1, got_2 = move(own, there(first)), move(own, there(second))
    energies = move(occ_energy, there(first)), move(occ_energy, there(second))
    keep, give = kernel(pair_tile, [(virt, half)] * 2, [chip, mine, other], [got_1, got_2], energies)
    whole = (CHIPS, quarter, half)
    tile = kernel(add_tiles, [whole], [], [keep, core_swap(give)])[0]
    row_energy = lax.dynamic_slice_in_dim(virt_energy, chip * quarter, quarter, 0)
    column_energy = lax.dynamic_slice_in_dim(virt_energy, mine, half, 0)
    denominator = (row_energy - (energies[0] + energies[1]))[:, None] + column_energy[None, :]
    amp = shared(kernel(divide, [whole], [], [shared(tile), denominator])[0])
    part_1, part_2 = kernel(
        density_parts, [(rows, virt)] * 2, [chip, mine, other], [got_1, got_2, amp, core_swap(amp)]
    )
    return (move(part_1, back(first)) + move(part_2, back(second)))[None]


def solution(mesh):
    cube = Mesh(mesh.devices.reshape(mesh.devices.shape[0], CHIPS, 2), (*PLACES, "core"))
    spec = P("occ", ("z", "core"), None)
    return jax.shard_map(local, mesh=cube, in_specs=(spec, P("occ"), P()), out_specs=spec, check_vma=False)
```

time: 155 us -> 156 us (level)
  starting transfers between devices: 42.7 us -> 48.2 us
  waiting for transfers between devices: 83.5 us -> 80.7 us
  local copies, waits for them, and re-layouts: 2.99 us -> 0.75 us
    ppermute x4 -> x6, starting transfers between devices: 29.6 us -> 36.6 us  [move(): return lax.ppermute(x, PLACES, pairs)]
    ppermute x4 -> x6, waiting for transfers between devices: 72.7 us -> 68.9 us  [move(): return lax.ppermute(x, PLACES, pairs)]
  transfers between devices with their start and end apart: 7 -> 9, of which waited for: 6 -> 7; matrix products, arithmetic and copies ran while one was open for 1% -> 0% of each run, Pallas kernels for 0% -> 0%
where the time goes in v6:
time: 156 us; the launch traced here: 155 us
  waiting for transfers between devices  80.7 us (52%)
  starting transfers between devices  48.2 us (31%)
  blocking collectives  18.3 us (12%)
  Pallas kernels  4.61 us (3%)
    ppermute x6, waiting for transfers between devices, move(): return lax.ppermute(x, PLACES, pairs)  68.9 us
    ppermute x6, starting transfers between devices, move(): return lax.ppermute(x, PLACES, pairs)  36.6 us
    all_to_all x1, blocking collectives, shared(): return lax.all_to_all(x, PLACES, 0, 0, axis_index_groups=groups, tiled=True)  18.3 us
    all_to_all x1, waiting for transfers between devices, shared(): return lax.all_to_all(x, PLACES, 0, 0, axis_index_groups=groups, tiled=True)  8.72 us
    ppermute x2, starting transfers between devices, core_swap(): return lax.ppermute(x, 'core', [(0, 1), (1, 0)])  6.78 us
    all_to_all x1, starting transfers between devices, shared(): return lax.all_to_all(x, PLACES, 0, 0, axis_index_groups=groups, tiled=True)  4.84 us
    pallas_call x4, Pallas kernels, kernel(): pl.pallas_call(run, out_shape=[jax.ShapeDtypeStruct(s, jnp.float32) for s...  4.61 us
  transfers between devices with their start and end apart: 9, of which 7 were waited for; matrix products, arithmetic and copies ran while one was open for 0% of the time, Pallas kernels for 0%

profile of v6, /device:TPU:1, one launch (start us, length us, event | category | flops | bytes accessed | tf_op | source)
XLA Modules:
  0.0 155.1 jit_solution(5063923254297382108)
XLA Ops:
  0.0 20.2 %collective-permute-start.1 = (f32[384,512]{1,0:T(8,128)}, f32[384,512]{1,0:T(8,128)S(1)}, u32[]{:S(2)}, u32[]{:S(2)}) collective-permute-start(f32[384,512]{1,0:T(8,128)} %bitcast.7), channel_id=1, source_target_pairs={{0,764},{2,766},{4,8},{6,10},{8,4},{10,6},{12,16},{14,18},{16,12},... | collective-permute-start | bytes 2359304 | tf_op jit(solution)/shard_map/ppermute | solution.py:44
  20.2 1.9 %collective-permute-start = (f32[384,512]{1,0:T(8,128)}, f32[384,512]{1,0:T(8,128)S(1)}, u32[]{:S(2)}, u32[]{:S(2)}) collective-permute-start(f32[384,512]{1,0:T(8,128)} %bitcast.8), channel_id=1, source_target_pairs={{0,4},{2,6},{4,744},{6,746},{8,12},{10,14},{12,8},{14,10},{16,20},... | collective-permute-start | bytes 2359304 | tf_op jit(solution)/shard_map/ppermute | solution.py:44
  22.1 3.0 %collective-permute-start.3 = (f32[1]{0:T(128)}, f32[1]{0:T(128)}, u32[]{:S(2)}, u32[]{:S(2)}) collective-permute-start(f32[1]{0:T(128)} %param.4), channel_id=1, source_target_pairs={{0,764},{2,766},{4,8},{6,10},{8,4},{10,6},{12,16},{14,18},{16,12},... | collective-permute-start | bytes 20 | tf_op jit(solution)/shard_map/ppermute | solution.py:44
  25.2 3.9 %collective-permute-start.2 = (f32[1]{0:T(128)}, f32[1]{0:T(128)}, u32[]{:S(2)}, u32[]{:S(2)}) collective-permute-start(f32[1]{0:T(128)} %param.4), channel_id=1, source_target_pairs={{0,4},{2,6},{4,744},{6,746},{8,12},{10,14},{12,8},{14,10},{16,20},... | collective-permute-start | bytes 20 | tf_op jit(solution)/shard_map/ppermute | solution.py:44
  29.1 24.6 %collective-permute-done.3.refs_6_ = f32[1]{0:T(128)} collective-permute-done((f32[1]{0:T(128)}, f32[1]{0:T(128)}, u32[]{:S(2)}, u32[]{:S(2)}) %collective-permute-start.3) | collective-permute-done | bytes 36 | tf_op jit(solution)/shard_map/ppermute | solution.py:44
  53.8 5.7 %collective-permute-done.2.refs_5_ = f32[1]{0:T(128)} collective-permute-done((f32[1]{0:T(128)}, f32[1]{0:T(128)}, u32[]{:S(2)}, u32[]{:S(2)}) %collective-permute-start.2) | collective-permute-done | bytes 36 | tf_op jit(solution)/shard_map/ppermute | solution.py:44
  59.5 2.3 %shard_map.37 = (f32[512,256]{1,0:T(8,128)S(1)}, f32[512,256]{1,0:T(8,128)S(1)}) custom-call(s32[1]{0:T(128)} %bitcast.refs_0_, s32[1]{0:T(128)} %bitcast.1.refs_1_, s32[1]{0:T(128)} %bitcast.2.refs_2_, f32[384,512]{1,0:T(8,128)S(1)} %collective-permute-done.refs_3_, f32[384,512]{1,0:T(8,128)S(1)} %collective-permute-done.1.refs_4_, ...), custom_call_target="tpu_custom_call" | custom-call | tf_op jit(solution)/shard_map/pallas_call | solution.py:57
  61.8 3.4 %collective-permute-start.4 = (f32[512,256]{1,0:T(8,128)S(1)}, f32[512,256]{1,0:T(8,128)S(1)}, u32[]{:S(2)}, u32[]{:S(2)}) collective-permute-start(f32[512,256]{1,0:T(8,128)S(1)} %get-tuple-element.10), channel_id=1, source_target_pairs={{0,1},{1,0},{2,3},{3,2},{4,5},{5,4},{6,7},{7,6},{8,9},{9,8},{10,11... | collective-permute-start | bytes 1572872 | tf_op jit(solution)/shard_map/ppermute | solution.py:48
  65.2 1.5 collective-permute-done.4.refs_1_
  66.7 0.8 shard_map.38
  67.6 4.8 %all-to-all-start = ((f32[4,128,256]{2,1,0:T(8,128)}), f32[4,128,256]{2,1,0:T(8,128)S(1)}, u32[]{:S(2)}, u32[]{:S(2)}) async-start(f32[4,128,256]{2,1,0:T(8,128)} %shard_map.38), calls=%async_computation | async-start | bytes 1048576 | tf_op jit(solution)/shard_map/all_to_all | solution.py:145
  72.4 0.7 copy-done
  74.4 0.1 dynamic-slice_subtract_fusion
  74.5 0.1 broadcast_add_fusion.refs_1_
  74.6 8.7 %all-to-all-done.refs_0_ = f32[4,128,256]{2,1,0:T(8,128)S(1)} async-done(((f32[4,128,256]{2,1,0:T(8,128)}), f32[4,128,256]{2,1,0:T(8,128)S(1)}, u32[]{:S(2)}, u32[]{:S(2)}) %all-to-all-start) | async-done | bytes 524320 | tf_op jit(solution)/shard_map/all_to_all | solution.py:145
  83.4 18.3 %all_to_all.10.refs_5_ = f32[4,128,256]{2,1,0:T(8,128)S(1)} all-to-all(f32[4,128,256]{2,1,0:T(8,128)S(1)} %shard_map.39), channel_id=1, replica_groups={{4,6,8,10},{12,14,16,18},{20,22,0,2},{28,30,32,34},{36,38,40,42},{44,46..., dimensions={0} | all-to-all | bytes 1048576 | tf_op jit(solution)/shard_map/all_to_all | solution.py:145
  101.6 3.4 %collective-permute-start.5 = (f32[4,128,256]{2,1,0:T(8,128)S(1)}, f32[4,128,256]{2,1,0:T(8,128)S(1)}, u32[]{:S(2)}, u32[]{:S(2)}) collective-permute-start(f32[4,128,256]{2,1,0:T(8,128)S(1)} %all_to_all.10.refs_5_), channel_id=1, source_target_pairs={{0,1},{1,0},{2,3},{3,2},{4,5},{5,4},{6,7},{7,6},{8,9},{9,8},{10,11... | collective-permute-start | bytes 1572872 | tf_op jit(solution)/shard_map/ppermute | solution.py:48
  105.0 1.5 collective-permute-done.5.refs_6_
  106.5 1.4 shard_map.40
  107.9 3.7 %collective-permute-start.6 = (f32[384,512]{1,0:T(8,128)S(1)}, f32[384,512]{1,0:T(8,128)S(1)}, u32[]{:S(2)}, u32[]{:S(2)}) collective-permute-start(f32[384,512]{1,0:T(8,128)S(1)} %get-tuple-element.11), channel_id=1, source_target_pairs={{4,0},{6,2},{744,4},{746,6},{12,8},{14,10},{8,12},{10,14},{20,16},... | collective-permute-start | bytes 2359304 | tf_op jit(solution)/shard_map/ppermute | solution.py:44
  111.7 3.8 %collective-permute-start.7 = (f32[384,512]{1,0:T(8,128)S(1)}, f32[384,512]{1,0:T(8,128)S(1)}, u32[]{:S(2)}, u32[]{:S(2)}) collective-permute-start(f32[384,512]{1,0:T(8,128)S(1)} %get-tuple-element.12), channel_id=1, source_target_pairs={{764,0},{766,2},{8,4},{10,6},{4,8},{6,10},{16,12},{18,14},{12,16},... | collective-permute-start | bytes 2359304 | tf_op jit(solution)/shard_map/ppermute | solution.py:44
  115.4 30.9 %collective-permute-done.6 = f32[384,512]{1,0:T(8,128)S(1)} collective-permute-done((f32[384,512]{1,0:T(8,128)S(1)}, f32[384,512]{1,0:T(8,128)S(1)}, u32[]{:S(2)}, u32[]{:S(2)}) %collective-permute-start.6) | collective-permute-done | bytes 786464 | tf_op jit(solution)/shard_map/ppermute | solution.py:44
  146.3 7.7 %collective-permute-done.7 = f32[384,512]{1,0:T(8,128)S(1)} collective-permute-done((f32[384,512]{1,0:T(8,128)S(1)}, f32[384,512]{1,0:T(8,128)S(1)}, u32[]{:S(2)}, u32[]{:S(2)}) %collective-permute-start.7) | collective-permute-done | bytes 786464 | tf_op jit(solution)/shard_map/ppermute | solution.py:44
  154.0 1.0 add_bitcast_fusion
  (5 shorter events, 0.1 us)
Async XLA Ops:
  0.0 59.5 %collective-permute-start.1 = (f32[384,512]{1,0:T(8,128)}, f32[384,512]{1,0:T(8,128)S(1)}, u32[]{:S(2)}, u32[]{:S(2)}) collective-permute-start(f32[384,512]{1,0:T(8,128)} %bitcast.7), channel_id=1, source_target_pairs={{0,764},{2,766},{4,8},{6,10},{8,4},{10,6},{12,16},{14,18},{16,12},... | collective-permute-start | bytes 2359304 | tf_op jit(solution)/shard_map/ppermute | solution.py:44
  20.2 39.3 %collective-permute-start = (f32[384,512]{1,0:T(8,128)}, f32[384,512]{1,0:T(8,128)S(1)}, u32[]{:S(2)}, u32[]{:S(2)}) collective-permute-start(f32[384,512]{1,0:T(8,128)} %bitcast.8), channel_id=1, source_target_pairs={{0,4},{2,6},{4,744},{6,746},{8,12},{10,14},{12,8},{14,10},{16,20},... | collective-permute-start | bytes 2359304 | tf_op jit(solution)/shard_map/ppermute | solution.py:44
  22.1 31.6 %collective-permute-start.3 = (f32[1]{0:T(128)}, f32[1]{0:T(128)}, u32[]{:S(2)}, u32[]{:S(2)}) collective-permute-start(f32[1]{0:T(128)} %param.4), channel_id=1, source_target_pairs={{0,764},{2,766},{4,8},{6,10},{8,4},{10,6},{12,16},{14,18},{16,12},... | collective-permute-start | bytes 20 | tf_op jit(solution)/shard_map/ppermute | solution.py:44
  25.2 34.3 %collective-permute-start.2 = (f32[1]{0:T(128)}, f32[1]{0:T(128)}, u32[]{:S(2)}, u32[]{:S(2)}) collective-permute-start(f32[1]{0:T(128)} %param.4), channel_id=1, source_target_pairs={{0,4},{2,6},{4,744},{6,746},{8,12},{10,14},{12,8},{14,10},{16,20},... | collective-permute-start | bytes 20 | tf_op jit(solution)/shard_map/ppermute | solution.py:44
  61.8 4.9 %collective-permute-start.4 = (f32[512,256]{1,0:T(8,128)S(1)}, f32[512,256]{1,0:T(8,128)S(1)}, u32[]{:S(2)}, u32[]{:S(2)}) collective-permute-start(f32[512,256]{1,0:T(8,128)S(1)} %get-tuple-element.10), channel_id=1, source_target_pairs={{0,1},{1,0},{2,3},{3,2},{4,5},{5,4},{6,7},{7,6},{8,9},{9,8},{10,11... | collective-permute-start | bytes 1572872 | tf_op jit(solution)/shard_map/ppermute | solution.py:48
  67.6 15.7 %all-to-all-start = ((f32[4,128,256]{2,1,0:T(8,128)}), f32[4,128,256]{2,1,0:T(8,128)S(1)}, u32[]{:S(2)}, u32[]{:S(2)}) async-start(f32[4,128,256]{2,1,0:T(8,128)} %shard_map.38), calls=%async_computation | async-start | bytes 1048576 | tf_op jit(solution)/shard_map/all_to_all | solution.py:145
  72.4 0.7 copy-start
  101.6 4.9 %collective-permute-start.5 = (f32[4,128,256]{2,1,0:T(8,128)S(1)}, f32[4,128,256]{2,1,0:T(8,128)S(1)}, u32[]{:S(2)}, u32[]{:S(2)}) collective-permute-start(f32[4,128,256]{2,1,0:T(8,128)S(1)} %all_to_all.10.refs_5_), channel_id=1, source_target_pairs={{0,1},{1,0},{2,3},{3,2},{4,5},{5,4},{6,7},{7,6},{8,9},{9,8},{10,11... | collective-permute-start | bytes 1572872 | tf_op jit(solution)/shard_map/ppermute | solution.py:48
  107.9 38.4 %collective-permute-start.6 = (f32[384,512]{1,0:T(8,128)S(1)}, f32[384,512]{1,0:T(8,128)S(1)}, u32[]{:S(2)}, u32[]{:S(2)}) collective-permute-start(f32[384,512]{1,0:T(8,128)S(1)} %get-tuple-element.11), channel_id=1, source_target_pairs={{4,0},{6,2},{744,4},{746,6},{12,8},{14,10},{8,12},{10,14},{20,16},... | collective-permute-start | bytes 2359304 | tf_op jit(solution)/shard_map/ppermute | solution.py:44
  111.7 42.4 %collective-permute-start.7 = (f32[384,512]{1,0:T(8,128)S(1)}, f32[384,512]{1,0:T(8,128)S(1)}, u32[]{:S(2)}, u32[]{:S(2)}) collective-permute-start(f32[384,512]{1,0:T(8,128)S(1)} %get-tuple-element.12), channel_id=1, source_target_pairs={{764,0},{766,2},{8,4},{10,6},{4,8},{6,10},{16,12},{18,14},{12,16},... | collective-permute-start | bytes 2359304 | tf_op jit(solution)/shard_map/ppermute | solution.py:44

commit v7 on v5

v7 whole, which is shorter than its diff:
```python
import jax
import jax.numpy as jnp
import numpy as np
from jax import lax
from jax.experimental import pallas as pl
from jax.experimental.pallas import tpu as pltpu
from jax.sharding import Mesh, PartitionSpec as P

CHIPS = 4
LEVELS = 3
RING = CHIPS * LEVELS
ROWS = 8
PLACES = ("occ", "z")
SMEM = pl.BlockSpec(memory_space=pltpu.SMEM)
VMEM = pl.BlockSpec(memory_space=pltpu.VMEM)
ANY = pl.BlockSpec(memory_space=pl.ANY)


def meeting(column, level, chunk):
    x, y = divmod(column, ROWS)
    crosses = (chunk + y + level) % 2
    plane = 2 + 2 * (x % 2) + chunk // 2
    return ((x ^ crosses) * ROWS + y) * RING + (level * CHIPS + plane) % RING


def meetings(occupied):
    above, below, groups = [0] * (occupied * CHIPS), [0] * (occupied * CHIPS), []
    for i in range(occupied):
        groups.append([meeting(*divmod(i, LEVELS), chunk) for chunk in range(CHIPS)])
        for chunk, goal in enumerate(groups[-1]):
            above[i * CHIPS + chunk] = goal
            below[(i + 1) % occupied * CHIPS + chunk] = goal
    return above, below, groups


def there(goals):
    return [(place, goal) for place, goal in enumerate(goals)]


def back(goals):
    return [(goal, place) for place, goal in enumerate(goals)]


def move(x, pairs):
    return lax.ppermute(x, PLACES, pairs)


def core_swap(x):
    return lax.ppermute(x, "core", [(0, 1), (1, 0)])


def kernel(body, shapes, scalars, arrays, after=()):
    used = len(scalars) + len(arrays)

    def run(*refs):
        body(*refs[:used], *refs[used + len(after) :])

    return pl.pallas_call(
        run,
        out_shape=[jax.ShapeDtypeStruct(s, jnp.float32) for s in shapes],
        in_specs=[SMEM] * len(scalars) + [VMEM] * len(arrays) + [ANY] * len(after),
        out_specs=[VMEM] * len(shapes),
        compiler_params=pltpu.CompilerParams(vmem_limit_bytes=24 * 2**20),
    )(*[s.reshape(1) for s in scalars], *arrays, *after)


def split(x):
    high = x.astype(jnp.bfloat16)
    return high, (x - high.astype(jnp.float32)).astype(jnp.bfloat16)


def dot(x, y, dims):
    def one(u, v):
        return lax.dot_general(u, v, (dims, ((), ())), preferred_element_type=jnp.float32)

    return one(x[0], y[0]) + (one(x[0], y[1]) + one(x[1], y[0]))


def block(start_ref, width):
    return pl.ds(pl.multiple_of(start_ref[0], width), width)


def pair_tile(mine_ref, other_ref, lower_ref, upper_ref, keep_ref, give_ref):
    width = keep_ref.shape[1]
    upper = split(upper_ref[...])
    for start_ref, out_ref in ((other_ref, give_ref), (mine_ref, keep_ref)):
        out_ref[...] = dot(upper, split(lower_ref[:, block(start_ref, width)]), ((0,), (0,)))


def add_tiles(keep_ref, got_ref, out_ref):
    out_ref[...] = (keep_ref[...] + got_ref[...]).reshape(out_ref.shape)


def divide(parts_ref, denominator_ref, out_ref):
    total = (parts_ref[0] + parts_ref[1]) + (parts_ref[2] + parts_ref[3])
    amplitude = total / denominator_ref[...]
    for k in range(CHIPS):
        out_ref[k] = amplitude


def density_parts(mine_ref, other_ref, lower_ref, upper_ref, amp_ref, swapped_ref, up_ref, down_ref):
    rows, virt = up_ref.shape
    width = amp_ref.shape[2]
    upper = split(upper_ref[...])
    total = None
    for start_ref, half_ref in ((mine_ref, amp_ref), (other_ref, swapped_ref)):
        columns = block(start_ref, width)
        amp = split(half_ref[...].reshape(virt, width))
        down_ref[:, columns] = dot(upper, amp, ((1,), (0,)))
        part = dot(split(lower_ref[:, columns]), amp, ((1,), (1,)))
        total = part if total is None else total + part
    up_ref[...] = total


def local(factors, occ_energy, virt_energy):
    own = factors[0]
    rows, virt = own.shape
    half, quarter = virt // 2, virt // CHIPS
    occupied = lax.axis_size("occ")
    above, below, groups = meetings(occupied)
    order = np.argsort(np.ravel(groups)) % CHIPS
    mine = lax.axis_index("core") * half
    other = half - mine
    place = lax.axis_index("occ") * CHIPS + lax.axis_index("z")
    chip = lax.dynamic_index_in_dim(jnp.asarray(order, jnp.int32), place, keepdims=False)

    def shared(x):
        return lax.all_to_all(x, PLACES, 0, 0, axis_index_groups=groups, tiled=True)

    lower, upper = move(own, there(above)), move(own, there(below))
    energies = move(occ_energy, there(above)), move(occ_energy, there(below))
    keep, give = kernel(pair_tile, [(virt, half)] * 2, [mine, other], [lower, upper], energies)
    whole = (CHIPS, quarter, half)
    tile = kernel(add_tiles, [whole], [], [keep, core_swap(give)])[0]
    row_energy = lax.dynamic_slice_in_dim(virt_energy, chip * quarter, quarter, 0)
    column_energy = lax.dynamic_slice_in_dim(virt_energy, mine, half, 0)
    denominator = (row_energy - (energies[0] + energies[1]))[:, None] + column_energy[None, :]
    amp = shared(kernel(divide, [whole], [], [shared(tile), denominator])[0])
    up, down = kernel(density_parts, [(rows, virt)] * 2, [mine, other], [lower, upper, amp, core_swap(amp)])
    return (move(up, back(below)) + move(down, back(above)))[None]


def solution(mesh):
    cube = Mesh(mesh.devices.reshape(mesh.devices.shape[0], CHIPS, 2), (*PLACES, "core"))
    spec = P("occ", ("z", "core"), None)
    return jax.shard_map(local, mesh=cube, in_specs=(spec, P("occ"), P()), out_specs=spec, check_vma=False)
```

time: 155 us -> 171 us (1.10)
  the two profiles are of different devices: /device:TPU:1 before, /device:TPU:66 now
where the time goes in v7:
time: 171 us
  waiting for transfers between devices  93.4 us (55%)
  starting transfers between devices  56.7 us (33%)
  blocking collectives  10.7 us (6%)
  Pallas kernels  4.62 us (3%)
  local copies, waits for them, and re-layouts  2.03 us (1%)
  between operations  2.01 us (1%)
    ppermute x6, waiting for transfers between devices, move(): return lax.ppermute(x, PLACES, pairs)  85.9 us
    ppermute x6, starting transfers between devices, move(): return lax.ppermute(x, PLACES, pairs)  34.8 us
    all_to_all x1, starting transfers between devices, shared(): return lax.all_to_all(x, PLACES, 0, 0, axis_index_groups=groups, tiled=True)  18 us
    all_to_all x1, blocking collectives, shared(): return lax.all_to_all(x, PLACES, 0, 0, axis_index_groups=groups, tiled=True)  10.7 us
    pallas_call x4, Pallas kernels, kernel(): pl.pallas_call(run, out_shape=[jax.ShapeDtypeStruct(s, jnp.float32) for s...  4.62 us
    ppermute x2, starting transfers between devices, core_swap(): return lax.ppermute(x, 'core', [(0, 1), (1, 0)])  3.83 us
    all_to_all x1, waiting for transfers between devices, shared(): return lax.all_to_all(x, PLACES, 0, 0, axis_index_groups=groups, tiled=True)  3.76 us
    ppermute x2, waiting for transfers between devices, core_swap(): return lax.ppermute(x, 'core', [(0, 1), (1, 0)])  3.75 us
  transfers between devices with their start and end apart: 9, of which 7 were waited for; matrix products, arithmetic and copies ran while one was open for 1% of the time, Pallas kernels for 0%

profile of v7, /device:TPU:66, one launch (start us, length us, event | category | flops | bytes accessed | tf_op | source)
XLA Modules:
  0.0 170.6 jit_solution(18424665691889445192)
XLA Ops:
  0.0 16.5 %collective-permute-start.1 = (f32[384,512]{1,0:T(8,128)}, f32[384,512]{1,0:T(8,128)S(1)}, u32[]{:S(2)}, u32[]{:S(2)}) collective-permute-start(f32[384,512]{1,0:T(8,128)} %bitcast.7), channel_id=1, source_target_pairs={{0,552},{2,744},{4,554},{6,746},{8,4},{10,196},{12,6},{14,198},{16... | collective-permute-start | bytes 2359304 | tf_op jit(solution)/shard_map/ppermute | solution.py:45
  16.5 1.9 %collective-permute-start = (f32[384,512]{1,0:T(8,128)}, f32[384,512]{1,0:T(8,128)S(1)}, u32[]{:S(2)}, u32[]{:S(2)}) collective-permute-start(f32[384,512]{1,0:T(8,128)} %bitcast.8), channel_id=1, source_target_pairs={{0,4},{2,196},{4,6},{6,198},{8,204},{10,12},{12,206},{14,14},{16,2... | collective-permute-start | bytes 2359304 | tf_op jit(solution)/shard_map/ppermute | solution.py:45
  18.5 4.8 %collective-permute-start.3 = (f32[1]{0:T(128)}, f32[1]{0:T(128)}, u32[]{:S(2)}, u32[]{:S(2)}) collective-permute-start(f32[1]{0:T(128)} %param.5), channel_id=1, source_target_pairs={{0,552},{2,744},{4,554},{6,746},{8,4},{10,196},{12,6},{14,198},{16... | collective-permute-start | bytes 20 | tf_op jit(solution)/shard_map/ppermute | solution.py:45
  23.3 1.9 %collective-permute-start.2 = (f32[1]{0:T(128)}, f32[1]{0:T(128)}, u32[]{:S(2)}, u32[]{:S(2)}) collective-permute-start(f32[1]{0:T(128)} %param.5), channel_id=1, source_target_pairs={{0,4},{2,196},{4,6},{6,198},{8,204},{10,12},{12,206},{14,14},{16,2... | collective-permute-start | bytes 20 | tf_op jit(solution)/shard_map/ppermute | solution.py:45
  25.2 42.2 %collective-permute-done.3.refs_5_ = f32[1]{0:T(128)} collective-permute-done((f32[1]{0:T(128)}, f32[1]{0:T(128)}, u32[]{:S(2)}, u32[]{:S(2)}) %collective-permute-start.3) | collective-permute-done | bytes 36 | tf_op jit(solution)/shard_map/ppermute | solution.py:45
  67.4 2.9 %collective-permute-done.2.refs_4_ = f32[1]{0:T(128)} collective-permute-done((f32[1]{0:T(128)}, f32[1]{0:T(128)}, u32[]{:S(2)}, u32[]{:S(2)}) %collective-permute-start.2) | collective-permute-done | bytes 36 | tf_op jit(solution)/shard_map/ppermute | solution.py:45
  70.3 2.3 %shard_map.46 = (f32[512,256]{1,0:T(8,128)S(1)}, f32[512,256]{1,0:T(8,128)S(1)}) custom-call(s32[1]{0:T(128)} %bitcast.refs_0_, s32[1]{0:T(128)} %bitcast.1.refs_1_, f32[384,512]{1,0:T(8,128)S(1)} %collective-permute-done.refs_2_, f32[384,512]{1,0:T(8,128)S(1)} %collective-permute-done.1.refs_3_, f32[1]{0:T(128)} %collective-permute-done.2.refs_4_, ...), custom_call_target="tpu_custom_call" | custom-call | tf_op jit(solution)/shard_map/pallas_call | solution.py:58
  72.6 1.9 %collective-permute-start.4 = (f32[512,256]{1,0:T(8,128)S(1)}, f32[512,256]{1,0:T(8,128)S(1)}, u32[]{:S(2)}, u32[]{:S(2)}) collective-permute-start(f32[512,256]{1,0:T(8,128)S(1)} %get-tuple-element.10), channel_id=1, source_target_pairs={{0,1},{1,0},{2,3},{3,2},{4,5},{5,4},{6,7},{7,6},{8,9},{9,8},{10,11... | collective-permute-start | bytes 1572872 | tf_op jit(solution)/shard_map/ppermute | solution.py:49
  74.6 1.9 %collective-permute-done.4.refs_1_ = f32[512,256]{1,0:T(8,128)S(1)} collective-permute-done((f32[512,256]{1,0:T(8,128)S(1)}, f32[512,256]{1,0:T(8,128)S(1)}, u32[]{:S(2)}, u32[]{:S(2)}) %collective-permute-start.4) | collective-permute-done | bytes 524320 | tf_op jit(solution)/shard_map/ppermute | solution.py:49
  76.4 0.8 shard_map.47
  77.3 18.0 %all-to-all-start = ((f32[4,128,256]{2,1,0:T(8,128)}), f32[4,128,256]{2,1,0:T(8,128)S(1)}, u32[]{:S(2)}, u32[]{:S(2)}) async-start(f32[4,128,256]{2,1,0:T(8,128)} %shard_map.47), calls=%async_computation | async-start | bytes 1048576 | tf_op jit(solution)/shard_map/all_to_all | solution.py:128
  95.3 1.3 dynamic_slice.10
  97.3 0.7 copy-done
  99.4 0.1 broadcast_add_fusion.refs_1_
  99.4 3.8 %all-to-all-done.refs_0_ = f32[4,128,256]{2,1,0:T(8,128)S(1)} async-done(((f32[4,128,256]{2,1,0:T(8,128)}), f32[4,128,256]{2,1,0:T(8,128)S(1)}, u32[]{:S(2)}, u32[]{:S(2)}) %all-to-all-start) | async-done | bytes 524320 | tf_op jit(solution)/shard_map/all_to_all | solution.py:128
  103.3 10.7 %all_to_all.10.refs_4_ = f32[4,128,256]{2,1,0:T(8,128)S(1)} all-to-all(f32[4,128,256]{2,1,0:T(8,128)S(1)} %shard_map.48), channel_id=1, replica_groups={{4,196,6,198},{204,12,206,14},{20,212,22,214},{220,28,222,30},{36,228,3..., dimensions={0} | all-to-all | bytes 1048576 | tf_op jit(solution)/shard_map/all_to_all | solution.py:128
  114.0 1.9 %collective-permute-start.5 = (f32[4,128,256]{2,1,0:T(8,128)S(1)}, f32[4,128,256]{2,1,0:T(8,128)S(1)}, u32[]{:S(2)}, u32[]{:S(2)}) collective-permute-start(f32[4,128,256]{2,1,0:T(8,128)S(1)} %all_to_all.10.refs_4_), channel_id=1, source_target_pairs={{0,1},{1,0},{2,3},{3,2},{4,5},{5,4},{6,7},{7,6},{8,9},{9,8},{10,11... | collective-permute-start | bytes 1572872 | tf_op jit(solution)/shard_map/ppermute | solution.py:49
  115.9 1.9 %collective-permute-done.5.refs_5_ = f32[4,128,256]{2,1,0:T(8,128)S(1)} collective-permute-done((f32[4,128,256]{2,1,0:T(8,128)S(1)}, f32[4,128,256]{2,1,0:T(8,128)S(1)}, u32[]{:S(2)}, u32[]{:S(2)}) %collective-permute-start.5) | collective-permute-done | bytes 524320 | tf_op jit(solution)/shard_map/ppermute | solution.py:49
  117.7 1.4 shard_map.49
  119.2 1.9 %collective-permute-start.6 = (f32[384,512]{1,0:T(8,128)S(1)}, f32[384,512]{1,0:T(8,128)S(1)}, u32[]{:S(2)}, u32[]{:S(2)}) collective-permute-start(f32[384,512]{1,0:T(8,128)S(1)} %get-tuple-element.11), channel_id=1, source_target_pairs={{552,0},{744,2},{554,4},{746,6},{4,8},{196,10},{6,12},{198,14},{20... | collective-permute-start | bytes 2359304 | tf_op jit(solution)/shard_map/ppermute | solution.py:45
  121.1 7.7 %collective-permute-start.7 = (f32[384,512]{1,0:T(8,128)S(1)}, f32[384,512]{1,0:T(8,128)S(1)}, u32[]{:S(2)}, u32[]{:S(2)}) collective-permute-start(f32[384,512]{1,0:T(8,128)S(1)} %get-tuple-element.12), channel_id=1, source_target_pairs={{4,0},{196,2},{6,4},{198,6},{204,8},{12,10},{206,12},{14,14},{20,1... | collective-permute-start | bytes 2359304 | tf_op jit(solution)/shard_map/ppermute | solution.py:45
  128.9 39.6 %collective-permute-done.6 = f32[384,512]{1,0:T(8,128)S(1)} collective-permute-done((f32[384,512]{1,0:T(8,128)S(1)}, f32[384,512]{1,0:T(8,128)S(1)}, u32[]{:S(2)}, u32[]{:S(2)}) %collective-permute-start.6) | collective-permute-done | bytes 786464 | tf_op jit(solution)/shard_map/ppermute | solution.py:45
  168.4 1.2 collective-permute-done.7
  169.6 1.0 add_bitcast_fusion
  (6 shorter events, 0.2 us)
Async XLA Ops:
  0.0 70.3 %collective-permute-start.1 = (f32[384,512]{1,0:T(8,128)}, f32[384,512]{1,0:T(8,128)S(1)}, u32[]{:S(2)}, u32[]{:S(2)}) collective-permute-start(f32[384,512]{1,0:T(8,128)} %bitcast.7), channel_id=1, source_target_pairs={{0,552},{2,744},{4,554},{6,746},{8,4},{10,196},{12,6},{14,198},{16... | collective-permute-start | bytes 2359304 | tf_op jit(solution)/shard_map/ppermute | solution.py:45
  16.5 53.8 %collective-permute-start = (f32[384,512]{1,0:T(8,128)}, f32[384,512]{1,0:T(8,128)S(1)}, u32[]{:S(2)}, u32[]{:S(2)}) collective-permute-start(f32[384,512]{1,0:T(8,128)} %bitcast.8), channel_id=1, source_target_pairs={{0,4},{2,196},{4,6},{6,198},{8,204},{10,12},{12,206},{14,14},{16,2... | collective-permute-start | bytes 2359304 | tf_op jit(solution)/shard_map/ppermute | solution.py:45
  18.5 48.9 %collective-permute-start.3 = (f32[1]{0:T(128)}, f32[1]{0:T(128)}, u32[]{:S(2)}, u32[]{:S(2)}) collective-permute-start(f32[1]{0:T(128)} %param.5), channel_id=1, source_target_pairs={{0,552},{2,744},{4,554},{6,746},{8,4},{10,196},{12,6},{14,198},{16... | collective-permute-start | bytes 20 | tf_op jit(solution)/shard_map/ppermute | solution.py:45
  23.3 47.1 %collective-permute-start.2 = (f32[1]{0:T(128)}, f32[1]{0:T(128)}, u32[]{:S(2)}, u32[]{:S(2)}) collective-permute-start(f32[1]{0:T(128)} %param.5), channel_id=1, source_target_pairs={{0,4},{2,196},{4,6},{6,198},{8,204},{10,12},{12,206},{14,14},{16,2... | collective-permute-start | bytes 20 | tf_op jit(solution)/shard_map/ppermute | solution.py:45
  72.6 3.8 %collective-permute-start.4 = (f32[512,256]{1,0:T(8,128)S(1)}, f32[512,256]{1,0:T(8,128)S(1)}, u32[]{:S(2)}, u32[]{:S(2)}) collective-permute-start(f32[512,256]{1,0:T(8,128)S(1)} %get-tuple-element.10), channel_id=1, source_target_pairs={{0,1},{1,0},{2,3},{3,2},{4,5},{5,4},{6,7},{7,6},{8,9},{9,8},{10,11... | collective-permute-start | bytes 1572872 | tf_op jit(solution)/shard_map/ppermute | solution.py:49
  77.3 25.9 %all-to-all-start = ((f32[4,128,256]{2,1,0:T(8,128)}), f32[4,128,256]{2,1,0:T(8,128)S(1)}, u32[]{:S(2)}, u32[]{:S(2)}) async-start(f32[4,128,256]{2,1,0:T(8,128)} %shard_map.47), calls=%async_computation | async-start | bytes 1048576 | tf_op jit(solution)/shard_map/all_to_all | solution.py:128
  97.3 0.7 copy-start
  114.0 3.8 %collective-permute-start.5 = (f32[4,128,256]{2,1,0:T(8,128)S(1)}, f32[4,128,256]{2,1,0:T(8,128)S(1)}, u32[]{:S(2)}, u32[]{:S(2)}) collective-permute-start(f32[4,128,256]{2,1,0:T(8,128)S(1)} %all_to_all.10.refs_4_), channel_id=1, source_target_pairs={{0,1},{1,0},{2,3},{3,2},{4,5},{5,4},{6,7},{7,6},{8,9},{9,8},{10,11... | collective-permute-start | bytes 1572872 | tf_op jit(solution)/shard_map/ppermute | solution.py:49
  119.2 49.2 %collective-permute-start.6 = (f32[384,512]{1,0:T(8,128)S(1)}, f32[384,512]{1,0:T(8,128)S(1)}, u32[]{:S(2)}, u32[]{:S(2)}) collective-permute-start(f32[384,512]{1,0:T(8,128)S(1)} %get-tuple-element.11), channel_id=1, source_target_pairs={{552,0},{744,2},{554,4},{746,6},{4,8},{196,10},{6,12},{198,14},{20... | collective-permute-start | bytes 2359304 | tf_op jit(solution)/shard_map/ppermute | solution.py:45
  121.1 48.5 %collective-permute-start.7 = (f32[384,512]{1,0:T(8,128)S(1)}, f32[384,512]{1,0:T(8,128)S(1)}, u32[]{:S(2)}, u32[]{:S(2)}) collective-permute-start(f32[384,512]{1,0:T(8,128)S(1)} %get-tuple-element.12), channel_id=1, source_target_pairs={{4,0},{196,2},{6,4},{198,6},{204,8},{12,10},{206,12},{14,14},{20,1... | collective-permute-start | bytes 2359304 | tf_op jit(solution)/shard_map/ppermute | solution.py:45

commit v8 on v7

v8 whole, which is shorter than its diff:
```python
import jax
import jax.numpy as jnp
from jax import lax
from jax.experimental import pallas as pl
from jax.experimental.pallas import tpu as pltpu
from jax.sharding import Mesh, PartitionSpec as P

CHIPS = 4
PLACES = ("occ", "z")
SMEM = pl.BlockSpec(memory_space=pltpu.SMEM)
VMEM = pl.BlockSpec(memory_space=pltpu.VMEM)
ANY = pl.BlockSpec(memory_space=pl.ANY)


def neighbours(occupied):
    goals, groups = [], []
    for i in range(occupied):
        for z in range(CHIPS):
            goals.append((i + (1 if z < CHIPS // 2 else -1)) % occupied * CHIPS + z)
        groups.append([(i if z < CHIPS // 2 else (i - 1) % occupied) * CHIPS + z for z in range(CHIPS)])
    return goals, groups


def move(x, goals):
    return lax.ppermute(x, PLACES, list(enumerate(goals)))


def move_back(x, goals):
    return lax.ppermute(x, PLACES, [(goal, place) for place, goal in enumerate(goals)])


def core_swap(x):
    return lax.ppermute(x, "core", [(0, 1), (1, 0)])


def kernel(body, shapes, scalars, arrays, after=()):
    used = len(scalars) + len(arrays)

    def run(*refs):
        body(*refs[:used], *refs[used + len(after) :])

    return pl.pallas_call(
        run,
        out_shape=[jax.ShapeDtypeStruct(s, jnp.float32) for s in shapes],
        in_specs=[SMEM] * len(scalars) + [VMEM] * len(arrays) + [ANY] * len(after),
        out_specs=[VMEM] * len(shapes),
        compiler_params=pltpu.CompilerParams(vmem_limit_bytes=24 * 2**20),
    )(*[s.reshape(1) for s in scalars], *arrays, *after)


def split(x):
    high = x.astype(jnp.bfloat16)
    return high, (x - high.astype(jnp.float32)).astype(jnp.bfloat16)


def dot(x, y, dims):
    def one(u, v):
        return lax.dot_general(u, v, (dims, ((), ())), preferred_element_type=jnp.float32)

    return one(x[0], y[0]) + (one(x[0], y[1]) + one(x[1], y[0]))


def block(start_ref, width):
    return pl.ds(pl.multiple_of(start_ref[0], width), width)


def by_half(chip_ref, lower_half, upper_half):
    low = chip_ref[0] < CHIPS // 2
    pl.when(low)(lower_half)
    pl.when(jnp.logical_not(low))(upper_half)


def pair_tile(chip_ref, mine_ref, other_ref, own_ref, got_ref, keep_ref, give_ref):
    def body(lower_ref, upper_ref):
        upper = split(upper_ref[...])
        for start_ref, out_ref in ((other_ref, give_ref), (mine_ref, keep_ref)):
            out_ref[...] = dot(upper, split(lower_ref[:, block(start_ref, out_ref.shape[1])]), ((0,), (0,)))

    by_half(chip_ref, lambda: body(got_ref, own_ref), lambda: body(own_ref, got_ref))


def add_tiles(keep_ref, got_ref, out_ref):
    out_ref[...] = (keep_ref[...] + got_ref[...]).reshape(out_ref.shape)


def divide(parts_ref, denominator_ref, out_ref):
    total = (parts_ref[0] + parts_ref[1]) + (parts_ref[2] + parts_ref[3])
    amplitude = total / denominator_ref[...]
    for k in range(CHIPS):
        out_ref[k] = amplitude


def times_upper(mine_ref, other_ref, lower_ref, amp_ref, swapped_ref, out_ref):
    virt, width = lower_ref.shape[1], amp_ref.shape[2]
    total = None
    for start_ref, half_ref in ((mine_ref, amp_ref), (other_ref, swapped_ref)):
        amp = split(half_ref[...].reshape(virt, width))
        part = dot(split(lower_ref[:, block(start_ref, width)]), amp, ((1,), (1,)))
        total = part if total is None else total + part
    out_ref[...] = total


def times_lower(mine_ref, other_ref, upper_ref, amp_ref, swapped_ref, out_ref):
    virt, width = upper_ref.shape[1], amp_ref.shape[2]
    upper = split(upper_ref[...])
    for start_ref, half_ref in ((mine_ref, amp_ref), (other_ref, swapped_ref)):
        amp = split(half_ref[...].reshape(virt, width))
        out_ref[:, block(start_ref, width)] = dot(upper, amp, ((1,), (0,)))


def part_away(chip_ref, mine_ref, other_ref, own_ref, amp_ref, swapped_ref, out_ref):
    rest = (mine_ref, other_ref, own_ref, amp_ref, swapped_ref, out_ref)
    by_half(chip_ref, lambda: times_lower(*rest), lambda: times_upper(*rest))


def part_here(chip_ref, mine_ref, other_ref, got_ref, amp_ref, swapped_ref, out_ref):
    rest = (mine_ref, other_ref, got_ref, amp_ref, swapped_ref, out_ref)
    by_half(chip_ref, lambda: times_upper(*rest), lambda: times_lower(*rest))


def local(factors, occ_energy, virt_energy):
    own = factors[0]
    rows, virt = own.shape
    half, quarter = virt // 2, virt // CHIPS
    goals, groups = neighbours(lax.axis_size("occ"))
    mine = lax.axis_index("core") * half
    other = half - mine
    chip = lax.axis_index("z")
    at = [chip, mine, other]

    def shared(x):
        return lax.all_to_all(x, PLACES, 0, 0, axis_index_groups=groups, tiled=True)

    got = move(own, goals)
    got_energy = move(jnp.broadcast_to(occ_energy, (8, 128)), goals)
    keep, give = kernel(pair_tile, [(virt, half)] * 2, at, [own, got], [got_energy])
    whole = (CHIPS, quarter, half)
    tile = kernel(add_tiles, [whole], [], [keep, core_swap(give)])[0]
    row_energy = lax.dynamic_slice_in_dim(virt_energy, chip * quarter, quarter, 0)
    column_energy = lax.dynamic_slice_in_dim(virt_energy, mine, half, 0)
    denominator = (row_energy - (occ_energy + got_energy[0, 0]))[:, None] + column_energy[None, :]
    amp = shared(kernel(divide, [whole], [], [shared(tile), denominator])[0])
    swapped = core_swap(amp)
    away = kernel(part_away, [(rows, virt)], at, [own, amp, swapped])[0]
    here = kernel(part_here, [(rows, virt)], at, [got, amp, swapped], [away])[0]
    return (here + move_back(away, goals))[None]


def solution(mesh):
    cube = Mesh(mesh.devices.reshape(mesh.devices.shape[0], CHIPS, 2), (*PLACES, "core"))
    spec = P("occ", ("z", "core"), None)
    return jax.shard_map(local, mesh=cube, in_specs=(spec, P("occ"), P()), out_specs=spec, check_vma=False)
```

time: 171 us -> 159 us (0.930)
  the two profiles are of different devices: /device:TPU:66 before, /device:TPU:64 now
where the time goes in v8:
time: 159 us
  waiting for transfers between devices  93.1 us (59%)
  starting transfers between devices  36 us (23%)
  blocking collectives  20.8 us (13%)
  Pallas kernels  3.62 us (2%)
  local copies, waits for them, and re-layouts  2.44 us (2%)
    ppermute x1, waiting for transfers between devices, move_back(): lax.ppermute(x, PLACES, [(goal, place) for place, goal in enumerate(goals)])  38.3 us
    ppermute x2, waiting for transfers between devices, move(): return lax.ppermute(x, PLACES, list(enumerate(goals)))  34.3 us
    all_to_all x1, blocking collectives, shared(): return lax.all_to_all(x, PLACES, 0, 0, axis_index_groups=groups, tiled=True)  20.8 us
    ppermute x2, starting transfers between devices, move(): return lax.ppermute(x, PLACES, list(enumerate(goals)))  18.5 us
    all_to_all x1, waiting for transfers between devices, shared(): return lax.all_to_all(x, PLACES, 0, 0, axis_index_groups=groups, tiled=True)  16.8 us
    all_to_all x1, starting transfers between devices, shared(): return lax.all_to_all(x, PLACES, 0, 0, axis_index_groups=groups, tiled=True)  11.7 us
    ppermute x2, starting transfers between devices, core_swap(): return lax.ppermute(x, 'core', [(0, 1), (1, 0)])  3.86 us
    ppermute x2, waiting for transfers between devices, core_swap(): return lax.ppermute(x, 'core', [(0, 1), (1, 0)])  3.72 us
  transfers between devices with their start and end apart: 6, of which 5 were waited for; matrix products, arithmetic and copies ran while one was open for 0% of the time, Pallas kernels for 1%

profile of v8, /device:TPU:64, one launch (start us, length us, event | category | flops | bytes accessed | tf_op | source)
XLA Modules:
  0.0 158.6 jit_solution(17147890476711186705)
XLA Ops:
  0.0 10.9 %collective-permute-start = (f32[384,512]{1,0:T(8,128)}, f32[384,512]{1,0:T(8,128)S(1)}, u32[]{:S(2)}, u32[]{:S(2)}) collective-permute-start(f32[384,512]{1,0:T(8,128)} %bitcast.10), channel_id=1, source_target_pairs={{0,8},{2,10},{4,764},{6,766},{8,16},{10,18},{12,4},{14,6},{16,24},... | collective-permute-start | bytes 2359304 | tf_op jit(solution)/shard_map/ppermute | solution.py:25
  11.6 7.6 %collective-permute-start.1 = (f32[8,128]{1,0:T(8,128)S(1)}, f32[8,128]{1,0:T(8,128)S(1)}, u32[]{:S(2)}, u32[]{:S(2)}) collective-permute-start(f32[8,128]{1,0:T(8,128)S(1)} %broadcast_in_dim.4), channel_id=1, source_target_pairs={{0,8},{2,10},{4,764},{6,766},{8,16},{10,18},{12,4},{14,6},{16,24},... | collective-permute-start | bytes 12296 | tf_op jit(solution)/shard_map/ppermute | solution.py:25
  19.2 34.3 %collective-permute-done.1.refs_5_ = f32[8,128]{1,0:T(8,128)S(1)} collective-permute-done((f32[8,128]{1,0:T(8,128)S(1)}, f32[8,128]{1,0:T(8,128)S(1)}, u32[]{:S(2)}, u32[]{:S(2)}) %collective-permute-start.1) | collective-permute-done | bytes 4128 | tf_op jit(solution)/shard_map/ppermute | solution.py:25
  53.5 1.1 copy-done
  54.6 1.1 shard_map.40
  55.7 2.0 %collective-permute-start.2 = (f32[512,256]{1,0:T(8,128)S(1)}, f32[512,256]{1,0:T(8,128)S(1)}, u32[]{:S(2)}, u32[]{:S(2)}) collective-permute-start(f32[512,256]{1,0:T(8,128)S(1)} %get-tuple-element.8), channel_id=1, source_target_pairs={{0,1},{1,0},{2,3},{3,2},{4,5},{5,4},{6,7},{7,6},{8,9},{9,8},{10,11... | collective-permute-start | bytes 1572872 | tf_op jit(solution)/shard_map/ppermute | solution.py:33
  57.7 1.8 %collective-permute-done.2.refs_1_ = f32[512,256]{1,0:T(8,128)S(1)} collective-permute-done((f32[512,256]{1,0:T(8,128)S(1)}, f32[512,256]{1,0:T(8,128)S(1)}, u32[]{:S(2)}, u32[]{:S(2)}) %collective-permute-start.2) | collective-permute-done | bytes 524320 | tf_op jit(solution)/shard_map/ppermute | solution.py:33
  59.5 0.8 shard_map.41
  60.4 11.7 %all-to-all-start = ((f32[4,128,256]{2,1,0:T(8,128)}), f32[4,128,256]{2,1,0:T(8,128)S(1)}, u32[]{:S(2)}, u32[]{:S(2)}) async-start(f32[4,128,256]{2,1,0:T(8,128)} %shard_map.41), calls=%async_computation | async-start | bytes 1048576 | tf_op jit(solution)/shard_map/all_to_all | solution.py:132
  72.1 0.7 copy-done.2
  72.8 0.1 dynamic_slice.7
  72.9 0.5 slice.3
  74.0 0.1 dynamic-slice_subtract_fusion
  74.1 0.1 broadcast_add_fusion.refs_1_
  74.2 16.8 %all-to-all-done.refs_0_ = f32[4,128,256]{2,1,0:T(8,128)S(1)} async-done(((f32[4,128,256]{2,1,0:T(8,128)}), f32[4,128,256]{2,1,0:T(8,128)S(1)}, u32[]{:S(2)}, u32[]{:S(2)}) %all-to-all-start) | async-done | bytes 524320 | tf_op jit(solution)/shard_map/all_to_all | solution.py:132
  91.0 0.0 copy-start.1
  91.0 20.8 %all_to_all.10.refs_4_ = f32[4,128,256]{2,1,0:T(8,128)S(1)} all-to-all(f32[4,128,256]{2,1,0:T(8,128)S(1)} %shard_map.42), channel_id=1, replica_groups={{0,2,764,766},{8,10,4,6},{16,18,12,14},{24,26,20,22},{32,34,28,30},{40,..., dimensions={0} | all-to-all | bytes 1048576 | tf_op jit(solution)/shard_map/all_to_all | solution.py:132
  111.8 1.9 %collective-permute-start.3 = (f32[4,128,256]{2,1,0:T(8,128)S(1)}, f32[4,128,256]{2,1,0:T(8,128)S(1)}, u32[]{:S(2)}, u32[]{:S(2)}) collective-permute-start(f32[4,128,256]{2,1,0:T(8,128)S(1)} %all_to_all.10.refs_4_), channel_id=1, source_target_pairs={{0,1},{1,0},{2,3},{3,2},{4,5},{5,4},{6,7},{7,6},{8,9},{9,8},{10,11... | collective-permute-start | bytes 1572872 | tf_op jit(solution)/shard_map/ppermute | solution.py:33
  113.7 1.9 %collective-permute-done.3.refs_5_ = f32[4,128,256]{2,1,0:T(8,128)S(1)} collective-permute-done((f32[4,128,256]{2,1,0:T(8,128)S(1)}, f32[4,128,256]{2,1,0:T(8,128)S(1)}, u32[]{:S(2)}, u32[]{:S(2)}) %collective-permute-start.3) | collective-permute-done | bytes 524320 | tf_op jit(solution)/shard_map/ppermute | solution.py:33
  115.6 0.8 shard_map.43.refs_6_
  116.4 1.9 %collective-permute-start.4 = (f32[384,512]{1,0:T(8,128)S(1)}, f32[384,512]{1,0:T(8,128)S(1)}, u32[]{:S(2)}, u32[]{:S(2)}) collective-permute-start(f32[384,512]{1,0:T(8,128)S(1)} %shard_map.43.refs_6_), channel_id=1, source_target_pairs={{8,0},{10,2},{764,4},{766,6},{16,8},{18,10},{4,12},{6,14},{24,16},... | collective-permute-start | bytes 2359304 | tf_op jit(solution)/shard_map/ppermute | solution.py:29
  118.4 0.8 shard_map.44
  119.2 38.3 %collective-permute-done.4 = f32[384,512]{1,0:T(8,128)S(1)} collective-permute-done((f32[384,512]{1,0:T(8,128)S(1)}, f32[384,512]{1,0:T(8,128)S(1)}, u32[]{:S(2)}, u32[]{:S(2)}) %collective-permute-start.4) | collective-permute-done | bytes 786464 | tf_op jit(solution)/shard_map/ppermute | solution.py:29
  157.6 1.0 add_bitcast_fusion
  (6 shorter events, 0.1 us)
Async XLA Ops:
  0.0 53.5 %collective-permute-start = (f32[384,512]{1,0:T(8,128)}, f32[384,512]{1,0:T(8,128)S(1)}, u32[]{:S(2)}, u32[]{:S(2)}) collective-permute-start(f32[384,512]{1,0:T(8,128)} %bitcast.10), channel_id=1, source_target_pairs={{0,8},{2,10},{4,764},{6,766},{8,16},{10,18},{12,4},{14,6},{16,24},... | collective-permute-start | bytes 2359304 | tf_op jit(solution)/shard_map/ppermute | solution.py:25
  11.6 41.9 %collective-permute-start.1 = (f32[8,128]{1,0:T(8,128)S(1)}, f32[8,128]{1,0:T(8,128)S(1)}, u32[]{:S(2)}, u32[]{:S(2)}) collective-permute-start(f32[8,128]{1,0:T(8,128)S(1)} %broadcast_in_dim.4), channel_id=1, source_target_pairs={{0,8},{2,10},{4,764},{6,766},{8,16},{10,18},{12,4},{14,6},{16,24},... | collective-permute-start | bytes 12296 | tf_op jit(solution)/shard_map/ppermute | solution.py:25
  53.5 1.1 copy-start
  55.7 3.8 %collective-permute-start.2 = (f32[512,256]{1,0:T(8,128)S(1)}, f32[512,256]{1,0:T(8,128)S(1)}, u32[]{:S(2)}, u32[]{:S(2)}) collective-permute-start(f32[512,256]{1,0:T(8,128)S(1)} %get-tuple-element.8), channel_id=1, source_target_pairs={{0,1},{1,0},{2,3},{3,2},{4,5},{5,4},{6,7},{7,6},{8,9},{9,8},{10,11... | collective-permute-start | bytes 1572872 | tf_op jit(solution)/shard_map/ppermute | solution.py:33
  60.4 30.6 %all-to-all-start = ((f32[4,128,256]{2,1,0:T(8,128)}), f32[4,128,256]{2,1,0:T(8,128)S(1)}, u32[]{:S(2)}, u32[]{:S(2)}) async-start(f32[4,128,256]{2,1,0:T(8,128)} %shard_map.41), calls=%async_computation | async-start | bytes 1048576 | tf_op jit(solution)/shard_map/all_to_all | solution.py:132
  72.1 0.7 copy-start.2
  91.0 24.6 %copy-start.1 = (f32[1,384,512]{2,1,0:T(8,128)S(1)}, f32[1,384,512]{2,1,0:T(8,128)}, u32[]{:S(2)}) copy-start(f32[1,384,512]{2,1,0:T(8,128)} %param.3) | copy-start | bytes 2359300
  111.8 3.8 %collective-permute-start.3 = (f32[4,128,256]{2,1,0:T(8,128)S(1)}, f32[4,128,256]{2,1,0:T(8,128)S(1)}, u32[]{:S(2)}, u32[]{:S(2)}) collective-permute-start(f32[4,128,256]{2,1,0:T(8,128)S(1)} %all_to_all.10.refs_4_), channel_id=1, source_target_pairs={{0,1},{1,0},{2,3},{3,2},{4,5},{5,4},{6,7},{7,6},{8,9},{9,8},{10,11... | collective-permute-start | bytes 1572872 | tf_op jit(solution)/shard_map/ppermute | solution.py:33
  116.4 41.1 %collective-permute-start.4 = (f32[384,512]{1,0:T(8,128)S(1)}, f32[384,512]{1,0:T(8,128)S(1)}, u32[]{:S(2)}, u32[]{:S(2)}) collective-permute-start(f32[384,512]{1,0:T(8,128)S(1)} %shard_map.43.refs_6_), channel_id=1, source_target_pairs={{8,0},{10,2},{764,4},{766,6},{16,8},{18,10},{4,12},{6,14},{24,16},... | collective-permute-start | bytes 2359304 | tf_op jit(solution)/shard_map/ppermute | solution.py:29

commit v9 on v7

--- a/solution.py
+++ b/solution.py
@@ -1,6 +1,5 @@
 import jax
 import jax.numpy as jnp
-import numpy as np
 from jax import lax
 from jax.experimental import pallas as pl
 from jax.experimental.pallas import tpu as pltpu
@@ -9,27 +8,20 @@
 CHIPS = 4
 LEVELS = 3
 RING = CHIPS * LEVELS
-ROWS = 8
 PLACES = ("occ", "z")
 SMEM = pl.BlockSpec(memory_space=pltpu.SMEM)
 VMEM = pl.BlockSpec(memory_space=pltpu.VMEM)
 ANY = pl.BlockSpec(memory_space=pl.ANY)
 
 
-def meeting(column, level, chunk):
-    x, y = divmod(column, ROWS)
-    crosses = (chunk + y + level) % 2
-    plane = 2 + 2 * (x % 2) + chunk // 2
-    return ((x ^ crosses) * ROWS + y) * RING + (level * CHIPS + plane) % RING
-
-
 def meetings(occupied):
     above, below, groups = [0] * (occupied * CHIPS), [0] * (occupied * CHIPS), []
     for i in range(occupied):
-        groups.append([meeting(*divmod(i, LEVELS), chunk) for chunk in range(CHIPS)])
-        for chunk, goal in enumerate(groups[-1]):
-            above[i * CHIPS + chunk] = goal
-            below[(i + 1) % occupied * CHIPS + chunk] = goal
+        column, level = divmod(i, LEVELS)
+        groups.append([column * RING + (level * CHIPS + c + CHIPS // 2) % RING for c in range(CHIPS)])
+        for c, goal in enumerate(groups[-1]):
+            above[i * CHIPS + c] = goal
+            below[(i + 1) % occupied * CHIPS + c] = goal
     return above, below, groups
 
 
@@ -80,11 +72,9 @@
     return pl.ds(pl.multiple_of(start_ref[0], width), width)
 
 
-def pair_tile(mine_ref, other_ref, lower_ref, upper_ref, keep_ref, give_ref):
-    width = keep_ref.shape[1]
-    upper = split(upper_ref[...])
-    for start_ref, out_ref in ((other_ref, give_ref), (mine_ref, keep_ref)):
-        out_ref[...] = dot(upper, split(lower_ref[:, block(start_ref, width)]), ((0,), (0,)))
+def pair_tile(start_ref, lower_ref, upper_ref, out_ref):
+    lower = split(lower_ref[:, block(start_ref, out_ref.shape[1])])
+    out_ref[...] = dot(split(upper_ref[...]), lower, ((0,), (0,)))
 
 
 def add_tiles(keep_ref, got_ref, out_ref):
@@ -118,25 +108,26 @@
     half, quarter = virt // 2, virt // CHIPS
     occupied = lax.axis_size("occ")
     above, below, groups = meetings(occupied)
-    order = np.argsort(np.ravel(groups)) % CHIPS
     mine = lax.axis_index("core") * half
     other = half - mine
-    place = lax.axis_index("occ") * CHIPS + lax.axis_index("z")
-    chip = lax.dynamic_index_in_dim(jnp.asarray(order, jnp.int32), place, keepdims=False)
+    chip = lax.rem(lax.axis_index("z") + CHIPS // 2, CHIPS)
 
     def shared(x):
         return lax.all_to_all(x, PLACES, 0, 0, axis_index_groups=groups, tiled=True)
 
     lower, upper = move(own, there(above)), move(own, there(below))
-    energies = move(occ_energy, there(above)), move(occ_energy, there(below))
-    keep, give = kernel(pair_tile, [(virt, half)] * 2, [mine, other], [lower, upper], energies)
+    energy = jnp.broadcast_to(occ_energy, (8, 128))
+    energies = move(energy, there(above)), move(energy, there(below))
+    give = kernel(pair_tile, [(virt, half)], [other], [lower, upper], energies)[0]
+    keep = kernel(pair_tile, [(virt, half)], [mine], [lower, upper], [give])[0]
     whole = (CHIPS, quarter, half)
     tile = kernel(add_tiles, [whole], [], [keep, core_swap(give)])[0]
     row_energy = lax.dynamic_slice_in_dim(virt_energy, chip * quarter, quarter, 0)
     column_energy = lax.dynamic_slice_in_dim(virt_energy, mine, half, 0)
-    denominator = (row_energy - (energies[0] + energies[1]))[:, None] + column_energy[None, :]
+    denominator = (row_energy - (energies[0][0, 0] + energies[1][0, 0]))[:, None] + column_energy[None, :]
     amp = shared(kernel(divide, [whole], [], [shared(tile), denominator])[0])
-    up, down = kernel(density_parts, [(rows, virt)] * 2, [mine, other], [lower, upper, amp, core_swap(amp)])
+    swapped = core_swap(amp)
+    up, down = kernel(density_parts, [(rows, virt)] * 2, [mine, other], [lower, upper, amp, swapped])
     return (move(up, back(below)) + move(down, back(above)))[None]
 
 

time: 171 us -> 152 us (0.89)
  the two profiles are of different devices: /device:TPU:66 before, /device:TPU:1 now
where the time goes in v9:
time: 152 us; the launch traced here: 151 us
  waiting for transfers between devices  73.7 us (48%)
  starting transfers between devices  50.8 us (33%)
  blocking collectives  18.3 us (12%)
  Pallas kernels  3.58 us (2%)
  between operations  1.96 us (1%)
  local copies, waits for them, and re-layouts  1.82 us (1%)
    ppermute x6, waiting for transfers between devices, move(): return lax.ppermute(x, PLACES, pairs)  63.6 us
    ppermute x6, starting transfers between devices, move(): return lax.ppermute(x, PLACES, pairs)  37.8 us
    all_to_all x1, blocking collectives, shared(): return lax.all_to_all(x, PLACES, 0, 0, axis_index_groups=groups, tiled=True)  18.3 us
    all_to_all x1, waiting for transfers between devices, shared(): return lax.all_to_all(x, PLACES, 0, 0, axis_index_groups=groups, tiled=True)  7.73 us
    ppermute x2, starting transfers between devices, core_swap(): return lax.ppermute(x, 'core', [(0, 1), (1, 0)])  7.23 us
    all_to_all x1, starting transfers between devices, shared(): return lax.all_to_all(x, PLACES, 0, 0, axis_index_groups=groups, tiled=True)  5.82 us
    pallas_call x5, Pallas kernels, kernel(): pl.pallas_call(run, out_shape=[jax.ShapeDtypeStruct(s, jnp.float32) for s...  3.58 us
  transfers between devices with their start and end apart: 9, of which 6 were waited for; matrix products, arithmetic and copies ran while one was open for 1% of the time, Pallas kernels for 0%

profile of v9, /device:TPU:1, one launch (start us, length us, event | category | flops | bytes accessed | tf_op | source)
XLA Modules:
  0.0 151.3 jit_solution(10061331645175268747)
XLA Ops:
  0.0 20.2 %collective-permute-start.1 = (f32[384,512]{1,0:T(8,128)}, f32[384,512]{1,0:T(8,128)S(1)}, u32[]{:S(2)}, u32[]{:S(2)}) collective-permute-start(f32[384,512]{1,0:T(8,128)} %bitcast.8), channel_id=1, source_target_pairs={{0,764},{2,766},{4,744},{6,746},{8,4},{10,6},{12,8},{14,10},{16,12... | collective-permute-start | bytes 2359304 | tf_op jit(solution)/shard_map/ppermute | solution.py:37
  20.2 1.9 %collective-permute-start = (f32[384,512]{1,0:T(8,128)}, f32[384,512]{1,0:T(8,128)S(1)}, u32[]{:S(2)}, u32[]{:S(2)}) collective-permute-start(f32[384,512]{1,0:T(8,128)} %bitcast.9), channel_id=1, source_target_pairs={{0,4},{2,6},{4,8},{6,10},{8,12},{10,14},{12,16},{14,18},{16,20},{1... | collective-permute-start | bytes 2359304 | tf_op jit(solution)/shard_map/ppermute | solution.py:37
  22.8 6.3 %collective-permute-start.3 = (f32[8,128]{1,0:T(8,128)S(1)}, f32[8,128]{1,0:T(8,128)S(1)}, u32[]{:S(2)}, u32[]{:S(2)}) collective-permute-start(f32[8,128]{1,0:T(8,128)S(1)} %broadcast_in_dim.4), channel_id=1, source_target_pairs={{0,764},{2,766},{4,744},{6,746},{8,4},{10,6},{12,8},{14,10},{16,12... | collective-permute-start | bytes 12296 | tf_op jit(solution)/shard_map/ppermute | solution.py:37
  29.1 1.9 %collective-permute-start.2 = (f32[8,128]{1,0:T(8,128)S(1)}, f32[8,128]{1,0:T(8,128)S(1)}, u32[]{:S(2)}, u32[]{:S(2)}) collective-permute-start(f32[8,128]{1,0:T(8,128)S(1)} %broadcast_in_dim.4), channel_id=1, source_target_pairs={{0,4},{2,6},{4,8},{6,10},{8,12},{10,14},{12,16},{14,18},{16,20},{1... | collective-permute-start | bytes 12296 | tf_op jit(solution)/shard_map/ppermute | solution.py:37
  31.0 22.8 %collective-permute-done.3.refs_4_ = f32[8,128]{1,0:T(8,128)S(1)} collective-permute-done((f32[8,128]{1,0:T(8,128)S(1)}, f32[8,128]{1,0:T(8,128)S(1)}, u32[]{:S(2)}, u32[]{:S(2)}) %collective-permute-start.3) | collective-permute-done | bytes 4128 | tf_op jit(solution)/shard_map/ppermute | solution.py:37
  53.8 5.7 %collective-permute-done.2.refs_3_ = f32[8,128]{1,0:T(8,128)S(1)} collective-permute-done((f32[8,128]{1,0:T(8,128)S(1)}, f32[8,128]{1,0:T(8,128)S(1)}, u32[]{:S(2)}, u32[]{:S(2)}) %collective-permute-start.2) | collective-permute-done | bytes 4128 | tf_op jit(solution)/shard_map/ppermute | solution.py:37
  59.5 0.6 shard_map.40.refs_3_
  60.1 3.8 %collective-permute-start.4 = (f32[512,256]{1,0:T(8,128)S(1)}, f32[512,256]{1,0:T(8,128)S(1)}, u32[]{:S(2)}, u32[]{:S(2)}) collective-permute-start(f32[512,256]{1,0:T(8,128)S(1)} %shard_map.40.refs_3_), channel_id=1, source_target_pairs={{0,1},{1,0},{2,3},{3,2},{4,5},{5,4},{6,7},{7,6},{8,9},{9,8},{10,11... | collective-permute-start | bytes 1572872 | tf_op jit(solution)/shard_map/ppermute | solution.py:41
  63.9 0.6 shard_map.41.refs_0_
  64.6 0.9 collective-permute-done.4.refs_1_
  65.5 0.8 shard_map.42
  66.3 5.8 %all-to-all-start = ((f32[4,128,256]{2,1,0:T(8,128)}), f32[4,128,256]{2,1,0:T(8,128)S(1)}, u32[]{:S(2)}, u32[]{:S(2)}) async-start(f32[4,128,256]{2,1,0:T(8,128)} %shard_map.42), calls=%async_computation | async-start | bytes 1048576 | tf_op jit(solution)/shard_map/all_to_all | solution.py:116
  72.1 0.7 copy-done
  72.9 0.5 slice.7
  73.4 0.5 slice.6
  75.3 7.7 %all-to-all-done.refs_0_ = f32[4,128,256]{2,1,0:T(8,128)S(1)} async-done(((f32[4,128,256]{2,1,0:T(8,128)}), f32[4,128,256]{2,1,0:T(8,128)S(1)}, u32[]{:S(2)}, u32[]{:S(2)}) %all-to-all-start) | async-done | bytes 524320 | tf_op jit(solution)/shard_map/all_to_all | solution.py:116
  83.1 18.3 %all_to_all.10.refs_4_ = f32[4,128,256]{2,1,0:T(8,128)S(1)} all-to-all(f32[4,128,256]{2,1,0:T(8,128)S(1)} %shard_map.43), channel_id=1, replica_groups={{4,6,8,10},{12,14,16,18},{20,22,0,2},{28,30,32,34},{36,38,40,42},{44,46..., dimensions={0} | all-to-all | bytes 1048576 | tf_op jit(solution)/shard_map/all_to_all | solution.py:116
  101.3 3.4 %collective-permute-start.5 = (f32[4,128,256]{2,1,0:T(8,128)S(1)}, f32[4,128,256]{2,1,0:T(8,128)S(1)}, u32[]{:S(2)}, u32[]{:S(2)}) collective-permute-start(f32[4,128,256]{2,1,0:T(8,128)S(1)} %all_to_all.10.refs_4_), channel_id=1, source_target_pairs={{0,1},{1,0},{2,3},{3,2},{4,5},{5,4},{6,7},{7,6},{8,9},{9,8},{10,11... | collective-permute-start | bytes 1572872 | tf_op jit(solution)/shard_map/ppermute | solution.py:41
  104.7 1.5 %collective-permute-done.5.refs_5_ = f32[4,128,256]{2,1,0:T(8,128)S(1)} collective-permute-done((f32[4,128,256]{2,1,0:T(8,128)S(1)}, f32[4,128,256]{2,1,0:T(8,128)S(1)}, u32[]{:S(2)}, u32[]{:S(2)}) %collective-permute-start.5) | collective-permute-done | bytes 524320 | tf_op jit(solution)/shard_map/ppermute | solution.py:41
  106.3 1.4 shard_map.44
  107.7 1.9 %collective-permute-start.6 = (f32[384,512]{1,0:T(8,128)S(1)}, f32[384,512]{1,0:T(8,128)S(1)}, u32[]{:S(2)}, u32[]{:S(2)}) collective-permute-start(f32[384,512]{1,0:T(8,128)S(1)} %get-tuple-element.7), channel_id=1, source_target_pairs={{764,0},{766,2},{744,4},{746,6},{4,8},{6,10},{8,12},{10,14},{12,16... | collective-permute-start | bytes 2359304 | tf_op jit(solution)/shard_map/ppermute | solution.py:37
  109.6 5.6 %collective-permute-start.7 = (f32[384,512]{1,0:T(8,128)S(1)}, f32[384,512]{1,0:T(8,128)S(1)}, u32[]{:S(2)}, u32[]{:S(2)}) collective-permute-start(f32[384,512]{1,0:T(8,128)S(1)} %get-tuple-element.8), channel_id=1, source_target_pairs={{4,0},{6,2},{8,4},{10,6},{12,8},{14,10},{16,12},{18,14},{20,16},{2... | collective-permute-start | bytes 2359304 | tf_op jit(solution)/shard_map/ppermute | solution.py:37
  115.2 35.1 %collective-permute-done.6 = f32[384,512]{1,0:T(8,128)S(1)} collective-permute-done((f32[384,512]{1,0:T(8,128)S(1)}, f32[384,512]{1,0:T(8,128)S(1)}, u32[]{:S(2)}, u32[]{:S(2)}) %collective-permute-start.6) | collective-permute-done | bytes 786464 | tf_op jit(solution)/shard_map/ppermute | solution.py:37
  150.3 1.0 add_bitcast_fusion
  (9 shorter events, 0.3 us)
Async XLA Ops:
  0.0 59.5 %collective-permute-start.1 = (f32[384,512]{1,0:T(8,128)}, f32[384,512]{1,0:T(8,128)S(1)}, u32[]{:S(2)}, u32[]{:S(2)}) collective-permute-start(f32[384,512]{1,0:T(8,128)} %bitcast.8), channel_id=1, source_target_pairs={{0,764},{2,766},{4,744},{6,746},{8,4},{10,6},{12,8},{14,10},{16,12... | collective-permute-start | bytes 2359304 | tf_op jit(solution)/shard_map/ppermute | solution.py:37
  20.2 39.2 %collective-permute-start = (f32[384,512]{1,0:T(8,128)}, f32[384,512]{1,0:T(8,128)S(1)}, u32[]{:S(2)}, u32[]{:S(2)}) collective-permute-start(f32[384,512]{1,0:T(8,128)} %bitcast.9), channel_id=1, source_target_pairs={{0,4},{2,6},{4,8},{6,10},{8,12},{10,14},{12,16},{14,18},{16,20},{1... | collective-permute-start | bytes 2359304 | tf_op jit(solution)/shard_map/ppermute | solution.py:37
  22.8 31.0 %collective-permute-start.3 = (f32[8,128]{1,0:T(8,128)S(1)}, f32[8,128]{1,0:T(8,128)S(1)}, u32[]{:S(2)}, u32[]{:S(2)}) collective-permute-start(f32[8,128]{1,0:T(8,128)S(1)} %broadcast_in_dim.4), channel_id=1, source_target_pairs={{0,764},{2,766},{4,744},{6,746},{8,4},{10,6},{12,8},{14,10},{16,12... | collective-permute-start | bytes 12296 | tf_op jit(solution)/shard_map/ppermute | solution.py:37
  29.1 30.4 %collective-permute-start.2 = (f32[8,128]{1,0:T(8,128)S(1)}, f32[8,128]{1,0:T(8,128)S(1)}, u32[]{:S(2)}, u32[]{:S(2)}) collective-permute-start(f32[8,128]{1,0:T(8,128)S(1)} %broadcast_in_dim.4), channel_id=1, source_target_pairs={{0,4},{2,6},{4,8},{6,10},{8,12},{10,14},{12,16},{14,18},{16,20},{1... | collective-permute-start | bytes 12296 | tf_op jit(solution)/shard_map/ppermute | solution.py:37
  60.1 5.3 %collective-permute-start.4 = (f32[512,256]{1,0:T(8,128)S(1)}, f32[512,256]{1,0:T(8,128)S(1)}, u32[]{:S(2)}, u32[]{:S(2)}) collective-permute-start(f32[512,256]{1,0:T(8,128)S(1)} %shard_map.40.refs_3_), channel_id=1, source_target_pairs={{0,1},{1,0},{2,3},{3,2},{4,5},{5,4},{6,7},{7,6},{8,9},{9,8},{10,11... | collective-permute-start | bytes 1572872 | tf_op jit(solution)/shard_map/ppermute | solution.py:41
  66.3 16.7 %all-to-all-start = ((f32[4,128,256]{2,1,0:T(8,128)}), f32[4,128,256]{2,1,0:T(8,128)S(1)}, u32[]{:S(2)}, u32[]{:S(2)}) async-start(f32[4,128,256]{2,1,0:T(8,128)} %shard_map.42), calls=%async_computation | async-start | bytes 1048576 | tf_op jit(solution)/shard_map/all_to_all | solution.py:116
  72.1 0.7 copy-start
  101.3 4.9 %collective-permute-start.5 = (f32[4,128,256]{2,1,0:T(8,128)S(1)}, f32[4,128,256]{2,1,0:T(8,128)S(1)}, u32[]{:S(2)}, u32[]{:S(2)}) collective-permute-start(f32[4,128,256]{2,1,0:T(8,128)S(1)} %all_to_all.10.refs_4_), channel_id=1, source_target_pairs={{0,1},{1,0},{2,3},{3,2},{4,5},{5,4},{6,7},{7,6},{8,9},{9,8},{10,11... | collective-permute-start | bytes 1572872 | tf_op jit(solution)/shard_map/ppermute | solution.py:41
  107.7 42.6 %collective-permute-start.6 = (f32[384,512]{1,0:T(8,128)S(1)}, f32[384,512]{1,0:T(8,128)S(1)}, u32[]{:S(2)}, u32[]{:S(2)}) collective-permute-start(f32[384,512]{1,0:T(8,128)S(1)} %get-tuple-element.7), channel_id=1, source_target_pairs={{764,0},{766,2},{744,4},{746,6},{4,8},{6,10},{8,12},{10,14},{12,16... | collective-permute-start | bytes 2359304 | tf_op jit(solution)/shard_map/ppermute | solution.py:37
  109.6 40.7 %collective-permute-start.7 = (f32[384,512]{1,0:T(8,128)S(1)}, f32[384,512]{1,0:T(8,128)S(1)}, u32[]{:S(2)}, u32[]{:S(2)}) collective-permute-start(f32[384,512]{1,0:T(8,128)S(1)} %get-tuple-element.8), channel_id=1, source_target_pairs={{4,0},{6,2},{8,4},{10,6},{12,8},{14,10},{16,12},{18,14},{20,16},{2... | collective-permute-start | bytes 2359304 | tf_op jit(solution)/shard_map/ppermute | solution.py:37

commit v10 on v9

--- a/solution.py
+++ b/solution.py
@@ -81,9 +81,9 @@
     out_ref[...] = (keep_ref[...] + got_ref[...]).reshape(out_ref.shape)
 
 
-def divide(parts_ref, denominator_ref, out_ref):
+def divide(parts_ref, sums_ref, energy_ref, other_energy_ref, out_ref):
     total = (parts_ref[0] + parts_ref[1]) + (parts_ref[2] + parts_ref[3])
-    amplitude = total / denominator_ref[...]
+    amplitude = total / (sums_ref[...] - (energy_ref[:1, :1] + other_energy_ref[:1, :1]))
     for k in range(CHIPS):
         out_ref[k] = amplitude
 
@@ -118,14 +118,14 @@
     lower, upper = move(own, there(above)), move(own, there(below))
     energy = jnp.broadcast_to(occ_energy, (8, 128))
     energies = move(energy, there(above)), move(energy, there(below))
-    give = kernel(pair_tile, [(virt, half)], [other], [lower, upper], energies)[0]
+    row_energy = lax.dynamic_slice_in_dim(virt_energy, chip * quarter, quarter, 0)
+    column_energy = lax.dynamic_slice_in_dim(virt_energy, mine, half, 0)
+    sums = row_energy[:, None] + column_energy[None, :]
+    give = kernel(pair_tile, [(virt, half)], [other], [lower, upper], [*energies, sums])[0]
     keep = kernel(pair_tile, [(virt, half)], [mine], [lower, upper], [give])[0]
     whole = (CHIPS, quarter, half)
     tile = kernel(add_tiles, [whole], [], [keep, core_swap(give)])[0]
-    row_energy = lax.dynamic_slice_in_dim(virt_energy, chip * quarter, quarter, 0)
-    column_energy = lax.dynamic_slice_in_dim(virt_energy, mine, half, 0)
-    denominator = (row_energy - (energies[0][0, 0] + energies[1][0, 0]))[:, None] + column_energy[None, :]
-    amp = shared(kernel(divide, [whole], [], [shared(tile), denominator])[0])
+    amp = shared(kernel(divide, [whole], [], [shared(tile), sums, *energies])[0])
     swapped = core_swap(amp)
     up, down = kernel(density_parts, [(rows, virt)] * 2, [mine, other], [lower, upper, amp, swapped])
     return (move(up, back(below)) + move(down, back(above)))[None]

time: 152 us -> 151 us (level)
  blocking collectives: 18.3 us -> 34.9 us
  waiting for transfers between devices: 73.7 us -> 65.1 us
  starting transfers between devices: 50.8 us -> 45 us
    all_to_all x1 -> x2, blocking collectives: 18.3 us -> 34.9 us  [shared(): return lax.all_to_all(x, PLACES, 0, 0, axis_index_groups=groups, tiled=True)]
    all_to_all x1 -> x0, waiting for transfers between devices: 7.73 us -> none  [shared(): return lax.all_to_all(x, PLACES, 0, 0, axis_index_groups=groups, tiled=True)]
    all_to_all x1 -> x0, starting transfers between devices: 5.82 us -> none  [shared(): return lax.all_to_all(x, PLACES, 0, 0, axis_index_groups=groups, tiled=True)]
  transfers between devices with their start and end apart: 9 -> 8, of which waited for: 6 -> 5; matrix products, arithmetic and copies ran while one was open for 1% -> 0% of each run, Pallas kernels for 0% -> 0%
where the time goes in v10:
time: 151 us
  waiting for transfers between devices  65.1 us (43%)
  starting transfers between devices  45 us (30%)
  blocking collectives  34.9 us (23%)
  Pallas kernels  2.83 us (2%)
    ppermute x6, waiting for transfers between devices, move(): return lax.ppermute(x, PLACES, pairs)  62.7 us
    ppermute x6, starting transfers between devices, move(): return lax.ppermute(x, PLACES, pairs)  37.8 us
    all_to_all x2, blocking collectives, shared(): return lax.all_to_all(x, PLACES, 0, 0, axis_index_groups=groups, tiled=True)  34.9 us
    ppermute x2, starting transfers between devices, core_swap(): return lax.ppermute(x, 'core', [(0, 1), (1, 0)])  7.2 us
  transfers between devices with their start and end apart: 8, of which 5 were waited for; matrix products, arithmetic and copies ran while one was open for 0% of the time, Pallas kernels for 0%

profile of v10, /device:TPU:1, one launch (start us, length us, event | category | flops | bytes accessed | tf_op | source)
XLA Modules:
  0.0 150.5 jit_solution(6975606455852426615)
XLA Ops:
  0.0 20.2 %collective-permute-start.1 = (f32[384,512]{1,0:T(8,128)}, f32[384,512]{1,0:T(8,128)S(1)}, u32[]{:S(2)}, u32[]{:S(2)}) collective-permute-start(f32[384,512]{1,0:T(8,128)} %bitcast.7), channel_id=1, source_target_pairs={{0,764},{2,766},{4,744},{6,746},{8,4},{10,6},{12,8},{14,10},{16,12... | collective-permute-start | bytes 2359304 | tf_op jit(solution)/shard_map/ppermute | solution.py:37
  20.2 1.9 %collective-permute-start = (f32[384,512]{1,0:T(8,128)}, f32[384,512]{1,0:T(8,128)S(1)}, u32[]{:S(2)}, u32[]{:S(2)}) collective-permute-start(f32[384,512]{1,0:T(8,128)} %bitcast.8), channel_id=1, source_target_pairs={{0,4},{2,6},{4,8},{6,10},{8,12},{10,14},{12,16},{14,18},{16,20},{1... | collective-permute-start | bytes 2359304 | tf_op jit(solution)/shard_map/ppermute | solution.py:37
  22.8 6.3 %collective-permute-start.3 = (f32[8,128]{1,0:T(8,128)S(1)}, f32[8,128]{1,0:T(8,128)S(1)}, u32[]{:S(2)}, u32[]{:S(2)}) collective-permute-start(f32[8,128]{1,0:T(8,128)S(1)} %broadcast_in_dim.4), channel_id=1, source_target_pairs={{0,764},{2,766},{4,744},{6,746},{8,4},{10,6},{12,8},{14,10},{16,12... | collective-permute-start | bytes 12296 | tf_op jit(solution)/shard_map/ppermute | solution.py:37
  29.1 1.9 %collective-permute-start.2 = (f32[8,128]{1,0:T(8,128)S(1)}, f32[8,128]{1,0:T(8,128)S(1)}, u32[]{:S(2)}, u32[]{:S(2)}) collective-permute-start(f32[8,128]{1,0:T(8,128)S(1)} %broadcast_in_dim.4), channel_id=1, source_target_pairs={{0,4},{2,6},{4,8},{6,10},{8,12},{10,14},{12,16},{14,18},{16,20},{1... | collective-permute-start | bytes 12296 | tf_op jit(solution)/shard_map/ppermute | solution.py:37
  31.0 0.7 copy-done
  31.7 0.1 dynamic_slice.6
  31.8 0.1 dynamic_slice.7
  31.8 0.1 broadcast_add_fusion.refs_5_.refs_1_
  31.9 21.9 %collective-permute-done.3.refs_4_.refs_3_ = f32[8,128]{1,0:T(8,128)S(1)} collective-permute-done((f32[8,128]{1,0:T(8,128)S(1)}, f32[8,128]{1,0:T(8,128)S(1)}, u32[]{:S(2)}, u32[]{:S(2)}) %collective-permute-start.3) | collective-permute-done | bytes 4128 | tf_op jit(solution)/shard_map/ppermute | solution.py:37
  53.8 5.7 %collective-permute-done.2.refs_3_.refs_2_ = f32[8,128]{1,0:T(8,128)S(1)} collective-permute-done((f32[8,128]{1,0:T(8,128)S(1)}, f32[8,128]{1,0:T(8,128)S(1)}, u32[]{:S(2)}, u32[]{:S(2)}) %collective-permute-start.2) | collective-permute-done | bytes 4128 | tf_op jit(solution)/shard_map/ppermute | solution.py:37
  59.5 0.6 shard_map.40.refs_3_
  60.1 3.8 %collective-permute-start.4 = (f32[512,256]{1,0:T(8,128)S(1)}, f32[512,256]{1,0:T(8,128)S(1)}, u32[]{:S(2)}, u32[]{:S(2)}) collective-permute-start(f32[512,256]{1,0:T(8,128)S(1)} %shard_map.40.refs_3_), channel_id=1, source_target_pairs={{0,1},{1,0},{2,3},{3,2},{4,5},{5,4},{6,7},{7,6},{8,9},{9,8},{10,11... | collective-permute-start | bytes 1572872 | tf_op jit(solution)/shard_map/ppermute | solution.py:41
  63.9 0.6 shard_map.41.refs_0_
  64.6 0.9 collective-permute-done.4.refs_1_
  65.5 17.2 %all_to_all.10.refs_0_ = f32[4,128,256]{2,1,0:T(8,128)S(1)} all-to-all(f32[4,128,256]{2,1,0:T(8,128)S(1)} %shard_map.42), channel_id=1, replica_groups={{4,6,8,10},{12,14,16,18},{20,22,0,2},{28,30,32,34},{36,38,40,42},{44,46..., dimensions={0} | all-to-all | bytes 1048576 | tf_op jit(solution)/shard_map/all_to_all | solution.py:116
  82.7 0.1 shard_map.43
  82.8 17.8 %all_to_all.11.refs_4_ = f32[4,128,256]{2,1,0:T(8,128)S(1)} all-to-all(f32[4,128,256]{2,1,0:T(8,128)S(1)} %shard_map.43), channel_id=1, replica_groups={{4,6,8,10},{12,14,16,18},{20,22,0,2},{28,30,32,34},{36,38,40,42},{44,46..., dimensions={0} | all-to-all | bytes 1048576 | tf_op jit(solution)/shard_map/all_to_all | solution.py:116
  100.5 3.4 %collective-permute-start.5 = (f32[4,128,256]{2,1,0:T(8,128)S(1)}, f32[4,128,256]{2,1,0:T(8,128)S(1)}, u32[]{:S(2)}, u32[]{:S(2)}) collective-permute-start(f32[4,128,256]{2,1,0:T(8,128)S(1)} %all_to_all.11.refs_4_), channel_id=1, source_target_pairs={{0,1},{1,0},{2,3},{3,2},{4,5},{5,4},{6,7},{7,6},{8,9},{9,8},{10,11... | collective-permute-start | bytes 1572872 | tf_op jit(solution)/shard_map/ppermute | solution.py:41
  103.9 1.5 %collective-permute-done.5.refs_5_ = f32[4,128,256]{2,1,0:T(8,128)S(1)} collective-permute-done((f32[4,128,256]{2,1,0:T(8,128)S(1)}, f32[4,128,256]{2,1,0:T(8,128)S(1)}, u32[]{:S(2)}, u32[]{:S(2)}) %collective-permute-start.5) | collective-permute-done | bytes 524320 | tf_op jit(solution)/shard_map/ppermute | solution.py:41
  105.4 1.4 shard_map.44
  106.9 1.9 %collective-permute-start.6 = (f32[384,512]{1,0:T(8,128)S(1)}, f32[384,512]{1,0:T(8,128)S(1)}, u32[]{:S(2)}, u32[]{:S(2)}) collective-permute-start(f32[384,512]{1,0:T(8,128)S(1)} %get-tuple-element.7), channel_id=1, source_target_pairs={{764,0},{766,2},{744,4},{746,6},{4,8},{6,10},{8,12},{10,14},{12,16... | collective-permute-start | bytes 2359304 | tf_op jit(solution)/shard_map/ppermute | solution.py:37
  108.8 5.6 %collective-permute-start.7 = (f32[384,512]{1,0:T(8,128)S(1)}, f32[384,512]{1,0:T(8,128)S(1)}, u32[]{:S(2)}, u32[]{:S(2)}) collective-permute-start(f32[384,512]{1,0:T(8,128)S(1)} %get-tuple-element.8), channel_id=1, source_target_pairs={{4,0},{6,2},{8,4},{10,6},{12,8},{14,10},{16,12},{18,14},{20,16},{2... | collective-permute-start | bytes 2359304 | tf_op jit(solution)/shard_map/ppermute | solution.py:37
  114.4 35.1 %collective-permute-done.6 = f32[384,512]{1,0:T(8,128)S(1)} collective-permute-done((f32[384,512]{1,0:T(8,128)S(1)}, f32[384,512]{1,0:T(8,128)S(1)}, u32[]{:S(2)}, u32[]{:S(2)}) %collective-permute-start.6) | collective-permute-done | bytes 786464 | tf_op jit(solution)/shard_map/ppermute | solution.py:37
  149.5 1.0 add_bitcast_fusion
  (6 shorter events, 0.1 us)
Async XLA Ops:
  0.0 59.5 %collective-permute-start.1 = (f32[384,512]{1,0:T(8,128)}, f32[384,512]{1,0:T(8,128)S(1)}, u32[]{:S(2)}, u32[]{:S(2)}) collective-permute-start(f32[384,512]{1,0:T(8,128)} %bitcast.7), channel_id=1, source_target_pairs={{0,764},{2,766},{4,744},{6,746},{8,4},{10,6},{12,8},{14,10},{16,12... | collective-permute-start | bytes 2359304 | tf_op jit(solution)/shard_map/ppermute | solution.py:37
  20.2 39.2 %collective-permute-start = (f32[384,512]{1,0:T(8,128)}, f32[384,512]{1,0:T(8,128)S(1)}, u32[]{:S(2)}, u32[]{:S(2)}) collective-permute-start(f32[384,512]{1,0:T(8,128)} %bitcast.8), channel_id=1, source_target_pairs={{0,4},{2,6},{4,8},{6,10},{8,12},{10,14},{12,16},{14,18},{16,20},{1... | collective-permute-start | bytes 2359304 | tf_op jit(solution)/shard_map/ppermute | solution.py:37
  22.8 31.0 %collective-permute-start.3 = (f32[8,128]{1,0:T(8,128)S(1)}, f32[8,128]{1,0:T(8,128)S(1)}, u32[]{:S(2)}, u32[]{:S(2)}) collective-permute-start(f32[8,128]{1,0:T(8,128)S(1)} %broadcast_in_dim.4), channel_id=1, source_target_pairs={{0,764},{2,766},{4,744},{6,746},{8,4},{10,6},{12,8},{14,10},{16,12... | collective-permute-start | bytes 12296 | tf_op jit(solution)/shard_map/ppermute | solution.py:37
  29.1 30.4 %collective-permute-start.2 = (f32[8,128]{1,0:T(8,128)S(1)}, f32[8,128]{1,0:T(8,128)S(1)}, u32[]{:S(2)}, u32[]{:S(2)}) collective-permute-start(f32[8,128]{1,0:T(8,128)S(1)} %broadcast_in_dim.4), channel_id=1, source_target_pairs={{0,4},{2,6},{4,8},{6,10},{8,12},{10,14},{12,16},{14,18},{16,20},{1... | collective-permute-start | bytes 12296 | tf_op jit(solution)/shard_map/ppermute | solution.py:37
  31.0 0.7 copy-start
  60.1 5.3 %collective-permute-start.4 = (f32[512,256]{1,0:T(8,128)S(1)}, f32[512,256]{1,0:T(8,128)S(1)}, u32[]{:S(2)}, u32[]{:S(2)}) collective-permute-start(f32[512,256]{1,0:T(8,128)S(1)} %shard_map.40.refs_3_), channel_id=1, source_target_pairs={{0,1},{1,0},{2,3},{3,2},{4,5},{5,4},{6,7},{7,6},{8,9},{9,8},{10,11... | collective-permute-start | bytes 1572872 | tf_op jit(solution)/shard_map/ppermute | solution.py:41
  100.5 4.9 %collective-permute-start.5 = (f32[4,128,256]{2,1,0:T(8,128)S(1)}, f32[4,128,256]{2,1,0:T(8,128)S(1)}, u32[]{:S(2)}, u32[]{:S(2)}) collective-permute-start(f32[4,128,256]{2,1,0:T(8,128)S(1)} %all_to_all.11.refs_4_), channel_id=1, source_target_pairs={{0,1},{1,0},{2,3},{3,2},{4,5},{5,4},{6,7},{7,6},{8,9},{9,8},{10,11... | collective-permute-start | bytes 1572872 | tf_op jit(solution)/shard_map/ppermute | solution.py:41
  106.9 42.6 %collective-permute-start.6 = (f32[384,512]{1,0:T(8,128)S(1)}, f32[384,512]{1,0:T(8,128)S(1)}, u32[]{:S(2)}, u32[]{:S(2)}) collective-permute-start(f32[384,512]{1,0:T(8,128)S(1)} %get-tuple-element.7), channel_id=1, source_target_pairs={{764,0},{766,2},{744,4},{746,6},{4,8},{6,10},{8,12},{10,14},{12,16... | collective-permute-start | bytes 2359304 | tf_op jit(solution)/shard_map/ppermute | solution.py:37
  108.8 40.7 %collective-permute-start.7 = (f32[384,512]{1,0:T(8,128)S(1)}, f32[384,512]{1,0:T(8,128)S(1)}, u32[]{:S(2)}, u32[]{:S(2)}) collective-permute-start(f32[384,512]{1,0:T(8,128)S(1)} %get-tuple-element.8), channel_id=1, source_target_pairs={{4,0},{6,2},{8,4},{10,6},{12,8},{14,10},{16,12},{18,14},{20,16},{2... | collective-permute-start | bytes 2359304 | tf_op jit(solution)/shard_map/ppermute | solution.py:37

commit v11 on v10

--- a/solution.py
+++ b/solution.py
@@ -9,6 +9,7 @@
 LEVELS = 3
 RING = CHIPS * LEVELS
 PLACES = ("occ", "z")
+PLANES = (3, 5, 2, 4)
 SMEM = pl.BlockSpec(memory_space=pltpu.SMEM)
 VMEM = pl.BlockSpec(memory_space=pltpu.VMEM)
 ANY = pl.BlockSpec(memory_space=pl.ANY)
@@ -18,7 +19,7 @@
     above, below, groups = [0] * (occupied * CHIPS), [0] * (occupied * CHIPS), []
     for i in range(occupied):
         column, level = divmod(i, LEVELS)
-        groups.append([column * RING + (level * CHIPS + c + CHIPS // 2) % RING for c in range(CHIPS)])
+        groups.append([column * RING + (level * CHIPS + plane) % RING for plane in PLANES])
         for c, goal in enumerate(groups[-1]):
             above[i * CHIPS + c] = goal
             below[(i + 1) % occupied * CHIPS + c] = goal
@@ -110,7 +111,7 @@
     above, below, groups = meetings(occupied)
     mine = lax.axis_index("core") * half
     other = half - mine
-    chip = lax.rem(lax.axis_index("z") + CHIPS // 2, CHIPS)
+    chip = lax.dynamic_index_in_dim(jnp.asarray((3, 1, 2, 0), jnp.int32), lax.axis_index("z"), keepdims=False)
 
     def shared(x):
         return lax.all_to_all(x, PLACES, 0, 0, axis_index_groups=groups, tiled=True)

time: 151 us -> 144 us (0.954)
  waiting for transfers between devices: 65.1 us -> 58.9 us
  blocking collectives: 34.9 us -> 31.6 us
    ppermute x6, waiting for transfers between devices: 62.7 us -> 56.5 us  [move(): return lax.ppermute(x, PLACES, pairs)]
    all_to_all x2, blocking collectives: 34.9 us -> 31.6 us  [shared(): return lax.all_to_all(x, PLACES, 0, 0, axis_index_groups=groups, tiled=True)]
  transfers between devices with their start and end apart: 8 -> 8, of which waited for: 5 -> 6; matrix products, arithmetic and copies ran while one was open for 0% -> 1% of each run, Pallas kernels for 0% -> 0%
where the time goes in v11:
time: 144 us; the launch traced here: 142 us
  waiting for transfers between devices  58.9 us (41%)
  starting transfers between devices  44.5 us (31%)
  blocking collectives  31.6 us (22%)
  Pallas kernels  2.82 us (2%)
  local copies, waits for them, and re-layouts  2.08 us (1%)
    ppermute x6, waiting for transfers between devices, move(): return lax.ppermute(x, PLACES, pairs)  56.5 us
    ppermute x6, starting transfers between devices, move(): return lax.ppermute(x, PLACES, pairs)  37.4 us
    all_to_all x2, blocking collectives, shared(): return lax.all_to_all(x, PLACES, 0, 0, axis_index_groups=groups, tiled=True)  31.6 us
    ppermute x2, starting transfers between devices, core_swap(): return lax.ppermute(x, 'core', [(0, 1), (1, 0)])  7.06 us
  transfers between devices with their start and end apart: 8, of which 6 were waited for; matrix products, arithmetic and copies ran while one was open for 1% of the time, Pallas kernels for 0%

profile of v11, /device:TPU:1, one launch (start us, length us, event | category | flops | bytes accessed | tf_op | source)
XLA Modules:
  0.0 142.4 jit_solution(6696138549246091908)
XLA Ops:
  0.0 20.2 %collective-permute-start.1 = (f32[384,512]{1,0:T(8,128)}, f32[384,512]{1,0:T(8,128)S(1)}, u32[]{:S(2)}, u32[]{:S(2)}) collective-permute-start(f32[384,512]{1,0:T(8,128)} %bitcast.8), channel_id=1, source_target_pairs={{0,766},{2,746},{4,764},{6,744},{8,6},{10,10},{12,4},{14,8},{16,14... | collective-permute-start | bytes 2359304 | tf_op jit(solution)/shard_map/ppermute | solution.py:38
  20.2 1.9 %collective-permute-start = (f32[384,512]{1,0:T(8,128)}, f32[384,512]{1,0:T(8,128)S(1)}, u32[]{:S(2)}, u32[]{:S(2)}) collective-permute-start(f32[384,512]{1,0:T(8,128)} %bitcast.9), channel_id=1, source_target_pairs={{0,6},{2,10},{4,4},{6,8},{8,14},{10,18},{12,12},{14,16},{16,22},{1... | collective-permute-start | bytes 2359304 | tf_op jit(solution)/shard_map/ppermute | solution.py:38
  22.8 5.4 %collective-permute-start.3 = (f32[8,128]{1,0:T(8,128)S(1)}, f32[8,128]{1,0:T(8,128)S(1)}, u32[]{:S(2)}, u32[]{:S(2)}) collective-permute-start(f32[8,128]{1,0:T(8,128)S(1)} %broadcast_in_dim.4), channel_id=1, source_target_pairs={{0,766},{2,746},{4,764},{6,744},{8,6},{10,10},{12,4},{14,8},{16,14... | collective-permute-start | bytes 12296 | tf_op jit(solution)/shard_map/ppermute | solution.py:38
  28.2 2.5 %collective-permute-start.2 = (f32[8,128]{1,0:T(8,128)S(1)}, f32[8,128]{1,0:T(8,128)S(1)}, u32[]{:S(2)}, u32[]{:S(2)}) collective-permute-start(f32[8,128]{1,0:T(8,128)S(1)} %broadcast_in_dim.4), channel_id=1, source_target_pairs={{0,6},{2,10},{4,4},{6,8},{8,14},{10,18},{12,12},{14,16},{16,22},{1... | collective-permute-start | bytes 12296 | tf_op jit(solution)/shard_map/ppermute | solution.py:38
  30.7 0.6 copy-done.1
  31.4 0.6 dynamic_slice.10
  32.6 0.7 copy-done
  33.4 0.1 broadcast_add_fusion.refs_5_.refs_1_
  33.5 20.1 %collective-permute-done.3.refs_4_.refs_3_ = f32[8,128]{1,0:T(8,128)S(1)} collective-permute-done((f32[8,128]{1,0:T(8,128)S(1)}, f32[8,128]{1,0:T(8,128)S(1)}, u32[]{:S(2)}, u32[]{:S(2)}) %collective-permute-start.3) | collective-permute-done | bytes 4128 | tf_op jit(solution)/shard_map/ppermute | solution.py:38
  53.7 0.2 collective-permute-done.2.refs_3_.refs_2_
  53.9 0.6 shard_map.49.refs_3_
  54.5 3.3 %collective-permute-start.4 = (f32[512,256]{1,0:T(8,128)S(1)}, f32[512,256]{1,0:T(8,128)S(1)}, u32[]{:S(2)}, u32[]{:S(2)}) collective-permute-start(f32[512,256]{1,0:T(8,128)S(1)} %shard_map.49.refs_3_), channel_id=1, source_target_pairs={{0,1},{1,0},{2,3},{3,2},{4,5},{5,4},{6,7},{7,6},{8,9},{9,8},{10,11... | collective-permute-start | bytes 1572872 | tf_op jit(solution)/shard_map/ppermute | solution.py:42
  57.8 0.6 shard_map.50.refs_0_
  58.5 0.9 collective-permute-done.4.refs_1_
  59.4 15.6 %all_to_all.10.refs_0_ = f32[4,128,256]{2,1,0:T(8,128)S(1)} all-to-all(f32[4,128,256]{2,1,0:T(8,128)S(1)} %shard_map.51), channel_id=1, replica_groups={{6,10,4,8},{14,18,12,16},{22,2,20,0},{30,34,28,32},{38,42,36,40},{46,26..., dimensions={0} | all-to-all | bytes 1048576 | tf_op jit(solution)/shard_map/all_to_all | solution.py:117
  75.1 15.9 %all_to_all.11.refs_4_ = f32[4,128,256]{2,1,0:T(8,128)S(1)} all-to-all(f32[4,128,256]{2,1,0:T(8,128)S(1)} %shard_map.52), channel_id=1, replica_groups={{6,10,4,8},{14,18,12,16},{22,2,20,0},{30,34,28,32},{38,42,36,40},{46,26..., dimensions={0} | all-to-all | bytes 1048576 | tf_op jit(solution)/shard_map/all_to_all | solution.py:117
  91.1 3.8 %collective-permute-start.5 = (f32[4,128,256]{2,1,0:T(8,128)S(1)}, f32[4,128,256]{2,1,0:T(8,128)S(1)}, u32[]{:S(2)}, u32[]{:S(2)}) collective-permute-start(f32[4,128,256]{2,1,0:T(8,128)S(1)} %all_to_all.11.refs_4_), channel_id=1, source_target_pairs={{0,1},{1,0},{2,3},{3,2},{4,5},{5,4},{6,7},{7,6},{8,9},{9,8},{10,11... | collective-permute-start | bytes 1572872 | tf_op jit(solution)/shard_map/ppermute | solution.py:42
  94.8 1.5 %collective-permute-done.5.refs_5_ = f32[4,128,256]{2,1,0:T(8,128)S(1)} collective-permute-done((f32[4,128,256]{2,1,0:T(8,128)S(1)}, f32[4,128,256]{2,1,0:T(8,128)S(1)}, u32[]{:S(2)}, u32[]{:S(2)}) %collective-permute-start.5) | collective-permute-done | bytes 524320 | tf_op jit(solution)/shard_map/ppermute | solution.py:42
  96.3 1.4 %shard_map.53 = (f32[384,512]{1,0:T(8,128)S(1)}, f32[384,512]{1,0:T(8,128)S(1)}) custom-call(s32[1]{0:T(128)} %bitcast.refs_0_, s32[1]{0:T(128)} %bitcast.1.refs_0_.refs_1_, f32[384,512]{1,0:T(8,128)S(1)} %collective-permute-done.refs_1_.refs_2_, f32[384,512]{1,0:T(8,128)S(1)} %collective-permute-done.1.refs_2_.refs_3_, ...), custom_call_target="tpu_custom_call" | custom-call | tf_op jit(solution)/shard_map/pallas_call | solution.py:51
  97.8 4.5 %collective-permute-start.6 = (f32[384,512]{1,0:T(8,128)S(1)}, f32[384,512]{1,0:T(8,128)S(1)}, u32[]{:S(2)}, u32[]{:S(2)}) collective-permute-start(f32[384,512]{1,0:T(8,128)S(1)} %get-tuple-element.7), channel_id=1, source_target_pairs={{766,0},{746,2},{764,4},{744,6},{6,8},{10,10},{4,12},{8,14},{14,16... | collective-permute-start | bytes 2359304 | tf_op jit(solution)/shard_map/ppermute | solution.py:38
  102.3 2.9 %collective-permute-start.7 = (f32[384,512]{1,0:T(8,128)S(1)}, f32[384,512]{1,0:T(8,128)S(1)}, u32[]{:S(2)}, u32[]{:S(2)}) collective-permute-start(f32[384,512]{1,0:T(8,128)S(1)} %get-tuple-element.8), channel_id=1, source_target_pairs={{6,0},{10,2},{4,4},{8,6},{14,8},{18,10},{12,12},{16,14},{22,16},{2... | collective-permute-start | bytes 2359304 | tf_op jit(solution)/shard_map/ppermute | solution.py:38
  105.2 23.3 %collective-permute-done.6 = f32[384,512]{1,0:T(8,128)S(1)} collective-permute-done((f32[384,512]{1,0:T(8,128)S(1)}, f32[384,512]{1,0:T(8,128)S(1)}, u32[]{:S(2)}, u32[]{:S(2)}) %collective-permute-start.6) | collective-permute-done | bytes 786464 | tf_op jit(solution)/shard_map/ppermute | solution.py:38
  128.5 12.8 %collective-permute-done.7 = f32[384,512]{1,0:T(8,128)S(1)} collective-permute-done((f32[384,512]{1,0:T(8,128)S(1)}, f32[384,512]{1,0:T(8,128)S(1)}, u32[]{:S(2)}, u32[]{:S(2)}) %collective-permute-start.7) | collective-permute-done | bytes 786464 | tf_op jit(solution)/shard_map/ppermute | solution.py:38
  141.4 1.0 add_bitcast_fusion
  (9 shorter events, 0.3 us)
Async XLA Ops:
  0.0 53.9 %collective-permute-start.1 = (f32[384,512]{1,0:T(8,128)}, f32[384,512]{1,0:T(8,128)S(1)}, u32[]{:S(2)}, u32[]{:S(2)}) collective-permute-start(f32[384,512]{1,0:T(8,128)} %bitcast.8), channel_id=1, source_target_pairs={{0,766},{2,746},{4,764},{6,744},{8,6},{10,10},{12,4},{14,8},{16,14... | collective-permute-start | bytes 2359304 | tf_op jit(solution)/shard_map/ppermute | solution.py:38
  20.2 33.7 %collective-permute-start = (f32[384,512]{1,0:T(8,128)}, f32[384,512]{1,0:T(8,128)S(1)}, u32[]{:S(2)}, u32[]{:S(2)}) collective-permute-start(f32[384,512]{1,0:T(8,128)} %bitcast.9), channel_id=1, source_target_pairs={{0,6},{2,10},{4,4},{6,8},{8,14},{10,18},{12,12},{14,16},{16,22},{1... | collective-permute-start | bytes 2359304 | tf_op jit(solution)/shard_map/ppermute | solution.py:38
  22.8 30.9 %collective-permute-start.3 = (f32[8,128]{1,0:T(8,128)S(1)}, f32[8,128]{1,0:T(8,128)S(1)}, u32[]{:S(2)}, u32[]{:S(2)}) collective-permute-start(f32[8,128]{1,0:T(8,128)S(1)} %broadcast_in_dim.4), channel_id=1, source_target_pairs={{0,766},{2,746},{4,764},{6,744},{8,6},{10,10},{12,4},{14,8},{16,14... | collective-permute-start | bytes 12296 | tf_op jit(solution)/shard_map/ppermute | solution.py:38
  28.2 25.7 %collective-permute-start.2 = (f32[8,128]{1,0:T(8,128)S(1)}, f32[8,128]{1,0:T(8,128)S(1)}, u32[]{:S(2)}, u32[]{:S(2)}) collective-permute-start(f32[8,128]{1,0:T(8,128)S(1)} %broadcast_in_dim.4), channel_id=1, source_target_pairs={{0,6},{2,10},{4,4},{6,8},{8,14},{10,18},{12,12},{14,16},{16,22},{1... | collective-permute-start | bytes 12296 | tf_op jit(solution)/shard_map/ppermute | solution.py:38
  30.7 0.7 copy-start.1
  32.6 0.7 copy-start
  54.5 4.8 %collective-permute-start.4 = (f32[512,256]{1,0:T(8,128)S(1)}, f32[512,256]{1,0:T(8,128)S(1)}, u32[]{:S(2)}, u32[]{:S(2)}) collective-permute-start(f32[512,256]{1,0:T(8,128)S(1)} %shard_map.49.refs_3_), channel_id=1, source_target_pairs={{0,1},{1,0},{2,3},{3,2},{4,5},{5,4},{6,7},{7,6},{8,9},{9,8},{10,11... | collective-permute-start | bytes 1572872 | tf_op jit(solution)/shard_map/ppermute | solution.py:42
  91.1 5.3 %collective-permute-start.5 = (f32[4,128,256]{2,1,0:T(8,128)S(1)}, f32[4,128,256]{2,1,0:T(8,128)S(1)}, u32[]{:S(2)}, u32[]{:S(2)}) collective-permute-start(f32[4,128,256]{2,1,0:T(8,128)S(1)} %all_to_all.11.refs_4_), channel_id=1, source_target_pairs={{0,1},{1,0},{2,3},{3,2},{4,5},{5,4},{6,7},{7,6},{8,9},{9,8},{10,11... | collective-permute-start | bytes 1572872 | tf_op jit(solution)/shard_map/ppermute | solution.py:42
  97.8 30.7 %collective-permute-start.6 = (f32[384,512]{1,0:T(8,128)S(1)}, f32[384,512]{1,0:T(8,128)S(1)}, u32[]{:S(2)}, u32[]{:S(2)}) collective-permute-start(f32[384,512]{1,0:T(8,128)S(1)} %get-tuple-element.7), channel_id=1, source_target_pairs={{766,0},{746,2},{764,4},{744,6},{6,8},{10,10},{4,12},{8,14},{14,16... | collective-permute-start | bytes 2359304 | tf_op jit(solution)/shard_map/ppermute | solution.py:38
  102.3 39.1 %collective-permute-start.7 = (f32[384,512]{1,0:T(8,128)S(1)}, f32[384,512]{1,0:T(8,128)S(1)}, u32[]{:S(2)}, u32[]{:S(2)}) collective-permute-start(f32[384,512]{1,0:T(8,128)S(1)} %get-tuple-element.8), channel_id=1, source_target_pairs={{6,0},{10,2},{4,4},{8,6},{14,8},{18,10},{12,12},{16,14},{22,16},{2... | collective-permute-start | bytes 2359304 | tf_op jit(solution)/shard_map/ppermute | solution.py:38

commit v12 on v11

--- a/solution.py
+++ b/solution.py
@@ -89,18 +89,22 @@
         out_ref[k] = amplitude
 
 
-def density_parts(mine_ref, other_ref, lower_ref, upper_ref, amp_ref, swapped_ref, up_ref, down_ref):
-    rows, virt = up_ref.shape
-    width = amp_ref.shape[2]
-    upper = split(upper_ref[...])
-    total = None
-    for start_ref, half_ref in ((mine_ref, amp_ref), (other_ref, swapped_ref)):
-        columns = block(start_ref, width)
-        amp = split(half_ref[...].reshape(virt, width))
-        down_ref[:, columns] = dot(upper, amp, ((1,), (0,)))
-        part = dot(split(lower_ref[:, columns]), amp, ((1,), (1,)))
-        total = part if total is None else total + part
-    up_ref[...] = total
+def half_density(start_ref, lower_ref, upper_ref, half_ref):
+    amp = split(half_ref[...].reshape(lower_ref.shape[1], half_ref.shape[2]))
+    columns = block(start_ref, half_ref.shape[2])
+    return dot(split(lower_ref[:, columns]), amp, ((1,), (1,))), dot(split(upper_ref[...]), amp, ((1,), (0,)))
+
+
+def first_half(mine_ref, lower_ref, upper_ref, amp_ref, up_ref, down_ref):
+    up_ref[...], down_ref[...] = half_density(mine_ref, lower_ref, upper_ref, amp_ref)
+
+
+def density_parts(mine_ref, other_ref, lower_ref, upper_ref, swapped_ref, half_up_ref, half_down_ref, up_ref, down_ref):
+    width = swapped_ref.shape[2]
+    up, down = half_density(other_ref, lower_ref, upper_ref, swapped_ref)
+    up_ref[...] = half_up_ref[...] + up
+    down_ref[:, block(mine_ref, width)] = half_down_ref[...]
+    down_ref[:, block(other_ref, width)] = down
 
 
 def local(factors, occ_energy, virt_energy):
@@ -128,7 +132,8 @@
     tile = kernel(add_tiles, [whole], [], [keep, core_swap(give)])[0]
     amp = shared(kernel(divide, [whole], [], [shared(tile), sums, *energies])[0])
     swapped = core_swap(amp)
-    up, down = kernel(density_parts, [(rows, virt)] * 2, [mine, other], [lower, upper, amp, swapped])
+    halves = kernel(first_half, [(rows, virt), (rows, half)], [mine], [lower, upper, amp])
+    up, down = kernel(density_parts, [(rows, virt)] * 2, [mine, other], [lower, upper, swapped, *halves])
     return (move(up, back(below)) + move(down, back(above)))[None]
 
 

time: 144 us -> 144 us (level)
    pallas_call x5 -> x6, Pallas kernels: 2.82 us -> 2.99 us  [kernel(): pl.pallas_call(run, out_shape=[jax.ShapeDtypeStruct(s, jnp.float32) for s...]
  transfers between devices with their start and end apart: 8 -> 8, of which waited for: 6 -> 6; matrix products, arithmetic and copies ran while one was open for 1% -> 1% of each run, Pallas kernels for 0% -> 1%
where the time goes in v12:
time: 144 us; the launch traced here: 142 us
  waiting for transfers between devices  58.1 us (40%)
  starting transfers between devices  44.5 us (31%)
  blocking collectives  31.6 us (22%)
  Pallas kernels  2.99 us (2%)
  local copies, waits for them, and re-layouts  2.12 us (1%)
    ppermute x6, waiting for transfers between devices, move(): return lax.ppermute(x, PLACES, pairs)  56.5 us
    ppermute x6, starting transfers between devices, move(): return lax.ppermute(x, PLACES, pairs)  37.4 us
    all_to_all x2, blocking collectives, shared(): return lax.all_to_all(x, PLACES, 0, 0, axis_index_groups=groups, tiled=True)  31.6 us
    ppermute x2, starting transfers between devices, core_swap(): return lax.ppermute(x, 'core', [(0, 1), (1, 0)])  7.06 us
    pallas_call x6, Pallas kernels, kernel(): pl.pallas_call(run, out_shape=[jax.ShapeDtypeStruct(s, jnp.float32) for s...  2.99 us
  transfers between devices with their start and end apart: 8, of which 6 were waited for; matrix products, arithmetic and copies ran while one was open for 1% of the time, Pallas kernels for 1%

profile of v12, /device:TPU:1, one launch (start us, length us, event | category | flops | bytes accessed | tf_op | source)
XLA Modules:
  0.0 141.7 jit_solution(2496450910293524131)
XLA Ops:
  0.0 20.2 %collective-permute-start.1 = (f32[384,512]{1,0:T(8,128)}, f32[384,512]{1,0:T(8,128)S(1)}, u32[]{:S(2)}, u32[]{:S(2)}) collective-permute-start(f32[384,512]{1,0:T(8,128)} %bitcast.8), channel_id=1, source_target_pairs={{0,766},{2,746},{4,764},{6,744},{8,6},{10,10},{12,4},{14,8},{16,14... | collective-permute-start | bytes 2359304 | tf_op jit(solution)/shard_map/ppermute | solution.py:38
  20.2 1.9 %collective-permute-start = (f32[384,512]{1,0:T(8,128)}, f32[384,512]{1,0:T(8,128)S(1)}, u32[]{:S(2)}, u32[]{:S(2)}) collective-permute-start(f32[384,512]{1,0:T(8,128)} %bitcast.9), channel_id=1, source_target_pairs={{0,6},{2,10},{4,4},{6,8},{8,14},{10,18},{12,12},{14,16},{16,22},{1... | collective-permute-start | bytes 2359304 | tf_op jit(solution)/shard_map/ppermute | solution.py:38
  22.8 5.4 %collective-permute-start.3 = (f32[8,128]{1,0:T(8,128)S(1)}, f32[8,128]{1,0:T(8,128)S(1)}, u32[]{:S(2)}, u32[]{:S(2)}) collective-permute-start(f32[8,128]{1,0:T(8,128)S(1)} %broadcast_in_dim.4), channel_id=1, source_target_pairs={{0,766},{2,746},{4,764},{6,744},{8,6},{10,10},{12,4},{14,8},{16,14... | collective-permute-start | bytes 12296 | tf_op jit(solution)/shard_map/ppermute | solution.py:38
  28.2 2.5 %collective-permute-start.2 = (f32[8,128]{1,0:T(8,128)S(1)}, f32[8,128]{1,0:T(8,128)S(1)}, u32[]{:S(2)}, u32[]{:S(2)}) collective-permute-start(f32[8,128]{1,0:T(8,128)S(1)} %broadcast_in_dim.4), channel_id=1, source_target_pairs={{0,6},{2,10},{4,4},{6,8},{8,14},{10,18},{12,12},{14,16},{16,22},{1... | collective-permute-start | bytes 12296 | tf_op jit(solution)/shard_map/ppermute | solution.py:38
  30.7 0.6 copy-done.1
  31.4 0.6 dynamic_slice.10
  32.7 0.7 copy-done
  33.6 20.1 %collective-permute-done.3.refs_4_.refs_3_ = f32[8,128]{1,0:T(8,128)S(1)} collective-permute-done((f32[8,128]{1,0:T(8,128)S(1)}, f32[8,128]{1,0:T(8,128)S(1)}, u32[]{:S(2)}, u32[]{:S(2)}) %collective-permute-start.3) | collective-permute-done | bytes 4128 | tf_op jit(solution)/shard_map/ppermute | solution.py:38
  53.7 0.2 collective-permute-done.2.refs_3_.refs_2_
  53.9 0.6 shard_map.49.refs_3_
  54.5 3.3 %collective-permute-start.4 = (f32[512,256]{1,0:T(8,128)S(1)}, f32[512,256]{1,0:T(8,128)S(1)}, u32[]{:S(2)}, u32[]{:S(2)}) collective-permute-start(f32[512,256]{1,0:T(8,128)S(1)} %shard_map.49.refs_3_), channel_id=1, source_target_pairs={{0,1},{1,0},{2,3},{3,2},{4,5},{5,4},{6,7},{7,6},{8,9},{9,8},{10,11... | collective-permute-start | bytes 1572872 | tf_op jit(solution)/shard_map/ppermute | solution.py:42
  57.8 0.6 shard_map.50.refs_0_
  58.5 0.9 collective-permute-done.4.refs_1_
  59.4 15.6 %all_to_all.10.refs_0_ = f32[4,128,256]{2,1,0:T(8,128)S(1)} all-to-all(f32[4,128,256]{2,1,0:T(8,128)S(1)} %shard_map.51), channel_id=1, replica_groups={{6,10,4,8},{14,18,12,16},{22,2,20,0},{30,34,28,32},{38,42,36,40},{46,26..., dimensions={0} | all-to-all | bytes 1048576 | tf_op jit(solution)/shard_map/all_to_all | solution.py:121
  75.1 15.9 %all_to_all.11.refs_3_ = f32[4,128,256]{2,1,0:T(8,128)S(1)} all-to-all(f32[4,128,256]{2,1,0:T(8,128)S(1)} %shard_map.52), channel_id=1, replica_groups={{6,10,4,8},{14,18,12,16},{22,2,20,0},{30,34,28,32},{38,42,36,40},{46,26..., dimensions={0} | all-to-all | bytes 1048576 | tf_op jit(solution)/shard_map/all_to_all | solution.py:121
  91.1 3.8 %collective-permute-start.5 = (f32[4,128,256]{2,1,0:T(8,128)S(1)}, f32[4,128,256]{2,1,0:T(8,128)S(1)}, u32[]{:S(2)}, u32[]{:S(2)}) collective-permute-start(f32[4,128,256]{2,1,0:T(8,128)S(1)} %all_to_all.11.refs_3_), channel_id=1, source_target_pairs={{0,1},{1,0},{2,3},{3,2},{4,5},{5,4},{6,7},{7,6},{8,9},{9,8},{10,11... | collective-permute-start | bytes 1572872 | tf_op jit(solution)/shard_map/ppermute | solution.py:42
  94.8 0.8 shard_map.53
  95.6 0.7 collective-permute-done.5.refs_4_
  96.3 0.8 shard_map.54
  97.1 4.5 %collective-permute-start.6 = (f32[384,512]{1,0:T(8,128)S(1)}, f32[384,512]{1,0:T(8,128)S(1)}, u32[]{:S(2)}, u32[]{:S(2)}) collective-permute-start(f32[384,512]{1,0:T(8,128)S(1)} %get-tuple-element.11), channel_id=1, source_target_pairs={{766,0},{746,2},{764,4},{744,6},{6,8},{10,10},{4,12},{8,14},{14,16... | collective-permute-start | bytes 2359304 | tf_op jit(solution)/shard_map/ppermute | solution.py:38
  101.7 2.9 %collective-permute-start.7 = (f32[384,512]{1,0:T(8,128)S(1)}, f32[384,512]{1,0:T(8,128)S(1)}, u32[]{:S(2)}, u32[]{:S(2)}) collective-permute-start(f32[384,512]{1,0:T(8,128)S(1)} %get-tuple-element.12), channel_id=1, source_target_pairs={{6,0},{10,2},{4,4},{8,6},{14,8},{18,10},{12,12},{16,14},{22,16},{2... | collective-permute-start | bytes 2359304 | tf_op jit(solution)/shard_map/ppermute | solution.py:38
  104.5 23.3 %collective-permute-done.6 = f32[384,512]{1,0:T(8,128)S(1)} collective-permute-done((f32[384,512]{1,0:T(8,128)S(1)}, f32[384,512]{1,0:T(8,128)S(1)}, u32[]{:S(2)}, u32[]{:S(2)}) %collective-permute-start.6) | collective-permute-done | bytes 786464 | tf_op jit(solution)/shard_map/ppermute | solution.py:38
  127.9 12.8 %collective-permute-done.7 = f32[384,512]{1,0:T(8,128)S(1)} collective-permute-done((f32[384,512]{1,0:T(8,128)S(1)}, f32[384,512]{1,0:T(8,128)S(1)}, u32[]{:S(2)}, u32[]{:S(2)}) %collective-permute-start.7) | collective-permute-done | bytes 786464 | tf_op jit(solution)/shard_map/ppermute | solution.py:38
  140.7 1.0 add_bitcast_fusion
  (10 shorter events, 0.4 us)
Async XLA Ops:
  0.0 53.9 %collective-permute-start.1 = (f32[384,512]{1,0:T(8,128)}, f32[384,512]{1,0:T(8,128)S(1)}, u32[]{:S(2)}, u32[]{:S(2)}) collective-permute-start(f32[384,512]{1,0:T(8,128)} %bitcast.8), channel_id=1, source_target_pairs={{0,766},{2,746},{4,764},{6,744},{8,6},{10,10},{12,4},{14,8},{16,14... | collective-permute-start | bytes 2359304 | tf_op jit(solution)/shard_map/ppermute | solution.py:38
  20.2 33.7 %collective-permute-start = (f32[384,512]{1,0:T(8,128)}, f32[384,512]{1,0:T(8,128)S(1)}, u32[]{:S(2)}, u32[]{:S(2)}) collective-permute-start(f32[384,512]{1,0:T(8,128)} %bitcast.9), channel_id=1, source_target_pairs={{0,6},{2,10},{4,4},{6,8},{8,14},{10,18},{12,12},{14,16},{16,22},{1... | collective-permute-start | bytes 2359304 | tf_op jit(solution)/shard_map/ppermute | solution.py:38
  22.8 30.9 %collective-permute-start.3 = (f32[8,128]{1,0:T(8,128)S(1)}, f32[8,128]{1,0:T(8,128)S(1)}, u32[]{:S(2)}, u32[]{:S(2)}) collective-permute-start(f32[8,128]{1,0:T(8,128)S(1)} %broadcast_in_dim.4), channel_id=1, source_target_pairs={{0,766},{2,746},{4,764},{6,744},{8,6},{10,10},{12,4},{14,8},{16,14... | collective-permute-start | bytes 12296 | tf_op jit(solution)/shard_map/ppermute | solution.py:38
  28.2 25.7 %collective-permute-start.2 = (f32[8,128]{1,0:T(8,128)S(1)}, f32[8,128]{1,0:T(8,128)S(1)}, u32[]{:S(2)}, u32[]{:S(2)}) collective-permute-start(f32[8,128]{1,0:T(8,128)S(1)} %broadcast_in_dim.4), channel_id=1, source_target_pairs={{0,6},{2,10},{4,4},{6,8},{8,14},{10,18},{12,12},{14,16},{16,22},{1... | collective-permute-start | bytes 12296 | tf_op jit(solution)/shard_map/ppermute | solution.py:38
  30.7 0.7 copy-start.1
  32.6 0.7 copy-start
  54.5 4.8 %collective-permute-start.4 = (f32[512,256]{1,0:T(8,128)S(1)}, f32[512,256]{1,0:T(8,128)S(1)}, u32[]{:S(2)}, u32[]{:S(2)}) collective-permute-start(f32[512,256]{1,0:T(8,128)S(1)} %shard_map.49.refs_3_), channel_id=1, source_target_pairs={{0,1},{1,0},{2,3},{3,2},{4,5},{5,4},{6,7},{7,6},{8,9},{9,8},{10,11... | collective-permute-start | bytes 1572872 | tf_op jit(solution)/shard_map/ppermute | solution.py:42
  91.1 5.3 %collective-permute-start.5 = (f32[4,128,256]{2,1,0:T(8,128)S(1)}, f32[4,128,256]{2,1,0:T(8,128)S(1)}, u32[]{:S(2)}, u32[]{:S(2)}) collective-permute-start(f32[4,128,256]{2,1,0:T(8,128)S(1)} %all_to_all.11.refs_3_), channel_id=1, source_target_pairs={{0,1},{1,0},{2,3},{3,2},{4,5},{5,4},{6,7},{7,6},{8,9},{9,8},{10,11... | collective-permute-start | bytes 1572872 | tf_op jit(solution)/shard_map/ppermute | solution.py:42
  97.1 30.7 %collective-permute-start.6 = (f32[384,512]{1,0:T(8,128)S(1)}, f32[384,512]{1,0:T(8,128)S(1)}, u32[]{:S(2)}, u32[]{:S(2)}) collective-permute-start(f32[384,512]{1,0:T(8,128)S(1)} %get-tuple-element.11), channel_id=1, source_target_pairs={{766,0},{746,2},{764,4},{744,6},{6,8},{10,10},{4,12},{8,14},{14,16... | collective-permute-start | bytes 2359304 | tf_op jit(solution)/shard_map/ppermute | solution.py:38
  101.7 39.0 %collective-permute-start.7 = (f32[384,512]{1,0:T(8,128)S(1)}, f32[384,512]{1,0:T(8,128)S(1)}, u32[]{:S(2)}, u32[]{:S(2)}) collective-permute-start(f32[384,512]{1,0:T(8,128)S(1)} %get-tuple-element.12), channel_id=1, source_target_pairs={{6,0},{10,2},{4,4},{8,6},{14,8},{18,10},{12,12},{16,14},{22,16},{2... | collective-permute-start | bytes 2359304 | tf_op jit(solution)/shard_map/ppermute | solution.py:38

commit v13 on v12

--- a/solution.py
+++ b/solution.py
@@ -42,7 +42,7 @@
     return lax.ppermute(x, "core", [(0, 1), (1, 0)])
 
 
-def kernel(body, shapes, scalars, arrays, after=()):
+def kernel(body, shapes, scalars, arrays, after=(), dtype=jnp.float32):
     used = len(scalars) + len(arrays)
 
     def run(*refs):
@@ -50,7 +50,7 @@
 
     return pl.pallas_call(
         run,
-        out_shape=[jax.ShapeDtypeStruct(s, jnp.float32) for s in shapes],
+        out_shape=[jax.ShapeDtypeStruct(s, dtype) for s in shapes],
         in_specs=[SMEM] * len(scalars) + [VMEM] * len(arrays) + [ANY] * len(after),
         out_specs=[VMEM] * len(shapes),
         compiler_params=pltpu.CompilerParams(vmem_limit_bytes=24 * 2**20),
@@ -78,6 +78,17 @@
     out_ref[...] = dot(split(upper_ref[...]), lower, ((0,), (0,)))
 
 
+def split_slabs(lower_ref, upper_ref, *out_refs):
+    out_refs[0][...], out_refs[1][...] = split(lower_ref[...])
+    out_refs[2][...], out_refs[3][...] = split(upper_ref[...])
+
+
+def kept_tile(start_ref, lower_high_ref, lower_low_ref, upper_high_ref, upper_low_ref, out_ref):
+    columns = block(start_ref, out_ref.shape[1])
+    lower = lower_high_ref[:, columns], lower_low_ref[:, columns]
+    out_ref[...] = dot((upper_high_ref[...], upper_low_ref[...]), lower, ((0,), (0,)))
+
+
 def add_tiles(keep_ref, got_ref, out_ref):
     out_ref[...] = (keep_ref[...] + got_ref[...]).reshape(out_ref.shape)
 
@@ -89,19 +100,21 @@
         out_ref[k] = amplitude
 
 
-def half_density(start_ref, lower_ref, upper_ref, half_ref):
-    amp = split(half_ref[...].reshape(lower_ref.shape[1], half_ref.shape[2]))
+def half_density(start_ref, lower_refs, upper_refs, half_ref):
+    amp = split(half_ref[...].reshape(lower_refs[0].shape[1], half_ref.shape[2]))
     columns = block(start_ref, half_ref.shape[2])
-    return dot(split(lower_ref[:, columns]), amp, ((1,), (1,))), dot(split(upper_ref[...]), amp, ((1,), (0,)))
+    lower, upper = [ref[:, columns] for ref in lower_refs], [ref[...] for ref in upper_refs]
+    return dot(lower, amp, ((1,), (1,))), dot(upper, amp, ((1,), (0,)))
 
 
-def first_half(mine_ref, lower_ref, upper_ref, amp_ref, up_ref, down_ref):
-    up_ref[...], down_ref[...] = half_density(mine_ref, lower_ref, upper_ref, amp_ref)
+def first_half(mine_ref, lower_high, lower_low, upper_high, upper_low, amp_ref, up_ref, down_ref):
+    up_ref[...], down_ref[...] = half_density(mine_ref, (lower_high, lower_low), (upper_high, upper_low), amp_ref)
 
 
-def density_parts(mine_ref, other_ref, lower_ref, upper_ref, swapped_ref, half_up_ref, half_down_ref, up_ref, down_ref):
+def density_parts(mine_ref, other_ref, lower_high, lower_low, upper_high, upper_low, swapped_ref, *refs):
+    half_up_ref, half_down_ref, up_ref, down_ref = refs
     width = swapped_ref.shape[2]
-    up, down = half_density(other_ref, lower_ref, upper_ref, swapped_ref)
+    up, down = half_density(other_ref, (lower_high, lower_low), (upper_high, upper_low), swapped_ref)
     up_ref[...] = half_up_ref[...] + up
     down_ref[:, block(mine_ref, width)] = half_down_ref[...]
     down_ref[:, block(other_ref, width)] = down
@@ -127,13 +140,14 @@
     column_energy = lax.dynamic_slice_in_dim(virt_energy, mine, half, 0)
     sums = row_energy[:, None] + column_energy[None, :]
     give = kernel(pair_tile, [(virt, half)], [other], [lower, upper], [*energies, sums])[0]
-    keep = kernel(pair_tile, [(virt, half)], [mine], [lower, upper], [give])[0]
+    slabs = kernel(split_slabs, [(rows, virt)] * 4, [], [lower, upper], [give], jnp.bfloat16)
+    keep = kernel(kept_tile, [(virt, half)], [mine], slabs)[0]
     whole = (CHIPS, quarter, half)
     tile = kernel(add_tiles, [whole], [], [keep, core_swap(give)])[0]
     amp = shared(kernel(divide, [whole], [], [shared(tile), sums, *energies])[0])
     swapped = core_swap(amp)
-    halves = kernel(first_half, [(rows, virt), (rows, half)], [mine], [lower, upper, amp])
-    up, down = kernel(density_parts, [(rows, virt)] * 2, [mine, other], [lower, upper, swapped, *halves])
+    halves = kernel(first_half, [(rows, virt), (rows, half)], [mine], [*slabs, amp])
+    up, down = kernel(density_parts, [(rows, virt)] * 2, [mine, other], [*slabs, swapped, *halves])
     return (move(up, back(below)) + move(down, back(above)))[None]
 
 

time: 144 us -> 144 us (level)
    pallas_call x6 -> x7, Pallas kernels: 2.99 us -> 3.26 us  [kernel(): pl.pallas_call(run, out_shape=[jax.ShapeDtypeStruct(s, dtype) for s in sh...]
where the time goes in v13:
time: 144 us; the launch traced here: 142 us
  waiting for transfers between devices  57.8 us (40%)
  starting transfers between devices  44.5 us (31%)
  blocking collectives  31.6 us (22%)
  Pallas kernels  3.26 us (2%)
  local copies, waits for them, and re-layouts  2.08 us (1%)
  between operations  1.44 us (1%)
    ppermute x6, waiting for transfers between devices, move(): return lax.ppermute(x, PLACES, pairs)  56.5 us
    ppermute x6, starting transfers between devices, move(): return lax.ppermute(x, PLACES, pairs)  37.4 us
    all_to_all x2, blocking collectives, shared(): return lax.all_to_all(x, PLACES, 0, 0, axis_index_groups=groups, tiled=True)  31.6 us
    ppermute x2, starting transfers between devices, core_swap(): return lax.ppermute(x, 'core', [(0, 1), (1, 0)])  7.06 us
    pallas_call x7, Pallas kernels, kernel(): pl.pallas_call(run, out_shape=[jax.ShapeDtypeStruct(s, dtype) for s in sh...  3.26 us
  transfers between devices with their start and end apart: 8, of which 6 were waited for; matrix products, arithmetic and copies ran while one was open for 1% of the time, Pallas kernels for 1%

profile of v13, /device:TPU:1, one launch (start us, length us, event | category | flops | bytes accessed | tf_op | source)
XLA Modules:
  0.0 141.7 jit_solution(11943730929078107849)
XLA Ops:
  0.0 20.2 %collective-permute-start.1 = (f32[384,512]{1,0:T(8,128)}, f32[384,512]{1,0:T(8,128)S(1)}, u32[]{:S(2)}, u32[]{:S(2)}) collective-permute-start(f32[384,512]{1,0:T(8,128)} %bitcast.8), channel_id=1, source_target_pairs={{0,766},{2,746},{4,764},{6,744},{8,6},{10,10},{12,4},{14,8},{16,14... | collective-permute-start | bytes 2359304 | tf_op jit(solution)/shard_map/ppermute | solution.py:38
  20.2 1.9 %collective-permute-start = (f32[384,512]{1,0:T(8,128)}, f32[384,512]{1,0:T(8,128)S(1)}, u32[]{:S(2)}, u32[]{:S(2)}) collective-permute-start(f32[384,512]{1,0:T(8,128)} %bitcast.9), channel_id=1, source_target_pairs={{0,6},{2,10},{4,4},{6,8},{8,14},{10,18},{12,12},{14,16},{16,22},{1... | collective-permute-start | bytes 2359304 | tf_op jit(solution)/shard_map/ppermute | solution.py:38
  22.8 5.4 %collective-permute-start.3 = (f32[8,128]{1,0:T(8,128)S(1)}, f32[8,128]{1,0:T(8,128)S(1)}, u32[]{:S(2)}, u32[]{:S(2)}) collective-permute-start(f32[8,128]{1,0:T(8,128)S(1)} %broadcast_in_dim.4), channel_id=1, source_target_pairs={{0,766},{2,746},{4,764},{6,744},{8,6},{10,10},{12,4},{14,8},{16,14... | collective-permute-start | bytes 12296 | tf_op jit(solution)/shard_map/ppermute | solution.py:38
  28.2 2.5 %collective-permute-start.2 = (f32[8,128]{1,0:T(8,128)S(1)}, f32[8,128]{1,0:T(8,128)S(1)}, u32[]{:S(2)}, u32[]{:S(2)}) collective-permute-start(f32[8,128]{1,0:T(8,128)S(1)} %broadcast_in_dim.4), channel_id=1, source_target_pairs={{0,6},{2,10},{4,4},{6,8},{8,14},{10,18},{12,12},{14,16},{16,22},{1... | collective-permute-start | bytes 12296 | tf_op jit(solution)/shard_map/ppermute | solution.py:38
  30.7 0.6 copy-done.1
  31.4 0.6 dynamic_slice.10
  32.6 0.7 copy-done
  33.5 20.1 %collective-permute-done.3.refs_4_.refs_3_ = f32[8,128]{1,0:T(8,128)S(1)} collective-permute-done((f32[8,128]{1,0:T(8,128)S(1)}, f32[8,128]{1,0:T(8,128)S(1)}, u32[]{:S(2)}, u32[]{:S(2)}) %collective-permute-start.3) | collective-permute-done | bytes 4128 | tf_op jit(solution)/shard_map/ppermute | solution.py:38
  53.9 0.6 shard_map.49.refs_2_
  54.5 3.3 %collective-permute-start.4 = (f32[512,256]{1,0:T(8,128)S(1)}, f32[512,256]{1,0:T(8,128)S(1)}, u32[]{:S(2)}, u32[]{:S(2)}) collective-permute-start(f32[512,256]{1,0:T(8,128)S(1)} %shard_map.49.refs_2_), channel_id=1, source_target_pairs={{0,1},{1,0},{2,3},{3,2},{4,5},{5,4},{6,7},{7,6},{8,9},{9,8},{10,11... | collective-permute-start | bytes 1572872 | tf_op jit(solution)/shard_map/ppermute | solution.py:42
  57.8 0.2 shard_map.50
  58.1 0.6 shard_map.51.refs_0_
  58.7 0.6 collective-permute-done.4.refs_1_
  59.4 15.6 %all_to_all.10.refs_0_ = f32[4,128,256]{2,1,0:T(8,128)S(1)} all-to-all(f32[4,128,256]{2,1,0:T(8,128)S(1)} %shard_map.52), channel_id=1, replica_groups={{6,10,4,8},{14,18,12,16},{22,2,20,0},{30,34,28,32},{38,42,36,40},{46,26..., dimensions={0} | all-to-all | bytes 1048576 | tf_op jit(solution)/shard_map/all_to_all | solution.py:134
  75.1 15.9 %all_to_all.11.refs_5_ = f32[4,128,256]{2,1,0:T(8,128)S(1)} all-to-all(f32[4,128,256]{2,1,0:T(8,128)S(1)} %shard_map.53), channel_id=1, replica_groups={{6,10,4,8},{14,18,12,16},{22,2,20,0},{30,34,28,32},{38,42,36,40},{46,26..., dimensions={0} | all-to-all | bytes 1048576 | tf_op jit(solution)/shard_map/all_to_all | solution.py:134
  91.1 3.8 %collective-permute-start.5 = (f32[4,128,256]{2,1,0:T(8,128)S(1)}, f32[4,128,256]{2,1,0:T(8,128)S(1)}, u32[]{:S(2)}, u32[]{:S(2)}) collective-permute-start(f32[4,128,256]{2,1,0:T(8,128)S(1)} %all_to_all.11.refs_5_), channel_id=1, source_target_pairs={{0,1},{1,0},{2,3},{3,2},{4,5},{5,4},{6,7},{7,6},{8,9},{9,8},{10,11... | collective-permute-start | bytes 1572872 | tf_op jit(solution)/shard_map/ppermute | solution.py:42
  94.8 0.8 shard_map.54
  95.7 0.7 collective-permute-done.5.refs_6_
  96.4 0.8 shard_map.55
  97.2 4.5 %collective-permute-start.6 = (f32[384,512]{1,0:T(8,128)S(1)}, f32[384,512]{1,0:T(8,128)S(1)}, u32[]{:S(2)}, u32[]{:S(2)}) collective-permute-start(f32[384,512]{1,0:T(8,128)S(1)} %get-tuple-element.19), channel_id=1, source_target_pairs={{766,0},{746,2},{764,4},{744,6},{6,8},{10,10},{4,12},{8,14},{14,16... | collective-permute-start | bytes 2359304 | tf_op jit(solution)/shard_map/ppermute | solution.py:38
  101.7 2.9 %collective-permute-start.7 = (f32[384,512]{1,0:T(8,128)S(1)}, f32[384,512]{1,0:T(8,128)S(1)}, u32[]{:S(2)}, u32[]{:S(2)}) collective-permute-start(f32[384,512]{1,0:T(8,128)S(1)} %get-tuple-element.20), channel_id=1, source_target_pairs={{6,0},{10,2},{4,4},{8,6},{14,8},{18,10},{12,12},{16,14},{22,16},{2... | collective-permute-start | bytes 2359304 | tf_op jit(solution)/shard_map/ppermute | solution.py:38
  104.6 23.3 %collective-permute-done.6 = f32[384,512]{1,0:T(8,128)S(1)} collective-permute-done((f32[384,512]{1,0:T(8,128)S(1)}, f32[384,512]{1,0:T(8,128)S(1)}, u32[]{:S(2)}, u32[]{:S(2)}) %collective-permute-start.6) | collective-permute-done | bytes 786464 | tf_op jit(solution)/shard_map/ppermute | solution.py:38
  127.9 12.8 %collective-permute-done.7 = f32[384,512]{1,0:T(8,128)S(1)} collective-permute-done((f32[384,512]{1,0:T(8,128)S(1)}, f32[384,512]{1,0:T(8,128)S(1)}, u32[]{:S(2)}, u32[]{:S(2)}) %collective-permute-start.7) | collective-permute-done | bytes 786464 | tf_op jit(solution)/shard_map/ppermute | solution.py:38
  140.7 1.0 add_bitcast_fusion
  (11 shorter events, 0.6 us)
Async XLA Ops:
  0.0 53.9 %collective-permute-start.1 = (f32[384,512]{1,0:T(8,128)}, f32[384,512]{1,0:T(8,128)S(1)}, u32[]{:S(2)}, u32[]{:S(2)}) collective-permute-start(f32[384,512]{1,0:T(8,128)} %bitcast.8), channel_id=1, source_target_pairs={{0,766},{2,746},{4,764},{6,744},{8,6},{10,10},{12,4},{14,8},{16,14... | collective-permute-start | bytes 2359304 | tf_op jit(solution)/shard_map/ppermute | solution.py:38
  20.2 33.7 %collective-permute-start = (f32[384,512]{1,0:T(8,128)}, f32[384,512]{1,0:T(8,128)S(1)}, u32[]{:S(2)}, u32[]{:S(2)}) collective-permute-start(f32[384,512]{1,0:T(8,128)} %bitcast.9), channel_id=1, source_target_pairs={{0,6},{2,10},{4,4},{6,8},{8,14},{10,18},{12,12},{14,16},{16,22},{1... | collective-permute-start | bytes 2359304 | tf_op jit(solution)/shard_map/ppermute | solution.py:38
  22.8 30.9 %collective-permute-start.3 = (f32[8,128]{1,0:T(8,128)S(1)}, f32[8,128]{1,0:T(8,128)S(1)}, u32[]{:S(2)}, u32[]{:S(2)}) collective-permute-start(f32[8,128]{1,0:T(8,128)S(1)} %broadcast_in_dim.4), channel_id=1, source_target_pairs={{0,766},{2,746},{4,764},{6,744},{8,6},{10,10},{12,4},{14,8},{16,14... | collective-permute-start | bytes 12296 | tf_op jit(solution)/shard_map/ppermute | solution.py:38
  28.2 25.7 %collective-permute-start.2 = (f32[8,128]{1,0:T(8,128)S(1)}, f32[8,128]{1,0:T(8,128)S(1)}, u32[]{:S(2)}, u32[]{:S(2)}) collective-permute-start(f32[8,128]{1,0:T(8,128)S(1)} %broadcast_in_dim.4), channel_id=1, source_target_pairs={{0,6},{2,10},{4,4},{6,8},{8,14},{10,18},{12,12},{14,16},{16,22},{1... | collective-permute-start | bytes 12296 | tf_op jit(solution)/shard_map/ppermute | solution.py:38
  30.7 0.7 copy-start.1
  32.6 0.7 copy-start
  54.5 4.8 %collective-permute-start.4 = (f32[512,256]{1,0:T(8,128)S(1)}, f32[512,256]{1,0:T(8,128)S(1)}, u32[]{:S(2)}, u32[]{:S(2)}) collective-permute-start(f32[512,256]{1,0:T(8,128)S(1)} %shard_map.49.refs_2_), channel_id=1, source_target_pairs={{0,1},{1,0},{2,3},{3,2},{4,5},{5,4},{6,7},{7,6},{8,9},{9,8},{10,11... | collective-permute-start | bytes 1572872 | tf_op jit(solution)/shard_map/ppermute | solution.py:42
  91.1 5.3 %collective-permute-start.5 = (f32[4,128,256]{2,1,0:T(8,128)S(1)}, f32[4,128,256]{2,1,0:T(8,128)S(1)}, u32[]{:S(2)}, u32[]{:S(2)}) collective-permute-start(f32[4,128,256]{2,1,0:T(8,128)S(1)} %all_to_all.11.refs_5_), channel_id=1, source_target_pairs={{0,1},{1,0},{2,3},{3,2},{4,5},{5,4},{6,7},{7,6},{8,9},{9,8},{10,11... | collective-permute-start | bytes 1572872 | tf_op jit(solution)/shard_map/ppermute | solution.py:42
  97.2 30.7 %collective-permute-start.6 = (f32[384,512]{1,0:T(8,128)S(1)}, f32[384,512]{1,0:T(8,128)S(1)}, u32[]{:S(2)}, u32[]{:S(2)}) collective-permute-start(f32[384,512]{1,0:T(8,128)S(1)} %get-tuple-element.19), channel_id=1, source_target_pairs={{766,0},{746,2},{764,4},{744,6},{6,8},{10,10},{4,12},{8,14},{14,16... | collective-permute-start | bytes 2359304 | tf_op jit(solution)/shard_map/ppermute | solution.py:38
  101.7 39.0 %collective-permute-start.7 = (f32[384,512]{1,0:T(8,128)S(1)}, f32[384,512]{1,0:T(8,128)S(1)}, u32[]{:S(2)}, u32[]{:S(2)}) collective-permute-start(f32[384,512]{1,0:T(8,128)S(1)} %get-tuple-element.20), channel_id=1, source_target_pairs={{6,0},{10,2},{4,4},{8,6},{14,8},{18,10},{12,12},{16,14},{22,16},{2... | collective-permute-start | bytes 2359304 | tf_op jit(solution)/shard_map/ppermute | solution.py:38
